TPU v7x, 32 devices: a whole 2x2x4 slice. The times are simulated.
32 devices in a mesh: row: 4 (over y, x), col: 8 (over z, core).
Axes of the slice: x: 2, y: 2, z: 4, core: 2. Of those that a mesh axis runs over, the one named last changes fastest.
Arguments:
- pixels: bfloat16 [384, 196, 768], P(('row', 'col')), may hold values from -6 to 6
- keep_idx: int32 [384, 49], P(('row', 'col')), may hold values from 0 to 195, as said below
- restore: int32 [384, 196], P(('row', 'col')), may hold values from 0 to 195
- enc_in: float32 [768, 7424], P('row', 'col'), may hold values from -0.21875 to 0.21875
- enc_fc2: float32 [3072, 768], P('row', 'col'), may hold values from -0.109375 to 0.109375
- dec_in: float32 [512, 4096], P('row', 'col'), may hold values from -0.25 to 0.25
- dec_fc2: float32 [2048, 512], P('row', 'col'), may hold values from -0.125 to 0.125
- head_w: float32 [512, 768], replicated, may hold values from -0.25 to 0.25
- small_vec: float32 [21248], replicated, as said below
- m_enc_in: float32 [768, 7424], P('row', 'col'), may hold values from -4.4703484e-08 to 4.4703484e-08
- m_enc_fc2: float32 [3072, 768], P('row', 'col'), may hold values from -4.4703484e-08 to 4.4703484e-08
- m_dec_in: float32 [512, 4096], P('row', 'col'), may hold values from -4.4703484e-08 to 4.4703484e-08
- m_dec_fc2: float32 [2048, 512], P('row', 'col'), may hold values from -4.4703484e-08 to 4.4703484e-08
- m_head: float32 [512, 768], replicated, may hold values from -4.4703484e-08 to 4.4703484e-08
- m_small: float32 [21248], replicated, may hold values from -4.4703484e-08 to 4.4703484e-08
- v_enc_in: float32 [768, 7424], P('row', 'col'), may hold values from 8.6050224e-19 to 3.442009e-18
- v_enc_fc2: float32 [3072, 768], P('row', 'col'), may hold values from 8.6050224e-19 to 3.442009e-18
- v_dec_in: float32 [512, 4096], P('row', 'col'), may hold values from 8.6050224e-19 to 3.442009e-18
- v_dec_fc2: float32 [2048, 512], P('row', 'col'), may hold values from 8.6050224e-19 to 3.442009e-18
- v_head: float32 [512, 768], replicated, may hold values from 8.6050224e-19 to 3.442009e-18
- v_small: float32 [21248], replicated, may hold values from 8.6050224e-19 to 3.442009e-18
Outputs:
- new_enc_in: float32 [768, 7424], P('row', 'col')
- new_enc_fc2: float32 [3072, 768], P('row', 'col')
- new_dec_in: float32 [512, 4096], P('row', 'col')
- new_dec_fc2: float32 [2048, 512], P('row', 'col')
- new_head: float32 [512, 768], replicated
- new_small: float32 [21248], replicated
- mo_enc_in: float32 [768, 7424], P('row', 'col')
- mo_enc_fc2: float32 [3072, 768], P('row', 'col')
- mo_dec_in: float32 [512, 4096], P('row', 'col')
- mo_dec_fc2: float32 [2048, 512], P('row', 'col')
- mo_head: float32 [512, 768], replicated
- mo_small: float32 [21248], replicated
- vo_enc_in: float32 [768, 7424], P('row', 'col')
- vo_enc_fc2: float32 [3072, 768], P('row', 'col')
- vo_dec_in: float32 [512, 4096], P('row', 'col')
- vo_dec_fc2: float32 [2048, 512], P('row', 'col')
- vo_head: float32 [512, 768], replicated
- vo_small: float32 [21248], replicated
- loss: float32 [], replicated
- grad_norm: float32 [], replicated
Inputs may be any that keep to these rules, and one draw needn't show every extreme that they name: Each row of keep_idx holds 49 different patch numbers; restore is a permutation of each image's patches with restore[keep_idx[i]] = i, and restore >= 49 exactly on the patches that keep_idx leaves out. `small_vec`: gains near one and biases, class and mask tokens of order a third.
All inputs are finite; a program needn't handle non-finite values.
Results may differ from a plain program's by a relative error of at most 0.006.
Values may be sent and summed in bfloat16 or wider, within the bound.
A program may use at most 384 MiB of HBM per device.

v0:
```python
import jax
import jax.numpy as jnp
from jax import lax
from jax.sharding import PartitionSpec as P

D = 768
HEADS = 12
FF = 3072
DD = 512
DHEADS = 16
DFF = 2048
PATCH_PIX = 768
GRID = 14
PATCHES = 196
KEEP = 49
MB = 2
STEP = 10


clip_limit = 0.0001
learn_rate = 0.08
beta_one = 0.9
beta_two = 0.999
adam_eps = 1e-08
decay_rate = 0.05


def low_value(v):
    return lax.optimization_barrier(v.astype(jnp.bfloat16)).astype(jnp.float32)


def low_keep(v):
    return (low_value(v), None)


def low_pass(kept, grad):
    return (grad,)


def back_value(v):
    return v


def back_keep(v):
    return (v, None)


def back_low(kept, grad):
    return (low_value(grad),)


def low(v):
    wrapped = jax.custom_vjp(low_value)
    wrapped.defvjp(low_keep, low_pass)
    return wrapped(v)


def low_back(v):
    wrapped = jax.custom_vjp(back_value)
    wrapped.defvjp(back_keep, back_low)
    return wrapped(v)


def half(value):
    return value.astype(jnp.bfloat16)


def mat_value(left, right):
    return jnp.dot(half(left), half(right), preferred_element_type=jnp.float32)


def mat_keep(left, right):
    return (mat_value(left, right), (half(left), half(right)))


def mat_back(kept, grad):
    left16, right16 = kept
    grad16 = half(grad)
    return (
        jnp.dot(grad16, right16.T, preferred_element_type=jnp.float32),
        jnp.dot(left16.T, grad16, preferred_element_type=jnp.float32),
    )


def mat_plain(left, right):
    wrapped = jax.custom_vjp(mat_value)
    wrapped.defvjp(mat_keep, mat_back)
    return wrapped(left, right)


def score_value(query, keyed):
    return jnp.einsum(
        "nqhd,nkhd->nhqk", half(query), half(keyed), preferred_element_type=jnp.float32
    )


def score_keep(query, keyed):
    return (score_value(query, keyed), (half(query), half(keyed)))


def score_back(kept, grad):
    query16, keyed16 = kept
    grad16 = half(grad)
    return (
        jnp.einsum("nhqk,nkhd->nqhd", grad16, keyed16, preferred_element_type=jnp.float32),
        jnp.einsum("nhqk,nqhd->nkhd", grad16, query16, preferred_element_type=jnp.float32),
    )


def score_mat(query, keyed):
    wrapped = jax.custom_vjp(score_value)
    wrapped.defvjp(score_keep, score_back)
    return wrapped(query, keyed)


def value_value(probs, valued):
    return jnp.einsum(
        "nhqk,nkhd->nqhd", half(probs), half(valued), preferred_element_type=jnp.float32
    )


def value_keep(probs, valued):
    return (value_value(probs, valued), (half(probs), half(valued)))


def value_back(kept, grad):
    probs16, valued16 = kept
    grad16 = half(grad)
    return (
        jnp.einsum("nqhd,nkhd->nhqk", grad16, valued16, preferred_element_type=jnp.float32),
        jnp.einsum("nhqk,nqhd->nkhd", probs16, grad16, preferred_element_type=jnp.float32),
    )


def value_mat(probs, valued):
    wrapped = jax.custom_vjp(value_value)
    wrapped.defvjp(value_keep, value_back)
    return wrapped(probs, valued)


def small_parts(vector):
    lengths = [
        D,
        D,
        2 * D,
        D,
        D,
        D,
        FF,
        D,
        D,
        D,
        D,
        D,
        DD,
        DD,
        DD,
        DD,
        2 * DD,
        DD,
        DD,
        DD,
        DFF,
        DD,
        DD,
        DD,
        PATCH_PIX,
    ]
    pieces = []
    start = 0
    for piece_len in lengths:
        pieces.append(vector[start : start + piece_len])
        start += piece_len
    return pieces


def sincos_table(width):
    quarter = width // 4
    frequency = 1.0 / 10000.0 ** (jnp.arange(quarter).astype(jnp.float32) / quarter)
    positions = jnp.arange(GRID * GRID)
    col_part = (positions % GRID).astype(jnp.float32)[:, None] * frequency[None, :]
    row_part = (positions // GRID).astype(jnp.float32)[:, None] * frequency[None, :]
    return jnp.concatenate(
        [jnp.sin(col_part), jnp.cos(col_part), jnp.sin(row_part), jnp.cos(row_part)], axis=1
    )


def layer_norm(values, gain, shift):
    centered = values - jnp.mean(values, axis=-1, keepdims=True)
    scale = lax.rsqrt(jnp.mean(centered * centered, axis=-1, keepdims=True) + 1e-06)
    return centered * scale * gain + shift


def project(values, weight):
    lead = values.shape[:-1]
    flat = low(values).reshape(-1, values.shape[-1])
    return mat_plain(flat, weight).reshape(lead + (weight.shape[1],))


def linear(values, weight, shift):
    return low_back(project(values, weight)) + shift


def block(tokens, weights_in, weight_out, biases, heads):
    norm_one, shift_one, qv_bias, proj_bias, norm_two, shift_two, hidden_bias, out_bias = biases
    width = tokens.shape[-1]
    batch_n, seq_len = (tokens.shape[0], tokens.shape[1])
    normed = layer_norm(tokens, norm_one, shift_one)
    packed = project(normed, weights_in[:, : 3 * width])
    query = packed[..., :width] + qv_bias[:width]
    keyed = packed[..., width : 2 * width]
    valued = packed[..., 2 * width :] + qv_bias[width:]

    def split_heads(part):
        return low_back(low(part)).reshape(batch_n, seq_len, heads, width // heads)

    raw = score_mat(split_heads(query), split_heads(keyed))
    scores = low_back(raw) * (width // heads) ** (-0.5)
    probs = low_back(low(jax.nn.softmax(scores, axis=-1)))
    mixed = value_mat(probs, split_heads(valued))
    mixed = low_back(mixed).reshape(batch_n, seq_len, width)
    tokens = tokens + linear(mixed, weights_in[:, 3 * width : 4 * width], proj_bias)
    normed = layer_norm(tokens, norm_two, shift_two)
    hidden = jax.nn.gelu(linear(normed, weights_in[:, 4 * width :], hidden_bias), approximate=False)
    return tokens + linear(hidden, weight_out, out_bias)


def group_loss(
    enc_in, enc_fc2, dec_in, dec_fc2, head_w, small_vec, pixels, keep_idx, restore, denominator
):
    head_w = low(head_w)
    parts = small_parts(small_vec)
    images = pixels.astype(jnp.float32)
    batch_n = images.shape[0]
    kept = jnp.take_along_axis(images, keep_idx[:, :, None], axis=1)
    embed = linear(kept, enc_in[:, :D], parts[10]) + jnp.take(sincos_table(D), keep_idx, axis=0)
    cls_rows = jnp.broadcast_to(parts[11], (batch_n, 1, D))
    tokens = jnp.concatenate([cls_rows, embed], axis=1)
    tokens = block(tokens, enc_in[:, D : 5 * D + FF], enc_fc2, parts[0:8], HEADS)
    tokens = layer_norm(tokens, parts[8], parts[9])
    decoded = linear(tokens, enc_in[:, 5 * D + FF :], parts[12])
    masked = restore >= KEEP
    picked = jnp.take_along_axis(decoded[:, 1:], jnp.minimum(restore, KEEP - 1)[:, :, None], axis=1)
    filled = jnp.where(masked[:, :, None], parts[13], picked) + sincos_table(DD)
    sequence = jnp.concatenate([decoded[:, :1], filled], axis=1)
    sequence = block(sequence, dec_in, dec_fc2, parts[14:22], DHEADS)
    sequence = layer_norm(sequence, parts[22], parts[23])
    predicted = linear(sequence[:, 1:], head_w, parts[24])
    centered = images - jnp.mean(images, axis=-1, keepdims=True)
    target = centered * lax.rsqrt(jnp.mean(centered * centered, axis=-1, keepdims=True) + 1e-06)
    error = jnp.mean((predicted - target) ** 2, axis=-1)
    return jnp.sum(jnp.where(masked, error, 0.0)) / denominator


def adamw(weight, first, second, grad):
    first = beta_one * first + (1.0 - beta_one) * grad
    second = beta_two * second + (1.0 - beta_two) * grad * grad
    first_hat = first / (1.0 - beta_one**STEP)
    second_hat = second / (1.0 - beta_two**STEP)
    weight = weight - learn_rate * (
        first_hat / (jnp.sqrt(second_hat) + adam_eps) + decay_rate * weight
    )
    return (weight, first, second)


def local(
    pixels,
    keep_idx,
    restore,
    enc_in,
    enc_fc2,
    dec_in,
    dec_fc2,
    head_w,
    small_vec,
    m_enc_in,
    m_enc_fc2,
    m_dec_in,
    m_dec_fc2,
    m_head,
    m_small,
    v_enc_in,
    v_enc_fc2,
    v_dec_in,
    v_dec_fc2,
    v_head,
    v_small,
):
    enc_half = enc_in.astype(jnp.bfloat16)
    fc2_half = enc_fc2.astype(jnp.bfloat16)
    dec_half = dec_in.astype(jnp.bfloat16)
    dfc2_half = dec_fc2.astype(jnp.bfloat16)
    devices = lax.axis_size("row") * lax.axis_size("col")
    per_batch = pixels.shape[0] // MB
    denominator = 1.0 * pixels.shape[0] * devices * (PATCHES - KEEP)
    shard_sums = (
        jnp.zeros_like(enc_in),
        jnp.zeros_like(enc_fc2),
        jnp.zeros_like(dec_in),
        jnp.zeros_like(dec_fc2),
    )
    head_sum = jnp.zeros_like(head_w)
    small_sum = jnp.zeros_like(small_vec)
    loss_sum = jnp.zeros((), jnp.float32)
    for batch in range(MB):
        rows_done = (
            lax.all_gather(enc_half, "row", axis=0, tiled=True),
            lax.all_gather(fc2_half, "row", axis=0, tiled=True),
            lax.all_gather(dec_half, "row", axis=0, tiled=True),
            lax.all_gather(dfc2_half, "row", axis=0, tiled=True),
        )
        gathered = (
            lax.all_gather(rows_done[0], "col", axis=1, tiled=True),
            lax.all_gather(rows_done[1], "col", axis=1, tiled=True),
            lax.all_gather(rows_done[2], "col", axis=1, tiled=True),
            lax.all_gather(rows_done[3], "col", axis=1, tiled=True),
        )
        wide = tuple((matrix.astype(jnp.float32) for matrix in gathered))
        lower = batch * per_batch
        group_pix = pixels[lower : lower + per_batch]
        group_keep = keep_idx[lower : lower + per_batch]
        group_restore = restore[lower : lower + per_batch]

        def local_loss(*params):
            return group_loss(*params, group_pix, group_keep, group_restore, denominator)

        loss_value, pull = jax.vjp(
            local_loss, wide[0], wide[1], wide[2], wide[3], head_w, small_vec
        )
        grads = pull(jnp.ones((), jnp.float32))
        loss_sum = loss_sum + loss_value
        head_sum = head_sum + grads[4]
        small_sum = small_sum + grads[5]
        col_shares = (
            lax.psum_scatter(
                grads[0].astype(jnp.bfloat16), "col", scatter_dimension=1, tiled=True
            ).astype(jnp.float32),
            lax.psum_scatter(
                grads[1].astype(jnp.bfloat16), "col", scatter_dimension=1, tiled=True
            ).astype(jnp.float32),
            lax.psum_scatter(
                grads[2].astype(jnp.bfloat16), "col", scatter_dimension=1, tiled=True
            ).astype(jnp.float32),
            lax.psum_scatter(
                grads[3].astype(jnp.bfloat16), "col", scatter_dimension=1, tiled=True
            ).astype(jnp.float32),
        )
        owned = (
            lax.psum_scatter(col_shares[0], "row", scatter_dimension=0, tiled=True),
            lax.psum_scatter(col_shares[1], "row", scatter_dimension=0, tiled=True),
            lax.psum_scatter(col_shares[2], "row", scatter_dimension=0, tiled=True),
            lax.psum_scatter(col_shares[3], "row", scatter_dimension=0, tiled=True),
        )
        shard_sums = tuple((total + piece for total, piece in zip(shard_sums, owned)))
    head_grad, small_grad, loss = lax.psum((head_sum, small_sum, loss_sum), ("row", "col"))
    local_squares = sum((jnp.sum(piece * piece) for piece in shard_sums))
    total_squares = lax.psum(local_squares, ("row", "col"))
    grad_norm = jnp.sqrt(
        total_squares + jnp.sum(head_grad * head_grad) + jnp.sum(small_grad * small_grad)
    )
    factor = clip_limit / jnp.maximum(grad_norm, clip_limit)
    weights = (enc_in, enc_fc2, dec_in, dec_fc2, head_w, small_vec)
    firsts = (m_enc_in, m_enc_fc2, m_dec_in, m_dec_fc2, m_head, m_small)
    seconds = (v_enc_in, v_enc_fc2, v_dec_in, v_dec_fc2, v_head, v_small)
    all_grads = (shard_sums[0], shard_sums[1], shard_sums[2], shard_sums[3], head_grad, small_grad)
    results = [
        adamw(w, m, v, g * factor) for w, m, v, g in zip(weights, firsts, seconds, all_grads)
    ]
    return (
        results[0][0],
        results[1][0],
        results[2][0],
        results[3][0],
        results[4][0],
        results[5][0],
        results[0][1],
        results[1][1],
        results[2][1],
        results[3][1],
        results[4][1],
        results[5][1],
        results[0][2],
        results[1][2],
        results[2][2],
        results[3][2],
        results[4][2],
        results[5][2],
        loss,
        grad_norm,
    )


def solution(mesh):
    return jax.shard_map(
        local,
        mesh=mesh,
        in_specs=(
            P(("row", "col"), None, None),
            P(("row", "col"), None),
            P(("row", "col"), None),
            P("row", "col"),
            P("row", "col"),
            P("row", "col"),
            P("row", "col"),
            P(),
            P(),
            P("row", "col"),
            P("row", "col"),
            P("row", "col"),
            P("row", "col"),
            P(),
            P(),
            P("row", "col"),
            P("row", "col"),
            P("row", "col"),
            P("row", "col"),
            P(),
            P(),
        ),
        out_specs=(
            P("row", "col"),
            P("row", "col"),
            P("row", "col"),
            P("row", "col"),
            P(),
            P(),
            P("row", "col"),
            P("row", "col"),
            P("row", "col"),
            P("row", "col"),
            P(),
            P(),
            P("row", "col"),
            P("row", "col"),
            P("row", "col"),
            P("row", "col"),
            P(),
            P(),
            P(),
            P(),
        ),
        check_vma=False,
    )
```

profile of v0, /device:TPU:0, one launch (start us, length us, event | category | flops | bytes accessed | tf_op | source)
XLA Modules:
  0.0 1689.9 jit_solution(5379185401099883371)
XLA Ops:
  10.2 12.2 all_gather.36
  22.5 21.6 %all-gather.6.cloned.1.call-done = bf16[768,928]{1,0:T(8,128)(2,1)} async-done(((bf16[192,928]{1,0:T(8,128)(2,1)}), bf16[768,928]{1,0:T(8,128)(2,1)}) %all-gather.6.cloned.1.call-update) | async-done | bytes 1425424 | tf_op jit(solution)/shard_map/all_gather | solution.py:307
  46.8 11.8 all_gather.34
  114.0 86.9 %all-gather.8.cloned.1.call-done = bf16[768,7424]{0,1:T(8,128)(2,1)} async-done(((bf16[768,928]{0,1:T(8,128)(2,1)}), bf16[768,7424]{0,1:T(8,128)(2,1)}) %all-gather.8.cloned.1.call-update) | async-done | bytes 11403280 | tf_op jit(solution)/shard_map/all_gather | solution.py:313
  235.9 10.2 multiply_convert_fusion.3
  260.0 14.4 gather_fusion.2
  295.9 11.2 fusion.356
  307.2 23.3 %copy.273 = f32[6,16,197,197]{3,1,2,0:T(8,128)} copy(f32[6,16,197,197]{2,3,1,0:T(8,128)} %fusion.356) | data formatting | bytes 29805312 | tf_op jit(solution)/shard_map/jvp(nqhd,nkhd->nhqk)/dot_general | solution.py:92
  330.4 23.4 %fusion.343 = (f32[6,16,197]{1,2,0:T(8,128)S(1)}, f32[6,16,197,197]{3,1,2,0:T(8,128)}) fusion(f32[6,16,197,197]{3,1,2,0:T(8,128)} %copy.273), kind=kOutput, calls=%fused_computation.686 | output fusion | flops 14902852 | bytes 29880960 | tf_op jit(solution)/shard_map/jvp()/sub | solution.py:219
  376.4 23.5 %multiply_convert_fusion.1 = (bf16[6,197,2048]{2,1,0:T(8,128)(2,1)}, f32[6,197,2048]{2,1,0:T(8,128)}) fusion(f32[6,197,2048]{2,1,0:T(8,128)S(1)} %get-tuple-element.243, f32[2048]{0:T(1024)S(1)} %slice.286, u8[197,2048]{1,0:T(8,128)(4,1)S(1)} %get-tuple-element.242), kind=kLoop, calls=%fused_computation.66 | loop fusion | flops 167030784 | bytes 24619008 | tf_op jit(solution)/shard_map/jvp()/convert_element_type | solution.py:29
  425.0 12.9 fusion.329
  468.7 36.1 %fusion.8 = f32[6,16,197]{1,2,0:T(8,128)S(1)} fusion(f32[6,16,197,197]{3,1,2,0:T(8,128)} %get-tuple-element.239, bf16[6,16,197,197]{3,1,2,0:T(8,128)(2,1)} %copy.425, f32[6,16,197]{1,2,0:T(8,128)} %multiply_divide_fusion.1), kind=kLoop, calls=%fused_computation.22 | loop fusion | flops 14883744 | bytes 22505280 | tf_op jit(solution)/shard_map/transpose(jvp())/reduce_sum | solution.py:219
  553.3 10.7 scatter_custom_fusion
  635.9 10.1 multiply_convert_fusion.2
  650.7 14.3 gather_fusion.5
  686.8 11.3 fusion.358
  698.1 23.3 %copy.299 = f32[6,16,197,197]{3,1,2,0:T(8,128)} copy(f32[6,16,197,197]{2,3,1,0:T(8,128)} %fusion.358) | data formatting | bytes 29805312 | tf_op jit(solution)/shard_map/jvp(nqhd,nkhd->nhqk)/dot_general | solution.py:92
  721.4 23.2 %fusion.353 = (f32[6,16,197]{1,2,0:T(8,128)S(1)}, f32[6,16,197,197]{3,1,2,0:T(8,128)}) fusion(f32[6,16,197,197]{3,1,2,0:T(8,128)} %copy.299), kind=kOutput, calls=%fused_computation.692 | output fusion | flops 14902852 | bytes 29880960 | tf_op jit(solution)/shard_map/jvp()/sub | solution.py:219
  767.7 22.3 %multiply_convert_fusion = (bf16[6,197,2048]{2,1,0:T(8,128)(2,1)S(1)}, f32[6,197,2048]{2,1,0:T(8,128)S(1)}) fusion(f32[6,197,2048]{2,1,0:T(8,128)S(1)} %get-tuple-element.266, f32[2048]{0:T(1024)S(1)} %copy-done.242, u8[197,2048]{1,0:T(8,128)(4,1)S(1)} %get-tuple-element.265), kind=kLoop, calls=%fused_computation.52 | loop fusion | flops 167030784 | bytes 24619008 | tf_op jit(solution)/shard_map/jvp()/convert_element_type | solution.py:29
  806.7 9.9 fusion.330
  880.2 36.2 %fusion.13 = f32[6,16,197]{1,2,0:T(8,128)S(1)} fusion(f32[6,16,197,197]{3,1,2,0:T(8,128)} %get-tuple-element.262, bf16[6,16,197,197]{3,1,2,0:T(8,128)(2,1)} %copy.424, f32[6,16,197]{1,2,0:T(8,128)S(1)} %multiply_divide_fusion), kind=kLoop, calls=%fused_computation.27 | loop fusion | flops 14883744 | bytes 22505280 | tf_op jit(solution)/shard_map/transpose(jvp())/reduce_sum | solution.py:219
  970.4 10.5 scatter_custom_fusion.1
  1062.0 15.8 copy.333
  1107.4 15.9 copy.335
  1141.0 88.4 %reduce-scatter.37.cloned.1.call-done = bf16[928,768]{1,0:T(8,128)(2,1)} async-done(((bf16[7424,768]{1,0:T(8,128)(2,1)}), bf16[928,768]{1,0:T(8,128)(2,1)}) %reduce-scatter.37.cloned.1.call-update) | async-done | bytes 1425424
  1231.1 117.2 %reduce-scatter.39.cloned.1.call-done = bf16[928,768]{1,0:T(8,128)(2,1)} async-done(((bf16[7424,768]{1,0:T(8,128)(2,1)}), bf16[928,768]{1,0:T(8,128)(2,1)}) %reduce-scatter.39.cloned.1.call-update) | async-done | bytes 1425424
  1355.5 129.5 %all-reduce.96.cloned.1.call-done = (f32[512,768]{1,0:T(8,128)}, f32[21248]{0:T(1024)}) async-done(((f32[512,768]{1,0:T(8,128)}, f32[21248]{0:T(1024)}), (f32[512,768]{1,0:T(8,128)}, f32[21248]{0:T(1024)})) %all-reduce.96.cloned.1.call-update) | async-done | bytes 1657872 | tf_op jit(solution)/shard_map/psum | solution.py:355
  1487.5 24.9 %reduce-scatter.35.cloned.1.call-done = f32[512,64]{0,1:T(8,128)} async-done(((f32[2048,64]{0,1:T(8,128)}), f32[512,64]{0,1:T(8,128)}) %reduce-scatter.35.cloned.1.call-update) | async-done | bytes 131088 | tf_op jit(solution)/shard_map/reduce_scatter | solution.py:352
  1513.9 29.5 %reduce-scatter.33.cloned.1.call-done = f32[128,512]{1,0:T(8,128)} async-done(((f32[512,512]{1,0:T(8,128)}), f32[128,512]{1,0:T(8,128)}) %reduce-scatter.33.cloned.1.call-update) | async-done | bytes 262160 | tf_op jit(solution)/shard_map/reduce_scatter | solution.py:351
  1545.1 30.6 %reduce-scatter.31.cloned.1.call-done = f32[768,96]{0,1:T(8,128)} async-done(((f32[3072,96]{0,1:T(8,128)}), f32[768,96]{0,1:T(8,128)}) %reduce-scatter.31.cloned.1.call-update) | async-done | bytes 294928 | tf_op jit(solution)/shard_map/reduce_scatter | solution.py:350
  1577.3 45.4 %reduce-scatter.29.cloned.1.call-done = f32[192,928]{1,0:T(8,128)} async-done(((f32[768,928]{1,0:T(8,128)}), f32[192,928]{1,0:T(8,128)}) %reduce-scatter.29.cloned.1.call-update) | async-done | bytes 712720 | tf_op jit(solution)/shard_map/reduce_scatter | solution.py:349
  1628.7 39.3 %all-reduce.92 = (f32[]{:T(128)}, f32[]{:T(128)}) all-reduce(f32[]{:T(128)S(6)} %add.935, f32[]{:T(128)S(6)} %multiply.330), channel_id=1, replica_groups=mesh['row'=4,'col'=8] {'row','col'}, use_global_device_ids=true, to_apply=%region_86.90 | all-reduce | flops 2 | bytes 16 | tf_op jit(solution)/shard_map/psum | solution.py:357
  (1192 shorter events, 667.4 us)
Async XLA Ops:
  7.2 37.0 %all-gather.6.cloned.1.call-start = ((), (), s32[]{:S(2)}) async-start(), calls=%async_computation.12 | async-start | bytes 1966080 | tf_op jit(solution)/shard_map/all_gather | solution.py:307
  9.2 102.6 %all-gather.12.cloned.1.call-start = ((), (), s32[]{:S(2)}) async-start(), calls=%async_computation.15 | async-start | bytes 4718592 | tf_op jit(solution)/shard_map/all_gather | solution.py:315
  22.5 178.4 %all-gather.8.cloned.1.call-start = ((), (), s32[]{:S(2)}) async-start(), calls=%async_computation.13 | async-start | bytes 12828672 | tf_op jit(solution)/shard_map/all_gather | solution.py:313
  46.7 205.7 %all-gather.10.cloned.1.call-start = ((), (), s32[]{:S(2)}) async-start(), calls=%async_computation.14 | async-start | bytes 5308416 | tf_op jit(solution)/shard_map/all_gather | solution.py:314
  58.6 342.2 %all-gather.14.cloned.1.call-start = ((), (), s32[]{:S(2)}) async-start(), calls=%async_computation.16 | async-start | bytes 2359296 | tf_op jit(solution)/shard_map/all_gather | solution.py:316
  68.5 1065.6 %reduce-scatter.25.cloned.1.call-start = ((), (), s32[]{:S(2)}) async-start(), calls=%async_computation.21 | async-start | bytes 2359296 | tf_op jit(solution)/shard_map/reduce_scatter | solution.py:344
  69.2 355.8 %copy-start.241 = (f32[2048]{0:T(1024)}, f32[2048]{0:T(1024)S(1)}, u32[]{:S(2)}) copy-start(f32[2048]{0:T(1024)S(1)} %slice.286) | copy-start | bytes 24580
  71.0 205.1 %copy-start.293 = (pred[6,196]{1,0:T(8,128)(4,1)}, pred[6,196]{1,0:T(8,128)(4,1)S(1)}, u32[]{:S(2)}) copy-start(pred[6,196]{1,0:T(8,128)(4,1)S(1)} %get-tuple-element.203) | copy-start | bytes 3532
  71.7 207.5 %copy-start.232 = (f32[512]{0:T(512)}, f32[512]{0:T(512)S(1)}, u32[]{:S(2)}) copy-start(f32[512]{0:T(512)S(1)} %get-tuple-element.198) | copy-start | bytes 6148
  71.7 344.5 %copy-start.237 = (f32[512]{0:T(512)}, f32[512]{0:T(512)S(1)}, u32[]{:S(2)}) copy-start(f32[512]{0:T(512)S(1)} %get-tuple-element.189) | copy-start | bytes 6148
  71.7 372.0 %copy-start.235 = (f32[512]{0:T(512)}, f32[512]{0:T(512)S(1)}, u32[]{:S(2)}) copy-start(f32[512]{0:T(512)S(1)} %get-tuple-element.193) | copy-start | bytes 6148
  72.3 158.5 %copy-start.211 = (f32[768]{0:T(1024)}, f32[768]{0:T(1024)S(1)}, u32[]{:S(2)}) copy-start(f32[768]{0:T(1024)S(1)} %get-tuple-element.181) | copy-start | bytes 9220
  72.3 185.3 %copy-start.226 = (f32[768]{0:T(1024)}, f32[768]{0:T(1024)S(1)}, u32[]{:S(2)}) copy-start(f32[768]{0:T(1024)S(1)} %get-tuple-element.178) | copy-start | bytes 9220
  72.4 185.3 %copy-start.269 = (f32[768]{0:T(1024)}, f32[768]{0:T(1024)S(1)}, u32[]{:S(2)}) copy-start(f32[768]{0:T(1024)S(1)} %get-tuple-element.177) | copy-start | bytes 9220
  111.8 164.4 %copy-start.96 = (f32[196,512]{1,0:T(8,128)}, f32[196,512]{1,0:T(8,128)S(1)}, u32[]{:S(2)}) copy-start(f32[196,512]{1,0:T(8,128)S(1)} %pad_maximum_fusion.5) | copy-start | bytes 1204228
  679.0 455.2 %reduce-scatter.27.cloned.1.call-start = ((), (), s32[]{:S(2)}) async-start(), calls=%async_computation.22 | async-start | bytes 2359296 | tf_op jit(solution)/shard_map/reduce_scatter | solution.py:344
  831.8 304.3 %reduce-scatter.21.cloned.1.call-start = ((), (), s32[]{:S(2)}) async-start(), calls=%async_computation.19 | async-start | bytes 4718592 | tf_op jit(solution)/shard_map/reduce_scatter | solution.py:341
  859.6 276.5 %reduce-scatter.23.cloned.1.call-start = ((), (), s32[]{:S(2)}) async-start(), calls=%async_computation.20 | async-start | bytes 4718592 | tf_op jit(solution)/shard_map/reduce_scatter | solution.py:341
  951.0 187.6 %reduce-scatter.17.cloned.1.call-start = ((), (), s32[]{:S(2)}) async-start(), calls=%async_computation.17 | async-start | bytes 5308416 | tf_op jit(solution)/shard_map/reduce_scatter | solution.py:338
  956.9 181.7 %reduce-scatter.19.cloned.1.call-start = ((), (), s32[]{:S(2)}) async-start(), calls=%async_computation.18 | async-start | bytes 5308416 | tf_op jit(solution)/shard_map/reduce_scatter | solution.py:338
  998.3 231.1 %reduce-scatter.37.cloned.1.call-start = ((), (), s32[]{:S(2)}) async-start(), calls=%async_computation.27 | async-start | bytes 12828672
  1077.8 270.5 %reduce-scatter.39.cloned.1.call-start = ((), (), s32[]{:S(2)}) async-start(), calls=%async_computation.28 | async-start | bytes 12828672
  1123.3 361.7 %all-reduce.96.cloned.1.call-start = ((), (), s32[]{:S(2)}) async-start(), calls=%async_computation.29 | async-start | bytes 3317760 | tf_op jit(solution)/shard_map/psum | solution.py:355
  1134.0 378.4 %reduce-scatter.35.cloned.1.call-start = ((), (), s32[]{:S(2)}) async-start(), calls=%async_computation.26 | async-start | bytes 655360 | tf_op jit(solution)/shard_map/reduce_scatter | solution.py:352
  1136.0 407.4 %reduce-scatter.33.cloned.1.call-start = ((), (), s32[]{:S(2)}) async-start(), calls=%async_computation.25 | async-start | bytes 1310720 | tf_op jit(solution)/shard_map/reduce_scatter | solution.py:351
  1138.5 437.2 %reduce-scatter.31.cloned.1.call-start = ((), (), s32[]{:S(2)}) async-start(), calls=%async_computation.24 | async-start | bytes 1474560 | tf_op jit(solution)/shard_map/reduce_scatter | solution.py:350
  1141.0 481.7 %reduce-scatter.29.cloned.1.call-start = ((), (), s32[]{:S(2)}) async-start(), calls=%async_computation.23 | async-start | bytes 3932160 | tf_op jit(solution)/shard_map/reduce_scatter | solution.py:349
  1352.3 317.8 %copy-start.200 = (f32[21248]{0:T(1024)S(1)}, f32[21248]{0:T(1024)}, u32[]{:S(2)}) copy-start(f32[21248]{0:T(1024)} %param.35) | copy-start | bytes 254980
  1352.3 317.8 %copy-start.239 = (f32[21248]{0:T(1024)S(1)}, f32[21248]{0:T(1024)}, u32[]{:S(2)}) copy-start(f32[21248]{0:T(1024)} %param.41) | copy-start | bytes 254980
  1352.3 317.8 %copy-start.240 = (f32[21248]{0:T(1024)S(1)}, f32[21248]{0:T(1024)}, u32[]{:S(2)}) copy-start(f32[21248]{0:T(1024)} %param.47) | copy-start | bytes 254980
  1352.3 319.4 %copy-start.72 = (f32[512,768]{1,0:T(8,128)S(1)}, f32[512,768]{1,0:T(8,128)}, u32[]{:S(2)}) copy-start(f32[512,768]{1,0:T(8,128)} %param.34) | copy-start | bytes 4718596
  1485.0 186.8 %copy-start.73 = (f32[512,768]{1,0:T(8,128)S(1)}, f32[512,768]{1,0:T(8,128)}, u32[]{:S(2)}) copy-start(f32[512,768]{1,0:T(8,128)} %get-tuple-element.95) | copy-start | bytes 4718596
  (368 other events, 3059.7 us)
Sparse Core Ops, SparseCore 0:
  10.4 33.6 all-gather.5
  45.8 47.1 all-gather.11
  95.2 105.6 all-gather.7
  202.4 50.0 all-gather.9
  253.9 27.9 all-gather.13
  679.1 34.5 reduce-scatter.24
  831.9 34.6 reduce-scatter.26
  869.0 48.6 reduce-scatter.20
  951.1 48.5 reduce-scatter.22
  1001.8 53.1 reduce-scatter.16
  1057.4 53.3 reduce-scatter.18
  1112.9 116.4 reduce-scatter.36
  1231.8 116.4 reduce-scatter.38
  1354.2 130.7 all-reduce.95
  1488.4 23.9 reduce-scatter.34
  1515.7 27.6 reduce-scatter.32
  1547.0 28.5 reduce-scatter.30
  1578.7 43.9 reduce-scatter.28
where the time goes:
time: 1700 us; the launch traced here: 1690 us
  waiting for transfers between devices  581 us (34%)
  other arithmetic  408 us (24%)
  matrix products  317 us (19%)
  local copies, waits for them, and re-layouts  283 us (17%)
  blocking collectives  73.1 us (4%)
  between operations  26.8 us (2%)
    unnamed x20, waiting for transfers between devices  206 us
    dot_general x42, matrix products, mat_plain(): return wrapped(left, right)  153 us
    psum x1, waiting for transfers between devices, local(): lax.psum((head_sum, small_sum, loss_sum), ('row', 'col'))  129 us
    convert_element_type x24, other arithmetic, low_value(): return lax.optimization_barrier(v.astype(jnp.bfloat16)).astype(jnp.float32)  104 us
    all_gather x1, waiting for transfers between devices, local(): lax.all_gather(rows_done[0], 'col', axis=1, tiled=True)  86.9 us
    unnamed x772, local copies, waits for them, and re-layouts  84.6 us
    reduce_sum x4, other arithmetic, block(): probs = low_back(low(jax.nn.softmax(scores, axis=-1)))  73.4 us
    dot_general x22, matrix products, mat_value(): return jnp.dot(half(left), half(right), preferred_element_type=jnp.float32)  71.3 us
  transfers between devices with their start and end apart: 18, of which 10 were waited for; matrix products, arithmetic and copies ran while one was open for 40% of the time, Pallas kernels for 0%

commit v1 on v0

v1 whole, which is shorter than its diff:
```python
import functools
import math

import jax
import jax.numpy as jnp
import ml_dtypes
import numpy as np
from jax import lax
from jax.experimental import pallas as pl
from jax.experimental.pallas import tpu as pltpu
from jax.sharding import PartitionSpec as P

D = 768
HEADS = 12
FF = 3072
DD = 512
DHEADS = 16
DFF = 2048
PIX = 768
GRID = 14
PATCHES = 196
KEEP = 49
STEP = 10
SMALL = 21248
ES = 56
DS = 208
SEL = 80
NOROW = 255
f32 = jnp.float32
bf = jnp.bfloat16

LENS = [
    D, D, 2 * D, D, D, D, FF, D, D, D, D, D,
    DD, DD, DD, DD, 2 * DD, DD, DD, DD, DFF, DD, DD, DD, PIX,
]
OFF = [0]
for piece in LENS:
    OFF.append(OFF[-1] + piece)


def part(ref, i):
    return ref[:, OFF[i] : OFF[i + 1]]


def dg(a, b, ca, cb):
    return lax.dot_general(a, b, (((ca,), (cb,)), ((), ())), preferred_element_type=f32)


def nn(a, b):
    return dg(a, b, 1, 0)


def nt(a, b):
    return dg(a, b, 1, 1)


def rows(total, size, fn):
    @pl.loop(0, total // size)
    def _(i):
        fn(pl.ds(pl.multiple_of(i * size, size), size))


def cols(total, size, fn):
    @pl.loop(0, total // size)
    def _(i):
        fn(pl.multiple_of(i * size, size))


def pieces(x):
    hi = x.astype(bf)
    rest = x - hi.astype(f32)
    mid = rest.astype(bf)
    low = (rest - mid.astype(f32)).astype(bf)
    return hi, mid, low


def gelu_pair(x):
    ax = jnp.abs(x)
    d = 1.0 + (0.3275911 * 0.7071067811865476) * ax
    r = pl.reciprocal(d, approx=True)
    t = r * (2.0 - d * r)
    e = jnp.exp(-0.5 * (x * x))
    poly = ((((0.5 * 1.061405429 * t - 0.5 * 1.453152027) * t + 0.5 * 1.421413741) * t
             - 0.5 * 0.284496736) * t + 0.5 * 0.254829592) * t
    q = poly * e
    phi = jnp.where(x >= 0.0, 1.0 - q, q)
    return x * phi, phi + x * (e * 0.3989422804014327)


def norm_rows(x, gain, shift):
    c = x - jnp.mean(x, axis=1, keepdims=True)
    rs = lax.rsqrt(jnp.mean(c * c, axis=1, keepdims=True) + 1e-06)
    xh = c * rs
    return xh, rs, xh * gain + shift


def norm_back(da, xh, rs, gain):
    g = da * gain
    m1 = jnp.mean(g, axis=1, keepdims=True)
    m2 = jnp.mean(g * xh, axis=1, keepdims=True)
    return rs * (g - m1 - xh * m2)


def rsum(x):
    return jnp.sum(x, axis=0, keepdims=True)


def lanes_of(x, h, hd):
    lane = lax.broadcasted_iota(jnp.int32, (1, 128), 1)
    return jnp.where((lane >= h * hd) & (lane < (h + 1) * hd), x, jnp.zeros_like(x))


def att_fwd(qkv, o, p, bias, rsl, width, g, slot, hd):
    c0 = pl.multiple_of(g * 128, 128)
    q = qkv[rsl, pl.ds(c0, 128)]
    k = qkv[rsl, pl.ds(pl.multiple_of(c0 + width, 128), 128)]
    v = qkv[rsl, pl.ds(pl.multiple_of(c0 + 2 * width, 128), 128)]
    acc = None
    for h in range(128 // hd):
        s = nt(lanes_of(k, h, hd), q) * (hd ** -0.5) + bias
        e = jnp.exp(s - jnp.max(s, axis=0, keepdims=True))
        pr = (e * (1.0 / jnp.sum(e, axis=0, keepdims=True))).astype(bf)
        p[slot + h] = pr
        t = dg(pr, lanes_of(v, h, hd), 0, 0)
        acc = t if acc is None else acc + t
    o[rsl, pl.ds(c0, 128)] = acc.astype(bf)


def att_bwd(qkv, do, p, dqkv, rsl, width, g, slot, hd):
    c0 = pl.multiple_of(g * 128, 128)
    c1 = pl.multiple_of(c0 + width, 128)
    c2 = pl.multiple_of(c0 + 2 * width, 128)
    q = qkv[rsl, pl.ds(c0, 128)]
    k = qkv[rsl, pl.ds(c1, 128)]
    v = qkv[rsl, pl.ds(c2, 128)]
    d = do[rsl, pl.ds(c0, 128)]
    aq = ak = av = None
    for h in range(128 // hd):
        pr = p[slot + h]
        dp = nt(lanes_of(v, h, hd), d).astype(bf).astype(f32)
        pf = pr.astype(f32)
        t = pf * dp
        ds = ((t - pf * jnp.sum(t, axis=0, keepdims=True)) * (hd ** -0.5)).astype(bf)
        tv = nn(pr, lanes_of(d, h, hd))
        tk = nn(ds, lanes_of(q, h, hd))
        tq = dg(ds, lanes_of(k, h, hd), 0, 0)
        if h == 0:
            aq, ak, av = tq, tk, tv
        else:
            aq, ak, av = aq + tq, ak + tk, av + tv
    dqkv[rsl, pl.ds(c0, 128)] = aq.astype(bf)
    dqkv[rsl, pl.ds(c1, 128)] = ak.astype(bf)
    dqkv[rsl, pl.ds(c2, 128)] = av.astype(bf)


def dec_kernel(scale, nb, y, codec, coder, pix, pos, sv, win, wout, hw,
               dy, dwin, dwout, dhw, dsm, loss,
               x, t, xh1, xh2, xhf, rs1, rs2, rsf, tm, tr, a1, a2, u, o, qkv, p, hid, gp, dpr, d16, lacc):
    M = nb * DS
    R = 32
    W = DD

    @pl.when(pl.program_id(0) == 0)
    def _():
        dsm[...] = jnp.zeros_like(dsm)
        loss[...] = jnp.zeros_like(loss)
        lacc[...] = jnp.zeros_like(lacc)
        for ref in (dwin, dwout, dhw):
            rows(ref.shape[0], 16, lambda r: ref.__setitem__((r, slice(None)), jnp.zeros((16, ref.shape[1]), f32)))

    def gsum(i, v, lo=0, n=None):
        a = OFF[i] + lo
        n = LENS[i] if n is None else n
        dsm[:, pl.ds(a, n)] += rsum(v)

    for b in range(nb):
        pick = (codec[b] == lax.broadcasted_iota(jnp.int32, (DS, SEL), 1)).astype(f32).astype(bf)
        tok = jnp.where(lax.broadcasted_iota(jnp.int32, (8, W), 0) == 0, part(sv, 13), 0.0)
        table = jnp.concatenate([y[b], jnp.zeros((8, W), f32), tok, jnp.zeros((8, W), f32)], axis=0)
        z = pos[...]
        for piece in pieces(table):
            z = z + nn(pick, piece)
        x[b * DS : (b + 1) * DS, :] = z

    def ln1(r):
        xh, rs, a = norm_rows(x[r, :], part(sv, 14), part(sv, 15))
        xh1[r, :] = xh
        rs1[r, :] = rs
        a1[r, :] = a.astype(bf)
    rows(M, R, ln1)

    qkv[:, 0:W] = (nn(a1[...], win[:, 0:W]) + sv[:, OFF[16] : OFF[16] + W]).astype(bf)
    qkv[:, W : 2 * W] = nn(a1[...], win[:, W : 2 * W]).astype(bf)
    qkv[:, 2 * W :] = (nn(a1[...], win[:, 2 * W : 3 * W]) + sv[:, OFF[16] + W : OFF[17]]).astype(bf)

    bias = jnp.where(lax.broadcasted_iota(jnp.int32, (DS, 1), 0) <= PATCHES, 0.0, -1e30).astype(f32)

    @pl.loop(0, nb * 4)
    def _(i):
        rsl = pl.ds(pl.multiple_of((i // 4) * DS, 16), DS)
        att_fwd(qkv, o, p, bias, rsl, W, i % 4, i * 4, 32)

    x[...] += nn(o[...], win[:, 3 * W : 4 * W]) + part(sv, 17)

    def ln2(r):
        xh, rs, a = norm_rows(x[r, :], part(sv, 18), part(sv, 19))
        xh2[r, :] = xh
        rs2[r, :] = rs
        a2[r, :] = a.astype(bf)
    rows(M, R, ln2)

    def fc1(c):
        h = nn(a2[...], win[:, pl.ds(pl.multiple_of(4 * W + c, 256), 256)])
        g, dg_ = gelu_pair(h + sv[:, pl.ds(pl.multiple_of(OFF[20] + c, 128), 256)])
        hid[:, pl.ds(c, 256)] = g.astype(bf)
        gp[:, pl.ds(c, 256)] = dg_.astype(bf)
    cols(DFF, 256, fc1)

    x[...] += nt(hid[...], wout[...]) + part(sv, 21)

    def lnf(r):
        xh, rs, a = norm_rows(x[r, :], part(sv, 22), part(sv, 23))
        xhf[r, :] = xh
        rsf[r, :] = rs
        u[r, :] = a.astype(bf)
    rows(M, R, lnf)

    for b in range(nb):
        def tstat(r):
            v = pix[b, r, :].astype(f32)
            m = jnp.mean(v, axis=1, keepdims=True)
            c = v - m
            q = pl.ds(pl.multiple_of(b * DS + r.start, 16), 16)
            tm[q, :] = m
            tr[q, :] = lax.rsqrt(jnp.mean(c * c, axis=1, keepdims=True) + 1e-06)
        rows(DS, 16, tstat)

    def headc(c):
        hwc = hw[:, pl.ds(c, 256)].astype(bf)
        pr = nn(u[...], hwc) + sv[:, pl.ds(pl.multiple_of(OFF[24] + c, 128), 256)]
        for b in range(nb):
            sl = slice(b * DS, (b + 1) * DS)
            tgt = (pix[b, :, pl.ds(c, 256)].astype(f32) - tm[sl, :]) * tr[sl, :]
            diff = jnp.where(codec[b] == 64, pr[sl] - tgt, 0.0)
            lacc[:, 0:256] += rsum(diff * diff)
            dp = diff * (2.0 * scale / PIX)
            dsm[:, pl.ds(pl.multiple_of(OFF[24] + c, 128), 256)] += rsum(dp)
            dpr[sl, pl.ds(c, 256)] = dp.astype(bf)
    cols(PIX, 256, headc)

    def hgrad(c):
        dhw[:, pl.ds(c, 256)] += dg(u[...], dpr[:, pl.ds(c, 256)], 0, 0)
    cols(PIX, 256, hgrad)
    t[...] = nt(dpr[...], hw[...].astype(bf))

    def lnfb(r):
        da = t[r, :]
        xh = xhf[r, :]
        gsum(22, da * xh)
        gsum(23, da)
        dx = norm_back(da, xh, rsf[r, :], part(sv, 22))
        gsum(21, dx)
        x[r, :] = dx
        d16[r, :] = dx.astype(bf)
    rows(M, R, lnfb)

    def fc1b(c):
        cs = pl.ds(c, 256)
        dwout[:, cs] += dg(d16[...], hid[:, cs], 0, 0)
        dh = nn(d16[...], wout[:, cs]) * gp[:, cs].astype(f32)
        dsm[:, pl.ds(pl.multiple_of(OFF[20] + c, 128), 256)] += rsum(dh)
        dh16 = dh.astype(bf)
        gp[:, cs] = dh16
        wc = pl.ds(pl.multiple_of(4 * W + c, 256), 256)
        dwin[:, wc] += dg(a2[...], dh16, 0, 0)
    cols(DFF, 256, fc1b)
    t[...] = nt(gp[...], win[:, 4 * W :])

    def ln2b(r):
        da = t[r, :]
        xh = xh2[r, :]
        gsum(18, da * xh)
        gsum(19, da)
        dx = x[r, :] + norm_back(da, xh, rs2[r, :], part(sv, 18))
        gsum(17, dx)
        x[r, :] = dx
        d16[r, :] = dx.astype(bf)
    rows(M, R, ln2b)

    dwin[:, 3 * W : 4 * W] += dg(o[...], d16[...], 0, 0)
    o[...] = nt(d16[...], win[:, 3 * W : 4 * W]).astype(bf)
    dqkv = gp

    @pl.loop(0, nb * 4)
    def _(i):
        rsl = pl.ds(pl.multiple_of((i // 4) * DS, 16), DS)
        att_bwd(qkv, o, p, dqkv, rsl, W, i % 4, i * 4, 32)

    def wq(c):
        cs = pl.ds(c, 256)
        dwin[:, cs] += dg(a1[...], dqkv[:, cs], 0, 0)
    cols(3 * W, 256, wq)
    def qb(r):
        dsm[:, OFF[16] : OFF[16] + W] += rsum(dqkv[r, 0:W].astype(f32))
        dsm[:, OFF[16] + W : OFF[17]] += rsum(dqkv[r, 2 * W : 3 * W].astype(f32))
    rows(M, R, qb)
    t[...] = nt(dqkv[:, 0 : 3 * W], win[:, 0 : 3 * W])

    def ln1b(r):
        da = t[r, :]
        xh = xh1[r, :]
        gsum(14, da * xh)
        gsum(15, da)
        x[r, :] = x[r, :] + norm_back(da, xh, rs1[r, :], part(sv, 14))
    rows(M, R, ln1b)

    for b in range(nb):
        pick = (coder[b] == lax.broadcasted_iota(jnp.int32, (SEL, DS), 0)).astype(f32).astype(bf)
        out = None
        for piece in pieces(x[b * DS : (b + 1) * DS, :]):
            v = nn(pick, piece)
            out = v if out is None else out + v
        dy[b] = out[0:ES]
        dsm[:, OFF[13] : OFF[14]] += out[64:65]

    @pl.when(pl.program_id(0) == pl.num_programs(0) - 1)
    def _():
        loss[...] = jnp.broadcast_to(jnp.sum(lacc[...], axis=1, keepdims=True) * (scale / PIX), (1, 128))


def decoder(y, codec, coder, pix, pos, sv, win, wout, hw, scale, nb=2):
    n = y.shape[0]
    M = nb * DS
    whole = lambda a: pl.BlockSpec(a.shape, lambda i: (0,) * a.ndim, pipeline_mode=pl.Buffered(1))
    fixed = lambda s: pl.BlockSpec(s, lambda i: (0,) * len(s), pipeline_mode=pl.Buffered(1))
    blk = lambda s: pl.BlockSpec((nb,) + s, lambda i: (i, 0, 0))
    V = pltpu.VMEM
    return pl.pallas_call(
        functools.partial(dec_kernel, scale, nb),
        grid=(n // nb,),
        in_specs=[blk((ES, DD)), blk((DS, 1)), blk((1, DS)), blk((DS, PIX)), whole(pos), whole(sv), whole(win), whole(wout), whole(hw)],
        out_specs=[blk((ES, DD)), fixed(win.shape), fixed(wout.shape), fixed(hw.shape), fixed((1, SMALL)), fixed((1, 128))],
        out_shape=[
            jax.ShapeDtypeStruct((n, ES, DD), f32), jax.ShapeDtypeStruct(win.shape, f32),
            jax.ShapeDtypeStruct(wout.shape, f32), jax.ShapeDtypeStruct(hw.shape, f32),
            jax.ShapeDtypeStruct((1, SMALL), f32), jax.ShapeDtypeStruct((1, 128), f32)],
        scratch_shapes=[
            V((M, DD), f32), V((M, DD), f32), V((M, DD), f32), V((M, DD), f32), V((M, DD), f32),
            V((M, 1), f32), V((M, 1), f32), V((M, 1), f32), V((M, 1), f32), V((M, 1), f32),
            V((M, DD), bf), V((M, DD), bf), V((M, DD), bf), V((M, DD), bf), V((M, 3 * DD), bf),
            V((nb * DHEADS, DS, DS), bf), V((M, DFF), bf), V((M, DFF), bf), V((M, PIX), bf), V((M, DD), bf),
            V((1, 256), f32)],
        compiler_params=pltpu.CompilerParams(vmem_limit_bytes=60 << 20),
        name="decoder",
    )(y, codec, coder, pix, pos, sv, win, wout, hw)


EG = 4 * ES
O_Q, O_P, O_F, O_E = D, 4 * D, 5 * D, 5 * D + FF


def enc_fwd_kernel(pix, keepc, pos3, sv, win, wout,
                   y, kept, xh1, xh2, xhf, rs1, rs2, rsf, a1, a2, e16, o, qkv, p, hid, gp, x, bias):
    n = pix.shape[0]
    M = n * ES
    R = 32
    W = D
    for i in range(0, n, 2):
        two = []
        for b in (i, i + 1):
            kc = keepc[b * ES : (b + 1) * ES, :]
            pick = (kc == lax.broadcasted_iota(jnp.int32, (ES, DS), 1)).astype(f32).astype(bf)
            two.append(nn(pick, pix[b]))
        kept[i * ES : (i + 2) * ES, :] = jnp.concatenate(two, axis=0).astype(bf)
    for lo in range(0, M, EG):
        sl = slice(lo, lo + EG)
        kc = keepc[sl, :]
        pick = (kc == lax.broadcasted_iota(jnp.int32, (EG, DS), 1)).astype(f32).astype(bf)
        v = nn(kept[sl, :], win[:, 0:W]) + part(sv, 10)
        v = v + nn(pick, pos3[0:DS, :]) + nn(pick, pos3[DS : 2 * DS, :]) + nn(pick, pos3[2 * DS :, :])
        x[sl, :] = jnp.where(kc < PATCHES, v, jnp.where(kc == NOROW - 1, part(sv, 11), 0.0))

    def ln1(r):
        xh, rs, a = norm_rows(x[r, :], part(sv, 0), part(sv, 1))
        xh1[r, :] = xh
        rs1[r, :] = rs
        a1[r, :] = a.astype(bf)
    rows(M, R, ln1)
    qkv[:, 0:W] = (nn(a1[...], win[:, O_Q : O_Q + W]) + sv[:, OFF[2] : OFF[2] + W]).astype(bf)
    qkv[:, W : 2 * W] = nn(a1[...], win[:, O_Q + W : O_Q + 2 * W]).astype(bf)
    qkv[:, 2 * W :] = (nn(a1[...], win[:, O_Q + 2 * W : O_P]) + sv[:, OFF[2] + W : OFF[3]]).astype(bf)

    ki = lax.broadcasted_iota(jnp.int32, (EG, EG), 0)
    qi = lax.broadcasted_iota(jnp.int32, (EG, EG), 1)
    same = jnp.zeros((EG, EG), jnp.bool_)
    for j in range(4):
        same = same | ((ki >= j * ES) & (ki < j * ES + KEEP + 1) & (qi >= j * ES) & (qi < (j + 1) * ES))
    bias[...] = jnp.where(same, 0.0, -1e30).astype(f32)

    @pl.loop(0, (n // 4) * 6)
    def _(i):
        rsl = pl.ds(pl.multiple_of((i // 6) * EG, 16), EG)
        att_fwd(qkv, o, p, bias[...], rsl, W, i % 6, i * 2, 64)

    x[...] += nn(o[...], win[:, O_P : O_P + W]) + part(sv, 3)

    def ln2(r):
        xh, rs, a = norm_rows(x[r, :], part(sv, 4), part(sv, 5))
        xh2[r, :] = xh
        rs2[r, :] = rs
        a2[r, :] = a.astype(bf)
    rows(M, R, ln2)

    def fc1(c):
        h = nn(a2[...], win[:, pl.ds(pl.multiple_of(O_F + c, 256), 256)])
        g, dg_ = gelu_pair(h + sv[:, pl.ds(pl.multiple_of(OFF[6] + c, 128), 256)])
        hid[:, pl.ds(c, 256)] = g.astype(bf)
        gp[:, pl.ds(c, 256)] = dg_.astype(bf)
    cols(FF, 256, fc1)
    x[...] += nt(hid[...], wout[...]) + part(sv, 7)

    def lnf(r):
        xh, rs, a = norm_rows(x[r, :], part(sv, 8), part(sv, 9))
        xhf[r, :] = xh
        rsf[r, :] = rs
        e16[r, :] = a.astype(bf)
    rows(M, R, lnf)
    y[...] = nn(e16[...], win[:, O_E:]) + part(sv, 12)


def vspec(k):
    return [pl.BlockSpec(memory_space=pltpu.VMEM)] * k


def encoder_fwd(pix, keepc, pos3, sv, win, wout):
    n = pix.shape[0]
    M = n * ES
    S = jax.ShapeDtypeStruct
    V = pltpu.VMEM
    outs = [S((M, DD), f32), S((M, D), bf), S((M, D), f32), S((M, D), f32), S((M, D), f32),
            S((M, 1), f32), S((M, 1), f32), S((M, 1), f32), S((M, D), bf), S((M, D), bf), S((M, D), bf), S((M, D), bf),
            S((M, 3 * D), bf), S((n // 4 * HEADS, EG, EG), bf), S((M, FF), bf), S((M, FF), bf)]
    return pl.pallas_call(
        enc_fwd_kernel,
        in_specs=vspec(6), out_specs=vspec(len(outs)), out_shape=outs,
        scratch_shapes=[V((M, D), f32), V((EG, EG), f32)],
        compiler_params=pltpu.CompilerParams(vmem_limit_bytes=60 << 20),
        name="encoder_fwd",
    )(pix, keepc, pos3, sv, win, wout)


def enc_bwd_kernel(dy, keepc, sv, win, wout, kept, xh1, xh2, xhf, rs1, rs2, rsf, a1, a2, e16, o, qkv, p, hid, gp,
                   dwin, dwout, dsm, x, t, d16, dqkv, stage, sem):
    M = dy.shape[0]
    R = 32
    W = D
    CW = 256
    dsm[...] = jnp.zeros_like(dsm)

    def gsum(i, v, lo=0, n=None):
        a = OFF[i] + lo
        n = LENS[i] if n is None else n
        dsm[:, pl.ds(a, n)] += rsum(v)

    def put(out, count, base, value):
        def copy(i, slot):
            return pltpu.make_async_copy(stage.at[slot], out.at[:, pl.ds(pl.multiple_of(base + i * CW, 128), CW)], sem.at[slot])

        @pl.loop(0, count)
        def _(i):
            slot = lax.rem(i, 2)

            @pl.when(i >= 2)
            def _():
                copy(i - 2, slot).wait()
            stage[slot] = value(pl.multiple_of(i * CW, CW)).astype(bf)
            copy(i, slot).start()
        for i in range(max(count - 2, 0), count):
            copy(i, i % 2).wait()

    def emb(r):
        v = dy[r, :]
        gsum(12, v)
        d16[r, 0:DD] = v.astype(bf)
    rows(M, R, emb)
    put(dwin, DD // CW, O_E, lambda c: dg(e16[...], d16[:, pl.ds(c, CW)], 0, 0))
    t[...] = nt(d16[:, 0:DD], win[:, O_E:])

    def lnfb(r):
        da = t[r, :]
        xh = xhf[r, :]
        gsum(8, da * xh)
        gsum(9, da)
        dx = norm_back(da, xh, rsf[r, :], part(sv, 8))
        gsum(7, dx)
        x[r, :] = dx
        d16[r, :] = dx.astype(bf)
    rows(M, R, lnfb)
    put(dwout, FF // CW, 0, lambda c: dg(d16[...], hid[:, pl.ds(c, CW)], 0, 0))

    def fc1b(c):
        cs = pl.ds(c, CW)
        dh = nn(d16[...], wout[:, cs]) * gp[:, cs].astype(f32)
        dsm[:, pl.ds(pl.multiple_of(OFF[6] + c, 128), CW)] += rsum(dh)
        gp[:, cs] = dh.astype(bf)
        return dg(a2[...], gp[:, cs], 0, 0)
    put(dwin, FF // CW, O_F, fc1b)
    t[...] = nt(gp[...], win[:, O_F:O_E])

    def ln2b(r):
        da = t[r, :]
        xh = xh2[r, :]
        gsum(4, da * xh)
        gsum(5, da)
        dx = x[r, :] + norm_back(da, xh, rs2[r, :], part(sv, 4))
        gsum(3, dx)
        x[r, :] = dx
        d16[r, :] = dx.astype(bf)
    rows(M, R, ln2b)
    put(dwin, D // CW, O_P, lambda c: dg(o[...], d16[:, pl.ds(c, CW)], 0, 0))
    d16[...] = nt(d16[...], win[:, O_P:O_F]).astype(bf)

    @pl.loop(0, (M // EG) * 6)
    def _(i):
        rsl = pl.ds(pl.multiple_of((i // 6) * EG, 16), EG)
        att_bwd(qkv, d16, p, dqkv, rsl, W, i % 6, i * 2, 64)

    put(dwin, 3 * D // CW, O_Q, lambda c: dg(a1[...], dqkv[:, pl.ds(c, CW)], 0, 0))
    def qb(r):
        dsm[:, OFF[2] : OFF[2] + W] += rsum(dqkv[r, 0:W].astype(f32))
        dsm[:, OFF[2] + W : OFF[3]] += rsum(dqkv[r, 2 * W : 3 * W].astype(f32))
    rows(M, R, qb)
    t[...] = nt(dqkv[...], win[:, O_Q:O_P])

    def ln1b(r):
        da = t[r, :]
        xh = xh1[r, :]
        gsum(0, da * xh)
        gsum(1, da)
        dx = x[r, :] + norm_back(da, xh, rs1[r, :], part(sv, 0))
        kc = keepc[r, :]
        gsum(11, jnp.where(kc == NOROW - 1, dx, 0.0))
        dx = jnp.where(kc < PATCHES, dx, 0.0)
        gsum(10, dx)
        d16[r, :] = dx.astype(bf)
    rows(M, R, ln1b)
    put(dwin, D // CW, 0, lambda c: dg(kept[...], d16[:, pl.ds(c, CW)], 0, 0))


def encoder_bwd(dy, keepc, sv, win, wout, saved):
    M = dy.shape[0]
    S = jax.ShapeDtypeStruct
    V = pltpu.VMEM
    anyspec = pl.BlockSpec(memory_space=pl.ANY)
    return pl.pallas_call(
        enc_bwd_kernel,
        in_specs=vspec(5 + len(saved)),
        out_specs=[anyspec, anyspec, pl.BlockSpec(memory_space=pltpu.VMEM)],
        out_shape=[S(win.shape, bf), S(wout.shape, bf), S((1, SMALL), f32)],
        scratch_shapes=[V((M, D), f32), V((M, D), f32), V((M, D), bf), V((M, 3 * D), bf), V((2, D, 256), bf),
                        pltpu.SemaphoreType.DMA((2,))],
        compiler_params=pltpu.CompilerParams(vmem_limit_bytes=62 << 20),
        name="encoder_bwd",
    )(dy, keepc, sv, win, wout, *saved)


def sincos_np(width):
    quarter = width // 4
    freq = (1.0 / np.float32(10000.0) ** (np.arange(quarter, dtype=np.float32) / np.float32(quarter))).astype(np.float32)
    pos = np.arange(GRID * GRID)
    cp = (pos % GRID).astype(np.float32)[:, None] * freq[None, :]
    rp = (pos // GRID).astype(np.float32)[:, None] * freq[None, :]
    return np.concatenate([np.sin(cp), np.cos(cp), np.sin(rp), np.cos(rp)], axis=1).astype(np.float32)


def tables():
    dec = np.zeros((DS, DD), np.float32)
    dec[:PATCHES] = sincos_np(DD)
    enc = np.zeros((DS, D), np.float32)
    enc[:PATCHES] = sincos_np(D)
    b = ml_dtypes.bfloat16
    hi = enc.astype(b)
    mid = (enc - hi.astype(np.float32)).astype(b)
    lo = (enc - hi.astype(np.float32) - mid.astype(np.float32)).astype(b)
    return dec, np.concatenate([hi, mid, lo], axis=0)


def step(pixels, keep, restore, A, BT, C, DT, hw, small, denom):
    n = pixels.shape[0]
    dec_pos, enc_pos = tables()
    pix = jnp.pad(pixels, ((0, 0), (0, DS - PATCHES), (0, 0)))
    keepc = jnp.concatenate([keep, jnp.full((n, 1), NOROW - 1, jnp.int32), jnp.full((n, ES - KEEP - 1), NOROW, jnp.int32)], axis=1).reshape(n * ES, 1)
    code = jnp.concatenate([jnp.where(restore < KEEP, restore, 64), jnp.full((n, 1), KEEP, jnp.int32), jnp.full((n, DS - PATCHES - 1), NOROW, jnp.int32)], axis=1)
    sv = small.reshape(1, SMALL)
    fw = encoder_fwd(pix, keepc, jnp.asarray(enc_pos), sv, A, BT)
    y, saved = fw[0], fw[1:]
    dy, dC, dDT, dhw, dsm_d, loss = decoder(y.reshape(n, ES, DD), code.reshape(n, DS, 1), code.reshape(n, 1, DS), pix, jnp.asarray(dec_pos), sv, C, DT, hw, 1.0 / denom)
    dA, dBT, dsm_e = encoder_bwd(dy.reshape(n * ES, DD), keepc, sv, A, BT, saved)
    return dA, dBT, dC, dDT, dhw, (dsm_d + dsm_e).reshape(SMALL), loss[0, 0]


def adamw(weight, first, second, grad):
    first = 0.9 * first + (1.0 - 0.9) * grad
    second = 0.999 * second + (1.0 - 0.999) * grad * grad
    first_hat = first / (1.0 - 0.9**STEP)
    second_hat = second / (1.0 - 0.999**STEP)
    weight = weight - 0.08 * (first_hat / (jnp.sqrt(second_hat) + 1e-08) + 0.05 * weight)
    return (weight, first, second)


def local(pixels, keep_idx, restore, *state):
    weights, firsts, seconds = state[0:6], state[6:12], state[12:18]
    devices = lax.axis_size("row") * lax.axis_size("col")
    denom = 1.0 * pixels.shape[0] * devices * (PATCHES - KEEP)

    def gather(v, flip):
        v = v.astype(bf)
        v = lax.all_gather(v, "row", axis=0, tiled=True)
        v = lax.all_gather(v, "col", axis=1, tiled=True)
        return v.T if flip else v

    A, BT, C, DT = (gather(w, f) for w, f in zip(weights[0:4], (False, True, False, True)))
    dA, dBT, dC, dDT, dhw, dsm, loss = step(pixels, keep_idx, restore, A, BT, C, DT, weights[4], weights[5], denom)

    def scatter(v, flip):
        v = v.astype(bf)
        v = v.T if flip else v
        v = lax.psum_scatter(v, "col", scatter_dimension=1, tiled=True)
        return lax.psum_scatter(v, "row", scatter_dimension=0, tiled=True).astype(f32)

    grads = [scatter(g, f) for g, f in zip((dA, dBT, dC, dDT), (False, True, False, True))]
    squares = sum(jnp.sum(g * g) for g in grads)
    dhw, dsm, loss, squares = lax.psum((dhw, dsm, loss, squares), ("row", "col"))
    grads += [dhw, dsm]
    norm = jnp.sqrt(squares + jnp.sum(dhw * dhw) + jnp.sum(dsm * dsm))
    factor = 0.0001 / jnp.maximum(norm, 0.0001)
    done = [adamw(w, m, v, g * factor) for w, m, v, g in zip(weights, firsts, seconds, grads)]
    return tuple(d[0] for d in done) + tuple(d[1] for d in done) + tuple(d[2] for d in done) + (loss, norm)


def solution(mesh):
    both = P(("row", "col"))
    big = [P("row", "col")] * 4 + [P()] * 2
    return jax.shard_map(
        local,
        mesh=mesh,
        in_specs=(both, both, both, *big, *big, *big),
        out_specs=(*big, *big, *big, P(), P()),
        check_vma=False,
    )
```

time: 1700 us -> 1220 us (0.72)
  Pallas kernels: 0 us -> 488 us
  other arithmetic: 408 us -> 34.4 us
  matrix products: 317 us -> 0 us
  local copies, waits for them, and re-layouts: 283 us -> 44.7 us
  waiting for transfers between devices: 581 us -> 551 us
    pallas_call x0 -> x3, Pallas kernels: none -> 488 us  [the longest x1 341 us: decoder(): pl.pallas_call(functools.partial(dec_kernel, scale, nb), grid=(n // nb,),...]
    dot_general x86 -> x0, matrix products: 309 us -> none  [the longest x42 153 us: mat_plain(): return wrapped(left, right)]
    convert_element_type x50 -> x5, other arithmetic: 160 us -> 7.96 us  [the longest x1 5.97 us: scatter(): v = v.astype(bf)]
    reduce_sum x64 -> x6, other arithmetic: 130 us -> 10.4 us  [the longest x4 6.45 us: local(): squares = sum((jnp.sum(g * g) for g in grads))]
    unnamed x20 -> x15, waiting for transfers between devices: 206 us -> 120 us
    unnamed x772 -> x54, local copies, waits for them, and re-layouts: 84.6 us -> 18.4 us
    dot_general x4 -> x0, local copies, waits for them, and re-layouts: 65.8 us -> none  [the longest x2 46.6 us: score_value(): jnp.einsum('nqhd,nkhd->nhqk', half(query), half(keyed), preferred_element...]
    gather x16 -> x0, local copies, waits for them, and re-layouts: 54.6 us -> none  [the longest x6 32.8 us: group_loss(): jnp.take_along_axis(decoded[:, 1:], jnp.minimum(restore, KEEP - 1)[:, :,...]
  transfers between devices with their start and end apart: 18 -> 14, of which waited for: 10 -> 11; matrix products, arithmetic and copies ran while one was open for 40% -> 5% of each run, Pallas kernels for 0% -> 12%
where the time goes in v1:
time: 1220 us; the launch traced here: 1210 us
  waiting for transfers between devices  551 us (45%)
  Pallas kernels  488 us (40%)
  blocking collectives  71.6 us (6%)
  local copies, waits for them, and re-layouts  44.7 us (4%)
  other arithmetic  34.4 us (3%)
  between operations  20.5 us (2%)
    pallas_call x1, Pallas kernels, decoder(): pl.pallas_call(functools.partial(dec_kernel, scale, nb), grid=(n // nb,),...  341 us
    psum x1, waiting for transfers between devices, local(): lax.psum((dhw, dsm, loss, squares), ('row', 'col'))  135 us
    unnamed x15, waiting for transfers between devices  120 us
    all_gather x4, waiting for transfers between devices, gather(): v = lax.all_gather(v, 'col', axis=1, tiled=True)  118 us
    reduce_scatter x4, waiting for transfers between devices, scatter(): lax.psum_scatter(v, 'row', scatter_dimension=0, tiled=True).astype(f32)  108 us
    pallas_call x1, Pallas kernels, encoder_bwd(): pl.pallas_call(enc_bwd_kernel, in_specs=vspec(5 + len(saved)), out_specs=...  84.3 us
    pallas_call x1, Pallas kernels, encoder_fwd(): pl.pallas_call(enc_fwd_kernel, in_specs=vspec(6), out_specs=vspec(len(out...  62.6 us
    psum x1, blocking collectives, local(): lax.psum((dhw, dsm, loss, squares), ('row', 'col'))  39.6 us
  transfers between devices with their start and end apart: 14, of which 11 were waited for; matrix products, arithmetic and copies ran while one was open for 5% of the time, Pallas kernels for 12%

profile of v1, /device:TPU:0, one launch (start us, length us, event | category | flops | bytes accessed | tf_op | source)
XLA Modules:
  0.0 1211.5 jit_solution(7947447774114796182)
XLA Ops:
  7.2 1.9 convert_element_type.32
  9.3 34.9 %all-gather.6.cloned.1.call-done = bf16[768,928]{1,0:T(8,128)(2,1)} async-done(((bf16[192,928]{1,0:T(8,128)(2,1)}), bf16[768,928]{1,0:T(8,128)(2,1)}) %all-gather.6.cloned.1.call-update) | async-done | bytes 1425424 | tf_op jit(solution)/shard_map/all_gather | solution.py:618
  44.1 2.6 copy.53
  46.8 11.9 all_gather.26
  58.9 9.7 all_gather.30
  68.7 10.4 all_gather.28
  83.3 4.3 pad.4.pix
  87.6 66.3 %all-gather.8.cloned.1.call-done = bf16[768,7424]{0,1:T(8,128)(2,1)} async-done(((bf16[768,928]{0,1:T(8,128)(2,1)}), bf16[768,7424]{0,1:T(8,128)(2,1)}) %all-gather.8.cloned.1.call-update) | async-done | bytes 11403280 | tf_op jit(solution)/shard_map/all_gather | solution.py:619
  153.9 15.3 %copy.55.win = bf16[768,7424]{1,0:T(8,128)(2,1)} copy(bf16[768,7424]{0,1:T(8,128)(2,1)} %all-gather.8.cloned.1.call-done) | data formatting | bytes 22806528 | tf_op jit(solution)/shard_map/all_gather | solution.py:619
  169.2 36.4 %all-gather.10.cloned.1.call-done = bf16[3072,768]{0,1:T(8,128)(2,1)} async-done(((bf16[3072,96]{0,1:T(8,128)(2,1)}), bf16[3072,768]{0,1:T(8,128)(2,1)}) %all-gather.10.cloned.1.call-update) | async-done | bytes 4718608 | tf_op jit(solution)/shard_map/all_gather | solution.py:619
  205.6 62.6 %encoder_fwd.1 = (f32[672,512]{1,0:T(8,128)}, bf16[672,768]{1,0:T(8,128)(2,1)}, f32[672,768]{1,0:T(8,128)}, f32[672,768]{1,0:T(8,128)}, f32[672,768]{1,0:T(8,128...) custom-call(bf16[12,208,768]{2,1,0:T(8,128)(2,1)} %pad.4.pix, ...), custom_call_target="tpu_custom_call" | custom-call | tf_op jit(solution)/shard_map/encoder_fwd/pallas_call | solution.py:443
  268.2 14.9 %all-gather.12.cloned.1.call-done.win = bf16[512,4096]{1,0:T(8,128)(2,1)} async-done(((bf16[512,512]{1,0:T(8,128)(2,1)}), bf16[512,4096]{1,0:T(8,128)(2,1)}) %all-gather.12.cloned.1.call-update) | async-done | bytes 4194320 | tf_op jit(solution)/shard_map/all_gather | solution.py:619
  283.2 341.4 %decoder.1 = (f32[12,56,512]{2,1,0:T(8,128)}, f32[512,4096]{1,0:T(8,128)}, f32[512,2048]{1,0:T(8,128)}, f32[512,768]{1,0:T(8,128)}, f32[1,21248]{1,0:T(1,128)}, /*index=5*/f32[1,128]{1,0:T(1,128)}) custom-call(f32[12,56,512]{2,1,0:T(8,128)} %bitcast.22, s32[12,208,1]{2,1,0:T(8,128)} %copy.56.codec, s32[12,1,208]{2,1,0:T(1,128)} %reshape.65.coder, ...), custom_call_target="tpu_custom_call" | custom-call | tf_op jit(solution)/shard_map/decoder/pallas_call | solution.py:338
  624.5 3.8 convert_bitcast_fusion
  628.5 6.0 convert_element_type.38
  634.5 84.3 %encoder_bwd.1 = (bf16[768,7424]{1,0:T(8,128)(2,1)}, bf16[768,3072]{1,0:T(8,128)(2,1)}, f32[1,21248]{1,0:T(1,128)}) custom-call(f32[672,512]{1,0:T(8,128)} %bitcast.21, s32[672,1]{1,0:T(8,128)} %reshape.70.keepc, f32[1,21248]{1,0:T(1,128)} %reshape.62.sv, bf16[768,7424]{1,0:T(8,128)(2,1)} %copy.55.win, bf16[768,3072]{1,0:T(8,128)(2,1)} %bitcast.17, ...), custom_call_target="tpu_custom_call" | custom-call | tf_op jit(solution)/shard_map/encoder_bwd/pallas_call | solution.py:555
  718.9 14.9 %copy.59 = bf16[768,7424]{0,1:T(8,128)(2,1)} copy(bf16[768,7424]{1,0:T(8,128)(2,1)} %get-tuple-element.62) | data formatting | bytes 22806528
  737.0 36.0 %reduce-scatter.13.cloned.1.call-done = bf16[3072,96]{0,1:T(8,128)(2,1)} async-done(((bf16[3072,768]{0,1:T(8,128)(2,1)}), bf16[3072,96]{0,1:T(8,128)(2,1)}) %reduce-scatter.13.cloned.1.call-update) | async-done | bytes 589840 | tf_op jit(solution)/shard_map/reduce_scatter | solution.py:628
  773.1 118.7 %reduce-scatter.25.cloned.1.call-done = bf16[928,768]{1,0:T(8,128)(2,1)} async-done(((bf16[7424,768]{1,0:T(8,128)(2,1)}), bf16[928,768]{1,0:T(8,128)(2,1)}) %reduce-scatter.25.cloned.1.call-update) | async-done | bytes 1425424
  891.8 2.5 copy.60
  894.4 135.0 %all-reduce.5.cloned.1.call-done = (f32[512,768]{1,0:T(8,128)}, f32[21248]{0:T(1024)}) async-done(((f32[512,768]{1,0:T(8,128)}, f32[21248]{0:T(1024)}), (f32[512,768]{1,0:T(8,128)}, f32[21248]{0:T(1024)})) %all-reduce.5.cloned.1.call-update) | async-done | bytes 1657872 | tf_op jit(solution)/shard_map/psum | solution.py:633
  1030.9 2.4 multiply_reduce_fusion
  1033.3 22.1 %reduce-scatter.23.cloned.1.call-done = bf16[512,64]{0,1:T(8,128)(2,1)} async-done(((bf16[2048,64]{0,1:T(8,128)(2,1)}), bf16[512,64]{0,1:T(8,128)(2,1)}) %reduce-scatter.23.cloned.1.call-update) | async-done | bytes 65552 | tf_op jit(solution)/shard_map/reduce_scatter | solution.py:629
  1056.9 26.3 %reduce-scatter.19.cloned.1.call-done = bf16[128,512]{1,0:T(8,128)(2,1)} async-done(((bf16[512,512]{1,0:T(8,128)(2,1)}), bf16[128,512]{1,0:T(8,128)(2,1)}) %reduce-scatter.19.cloned.1.call-update) | async-done | bytes 131088 | tf_op jit(solution)/shard_map/reduce_scatter | solution.py:629
  1084.7 26.4 %reduce-scatter.15.cloned.1.call-done = bf16[768,96]{0,1:T(8,128)(2,1)} async-done(((bf16[3072,96]{0,1:T(8,128)(2,1)}), bf16[768,96]{0,1:T(8,128)(2,1)}) %reduce-scatter.15.cloned.1.call-update) | async-done | bytes 147472 | tf_op jit(solution)/shard_map/reduce_scatter | solution.py:629
  1111.1 1.6 fusion.8
  1112.7 33.1 %reduce-scatter.11.cloned.1.call-done = bf16[192,928]{1,0:T(8,128)(2,1)} async-done(((bf16[768,928]{1,0:T(8,128)(2,1)}), bf16[192,928]{1,0:T(8,128)(2,1)}) %reduce-scatter.11.cloned.1.call-update) | async-done | bytes 356368 | tf_op jit(solution)/shard_map/reduce_scatter | solution.py:629
  1145.7 1.8 fusion.3
  1150.1 39.6 %all-reduce.1 = (f32[]{:T(128)}, f32[]{:T(128)}) all-reduce(f32[]{:T(128)S(6)} %add.136, f32[]{:T(128)S(1)} %bitcast.23), channel_id=1, replica_groups=mesh['row'=4,'col'=8] {'row','col'}, use_global_device_ids=true, to_apply=%region_12.13 | all-reduce | flops 2 | bytes 16 | tf_op jit(solution)/shard_map/psum | solution.py:633
  1191.8 1.7 multiply_subtract_fusion.5
  1193.6 5.0 multiply_subtract_fusion
  1201.5 1.8 multiply_subtract_fusion.1
  (107 shorter events, 15.4 us)
Async XLA Ops:
  7.2 37.0 %all-gather.6.cloned.1.call-start = ((), (), s32[]{:S(2)}) async-start(), calls=%async_computation.8 | async-start | bytes 1966080 | tf_op jit(solution)/shard_map/all_gather | solution.py:618
  9.2 37.6 %copy-start.4 = (f32[768,96]{0,1:T(8,128)S(1)}, f32[768,96]{0,1:T(8,128)}, u32[]{:S(2)}) copy-start(f32[768,96]{0,1:T(8,128)} %param.27) | copy-start | bytes 884740
  9.2 144.7 %all-gather.8.cloned.1.call-start = ((), (), s32[]{:S(2)}) async-start(), calls=%async_computation.9 | async-start | bytes 12828672 | tf_op jit(solution)/shard_map/all_gather | solution.py:619
  46.7 12.1 %copy-start.11 = (f32[512,64]{0,1:T(8,128)S(1)}, f32[512,64]{0,1:T(8,128)}, u32[]{:S(2)}) copy-start(f32[512,64]{0,1:T(8,128)} %param.29) | copy-start | bytes 393220
  46.7 21.9 %copy-start.5 = (f32[128,512]{1,0:T(8,128)S(1)}, f32[128,512]{1,0:T(8,128)}, u32[]{:S(2)}) copy-start(f32[128,512]{1,0:T(8,128)} %param.28) | copy-start | bytes 786436
  46.8 158.8 %all-gather.10.cloned.1.call-start = ((), (), s32[]{:S(2)}) async-start(), calls=%async_computation.10 | async-start | bytes 5308416 | tf_op jit(solution)/shard_map/all_gather | solution.py:619
  58.7 20.8 %copy-start.23 = (s32[12,196]{1,0:T(8,128)S(1)}, s32[12,196]{1,0:T(8,128)}, u32[]{:S(2)}) copy-start(s32[12,196]{1,0:T(8,128)} %param.25) | copy-start | bytes 28228
  58.7 21.4 %copy-start.13 = (f32[21248]{0:T(1024)S(1)}, f32[21248]{0:T(1024)}, u32[]{:S(2)}) copy-start(f32[21248]{0:T(1024)} %param.31) | copy-start | bytes 254980
  58.7 22.1 %copy-start.24 = (s32[12,49]{1,0:T(8,128)S(1)}, s32[12,49]{1,0:T(8,128)}, u32[]{:S(2)}) copy-start(s32[12,49]{1,0:T(8,128)} %param.24) | copy-start | bytes 7060
  58.8 209.5 %all-gather.14.cloned.1.call-start = ((), (), s32[]{:S(2)}) async-start(), calls=%async_computation.12 | async-start | bytes 2359296 | tf_op jit(solution)/shard_map/all_gather | solution.py:619
  68.6 214.6 %all-gather.12.cloned.1.call-start = ((), (), s32[]{:S(2)}) async-start(), calls=%async_computation.11 | async-start | bytes 4718592 | tf_op jit(solution)/shard_map/all_gather | solution.py:619
  79.1 656.6 %reduce-scatter.21.cloned.1.call-start = ((), (), s32[]{:S(2)}) async-start(), calls=%async_computation.18 | async-start | bytes 2359296 | tf_op jit(solution)/shard_map/reduce_scatter | solution.py:628
  628.4 108.1 %reduce-scatter.17.cloned.1.call-start = ((), (), s32[]{:S(2)}) async-start(), calls=%async_computation.16 | async-start | bytes 4718592 | tf_op jit(solution)/shard_map/reduce_scatter | solution.py:628
  634.4 138.5 %reduce-scatter.13.cloned.1.call-start = ((), (), s32[]{:S(2)}) async-start(), calls=%async_computation.14 | async-start | bytes 5308416 | tf_op jit(solution)/shard_map/reduce_scatter | solution.py:628
  718.9 172.9 %reduce-scatter.25.cloned.1.call-start = ((), (), s32[]{:S(2)}) async-start(), calls=%async_computation.20 | async-start | bytes 12828672
  733.9 295.5 %all-reduce.5.cloned.1.call-start = ((), (), s32[]{:S(2)}) async-start(), calls=%async_computation.21 | async-start | bytes 3317760 | tf_op jit(solution)/shard_map/psum | solution.py:633
  735.7 319.7 %reduce-scatter.23.cloned.1.call-start = ((), (), s32[]{:S(2)}) async-start(), calls=%async_computation.19 | async-start | bytes 327680 | tf_op jit(solution)/shard_map/reduce_scatter | solution.py:629
  736.4 346.7 %reduce-scatter.19.cloned.1.call-start = ((), (), s32[]{:S(2)}) async-start(), calls=%async_computation.17 | async-start | bytes 655360 | tf_op jit(solution)/shard_map/reduce_scatter | solution.py:629
  737.0 374.1 %reduce-scatter.15.cloned.1.call-start = ((), (), s32[]{:S(2)}) async-start(), calls=%async_computation.15 | async-start | bytes 737280 | tf_op jit(solution)/shard_map/reduce_scatter | solution.py:629
  773.0 372.7 %reduce-scatter.11.cloned.1.call-start = ((), (), s32[]{:S(2)}) async-start(), calls=%async_computation.13 | async-start | bytes 1966080 | tf_op jit(solution)/shard_map/reduce_scatter | solution.py:629
  894.3 299.1 %copy-start.2 = (f32[512,768]{1,0:T(8,128)S(1)}, f32[512,768]{1,0:T(8,128)}, u32[]{:S(2)}) copy-start(f32[512,768]{1,0:T(8,128)} %param.36) | copy-start | bytes 4718596
  894.4 255.8 %copy-start.25 = (f32[1,128]{1,0:T(1,128)S(1)}, f32[1,128]{1,0:T(1,128)}, u32[]{:S(2)}) copy-start(f32[1,128]{1,0:T(1,128)} %get-tuple-element.69) | copy-start | bytes 1540
  894.4 299.1 %copy-start = (f32[512,768]{1,0:T(8,128)S(1)}, f32[512,768]{1,0:T(8,128)}, u32[]{:S(2)}) copy-start(f32[512,768]{1,0:T(8,128)} %hw.1) | copy-start | bytes 4718596
  1193.5 5.0 copy-start.12
  1193.5 5.0 copy-start.18
  1193.5 5.0 copy-start.19
  1193.5 5.0 copy-start.20
  1193.5 5.9 copy-start.6
  1193.5 5.9 copy-start.10
  1193.5 5.8 copy-start.16
  1193.5 5.8 copy-start.17
  1199.4 2.1 copy-start.1
  (8 other events, 13.9 us)
Sparse Core Ops, SparseCore 0:
  10.4 33.6 all-gather.5
  46.9 106.9 all-gather.7
  155.5 50.0 all-gather.9
  207.0 27.7 all-gather.13
  236.3 46.7 all-gather.11
  628.5 34.5 reduce-scatter.20
  665.4 48.7 reduce-scatter.16
  719.0 53.9 reduce-scatter.12
  775.3 116.4 reduce-scatter.24
  898.5 130.8 all-reduce.4
  1032.1 23.2 reduce-scatter.22
  1058.3 24.7 reduce-scatter.18
  1086.0 25.0 reduce-scatter.14
  1114.8 30.9 reduce-scatter.10

commit v2 on v1

--- a/solution.py
+++ b/solution.py
@@ -154,8 +154,8 @@
 
 
 def dec_kernel(scale, nb, y, codec, coder, pix, pos, sv, win, wout, hw,
-               dy, dwin, dwout, dhw, dsm, loss,
-               x, t, xh1, xh2, xhf, rs1, rs2, rsf, tm, tr, a1, a2, u, o, qkv, p, hid, gp, dpr, d16, lacc):
+               dy, win_out, wout_out, dhw, dsm, loss,
+               dwin, dwout, x, t, xh1, xh2, xhf, rs1, rs2, rsf, tm, tr, a1, a2, u, o, qkv, p, hid, gp, dpr, d16, lacc):
     M = nb * DS
     R = 32
     W = DD
@@ -326,6 +326,8 @@
     @pl.when(pl.program_id(0) == pl.num_programs(0) - 1)
     def _():
         loss[...] = jnp.broadcast_to(jnp.sum(lacc[...], axis=1, keepdims=True) * (scale / PIX), (1, 128))
+        for src, dst in ((dwin, win_out), (dwout, wout_out)):
+            rows(DD, 16, lambda r: dst.__setitem__((r, slice(None)), src[r, :].astype(bf)))
 
 
 def decoder(y, codec, coder, pix, pos, sv, win, wout, hw, scale, nb=2):
@@ -341,10 +343,11 @@
         in_specs=[blk((ES, DD)), blk((DS, 1)), blk((1, DS)), blk((DS, PIX)), whole(pos), whole(sv), whole(win), whole(wout), whole(hw)],
         out_specs=[blk((ES, DD)), fixed(win.shape), fixed(wout.shape), fixed(hw.shape), fixed((1, SMALL)), fixed((1, 128))],
         out_shape=[
-            jax.ShapeDtypeStruct((n, ES, DD), f32), jax.ShapeDtypeStruct(win.shape, f32),
-            jax.ShapeDtypeStruct(wout.shape, f32), jax.ShapeDtypeStruct(hw.shape, f32),
+            jax.ShapeDtypeStruct((n, ES, DD), f32), jax.ShapeDtypeStruct(win.shape, bf),
+            jax.ShapeDtypeStruct(wout.shape, bf), jax.ShapeDtypeStruct(hw.shape, f32),
             jax.ShapeDtypeStruct((1, SMALL), f32), jax.ShapeDtypeStruct((1, 128), f32)],
         scratch_shapes=[
+            V(win.shape, f32), V(wout.shape, f32),
             V((M, DD), f32), V((M, DD), f32), V((M, DD), f32), V((M, DD), f32), V((M, DD), f32),
             V((M, 1), f32), V((M, 1), f32), V((M, 1), f32), V((M, 1), f32), V((M, 1), f32),
             V((M, DD), bf), V((M, DD), bf), V((M, DD), bf), V((M, DD), bf), V((M, 3 * DD), bf),
@@ -355,12 +358,396 @@
     )(y, codec, coder, pix, pos, sv, win, wout, hw)
 
 
+class Place:
+    def __init__(self, nrow, ncol):
+        side = math.isqrt(nrow)
+        self.nrow, self.ncol = nrow, ncol
+        self.n = {"x": side, "y": nrow // side, "z": ncol // 2}
+        row, col = lax.axis_index("row"), lax.axis_index("col")
+        self.at = {"x": row % side, "y": row // side, "z": col // 2, "core": col % 2}
+
+    def moved(self, **by):
+        at = {}
+        for k, v in self.at.items():
+            step = by.get(k, 0)
+            size = 2 if k == "core" else self.n[k]
+            at[k] = v if step == 0 else lax.rem(v + (step % size), size)
+        return at["y"] * self.n["x"] + at["x"], at["z"] * 2 + at["core"]
+
+    def greet(self):
+        sem = pltpu.get_barrier_semaphore()
+        count = 0
+        for axis in ("x", "y", "z", "core"):
+            size = 2 if axis == "core" else self.n[axis]
+            for step in sorted({1 % size, (size - 1) % size} - {0}):
+                pl.semaphore_signal(sem, inc=1, device_id=self.moved(**{axis: step}), device_id_type=pl.DeviceIdType.MESH)
+                count += 1
+        pl.semaphore_wait(sem, count)
+
+
+class Shapes:
+    def __init__(self, nrow, ncol):
+        self.nrow, self.ncol = nrow, ncol
+        self.awide, self.bwide = (5 * D + FF + DD) // ncol, FF // nrow
+        self.alanes, self.blanes = self.window(self.awide, ncol), self.window(self.bwide, nrow)
+        self.arows, self.brows = D // nrow, D // ncol
+        self.crows, self.clanes = DD // nrow, 4 * DD // ncol + DFF // ncol
+        self.drows, self.dlanes = DD // ncol, DFF // nrow
+        self.erows = -(-(DD * PIX + SMALL) // (nrow * ncol * 256 * 8)) * 8
+        self.blocks = {"A": (self.arows, self.alanes), "B": (self.brows, self.blanes), "C": (self.crows, self.clanes), "D": (self.drows, self.dlanes)}
+
+    @staticmethod
+    def window(wide, count):
+        return max(-(-((wide * c) % 128 + wide) // 128) * 128 for c in range(count))
+
+    def start(self, which, index):
+        wide, lanes, total = (self.awide, self.alanes, 5 * D + FF + DD) if which == "A" else (self.bwide, self.blanes, FF)
+        first = (wide * index) // 128
+        last = (total - lanes) // 128
+        if isinstance(index, int):
+            return min(first, last) * 128
+        return jnp.minimum(first, last) * 128
+
+
+STREAMS = (("A",), ("B", "C", "D"))
+ORDER = (("x", "y"), ("y", "x"))
+
+
+def gather_kernel(nrow, ncol, ain, bin_, cin, din, aout, bout, cout, dout, send, recv, csend, crecv, lsem):
+    place = Place(nrow, ncol)
+    sh = Shapes(nrow, ncol)
+    ins = {"A": ain, "B": bin_, "C": cin, "D": din}
+    mats = "ABCD"
+
+    def spot(m, row, col):
+        if m == "A":
+            return aout.at[col, pl.ds(pl.multiple_of(row * sh.arows, 16), sh.arows), :]
+        if m == "B":
+            return bout.at[row, pl.ds(pl.multiple_of(col * sh.brows, 16), sh.brows), :]
+        if m == "C":
+            return cout.at[pl.ds(pl.multiple_of(row * sh.crows, 16), sh.crows), pl.ds(pl.multiple_of(col * sh.clanes, 128), sh.clanes)]
+        return dout.at[pl.ds(pl.multiple_of(col * sh.drows, 16), sh.drows), pl.ds(pl.multiple_of(row * sh.dlanes, 128), sh.dlanes)]
+
+    nz = place.n["z"]
+    place.greet()
+    me = place.moved()
+    locals_ = [pltpu.make_async_copy(ins[m], spot(m, *me), lsem.at[i]) for i, m in enumerate(mats)]
+    for c in locals_:
+        c.start()
+    steps = []
+    for s in (0, 1):
+        p, q = ORDER[s]
+        for i in range(place.n[q]):
+            for j in range(place.n[p]):
+                for k in range(nz):
+                    steps.append((i + j + k, k, s, i, j, k))
+    steps.sort()
+    sent = []
+    late = []
+    for _, _, s, i, j, k in steps:
+        p, q = ORDER[s]
+        npp, nq = place.n[p], place.n[q]
+        slot = (i * npp + j) * nz + k
+        own = i == j == k == 0
+        for m in STREAMS[s]:
+            mi = mats.index(m)
+            dst = spot(m, *place.moved(**{q: -i, p: -j, "z": -k}))
+            src = ins[m] if own else dst
+            if not own:
+                pltpu.make_async_remote_copy(dst, dst, send.at[mi, slot], recv.at[mi, slot], device_id=place.moved(core=1), device_id_type=pl.DeviceIdType.MESH).wait_recv()
+            plan = []
+            if i == j == 0 and k < nz - 1:
+                plan.append(({"z": 1}, slot + 1))
+            if i == 0 and j < npp - 1:
+                plan.append(({p: 1}, slot + nz))
+            if i < nq - 1:
+                plan.append(({q: 1}, slot + nz * npp))
+            for by, there in plan:
+                c = pltpu.make_async_remote_copy(src, dst, send.at[mi, there], recv.at[mi, there], device_id=place.moved(**by), device_id_type=pl.DeviceIdType.MESH)
+                c.start()
+                sent.append(c)
+            c = pltpu.make_async_remote_copy(src, dst, csend.at[mi, slot], crecv.at[mi, slot], device_id=place.moved(core=1), device_id_type=pl.DeviceIdType.MESH)
+            c.start()
+            sent.append(c)
+            other = spot(m, *place.moved(**{q: -i, p: -j, "z": -k, "core": 1}))
+            late.append(pltpu.make_async_remote_copy(other, other, csend.at[mi, slot], crecv.at[mi, slot], device_id=place.moved(core=1), device_id_type=pl.DeviceIdType.MESH))
+    for c in late:
+        c.wait_recv()
+    for c in sent:
+        c.wait_send()
+    for c in locals_:
+        c.wait()
+
+
+def gather_weights(nrow, ncol, ain, bin_, cin, din):
+    sh = Shapes(nrow, ncol)
+    half = nrow * ncol // 2
+    S = jax.ShapeDtypeStruct
+    anyspec = pl.BlockSpec(memory_space=pl.ANY)
+    sem = pltpu.SemaphoreType.DMA
+    return pl.pallas_call(
+        functools.partial(gather_kernel, nrow, ncol),
+        in_specs=[anyspec] * 4, out_specs=[anyspec] * 4,
+        out_shape=[S((ncol, D, sh.alanes), bf), S((nrow, D, sh.blanes), bf), S((DD, 4 * DD + DFF), bf), S((DD, DFF), bf)],
+        scratch_shapes=[sem((4, half)), sem((4, half)), sem((4, half)), sem((4, half)), sem((4,))],
+        compiler_params=pltpu.CompilerParams(collective_id=0, has_side_effects=True),
+        name="gather_weights",
+    )(ain, bin_, cin, din)
+
+
+RSTREAMS = (("A",), ("B", "C", "D", "E"))
+
+
+def reduce_kernel(nrow, ncol, da, db, dc, dd, de, loss,
+                  ga, gb, gc, gd, eall, *scratch):
+    mats = "ABCDE"
+    acc, sib, rq, rp, rz = (dict(zip(mats, scratch[5 * t : 5 * t + 5])) for t in range(5))
+    ge, lsem, csend, crecv, send, qrecv, prec, zrecv, esend, erecv, ecs, ecr = scratch[25:]
+    place = Place(nrow, ncol)
+    sh = Shapes(nrow, ncol)
+    nz = place.n["z"]
+    ins = {"A": da, "B": db, "C": dc, "D": dd, "E": de}
+    outs = {"A": ga, "B": gb, "C": gc, "D": gd}
+
+    def spot(m, row, col):
+        if m == "A":
+            return da.at[pl.ds(pl.multiple_of(row * sh.arows, 16), sh.arows), pl.ds(pl.multiple_of(sh.start("A", col), 128), sh.alanes)]
+        if m == "B":
+            return db.at[pl.ds(pl.multiple_of(col * sh.brows, 16), sh.brows), pl.ds(pl.multiple_of(sh.start("B", row), 128), sh.blanes)]
+        if m == "C":
+            return dc.at[pl.ds(pl.multiple_of(row * sh.crows, 16), sh.crows), pl.ds(pl.multiple_of(col * sh.clanes, 128), sh.clanes)]
+        if m == "D":
+            return dd.at[pl.ds(pl.multiple_of(col * sh.drows, 16), sh.drows), pl.ds(pl.multiple_of(row * sh.dlanes, 128), sh.dlanes)]
+        return de.at[row * ncol + col]
+
+    place.greet()
+
+    def remote(src, dst, ssem, rsem, **by):
+        return pltpu.make_async_remote_copy(src, dst, ssem, rsem, device_id=place.moved(**by), device_id_type=pl.DeviceIdType.MESH)
+
+    steps = []
+    for s in (0, 1):
+        p, q = ORDER[s]
+        for i in range(place.n[q]):
+            for j in range(place.n[p]):
+                for k in range(nz):
+                    steps.append(((place.n[q] - 1 - i) + (place.n[p] - 1 - j) + (nz - 1 - k), s, i, j, k))
+    steps.sort()
+    sent = []
+    loads = {}
+    for _, s, i, j, k in steps:
+        p, q = ORDER[s]
+        slot = (i * place.n[p] + j) * nz + k
+        for m in RSTREAMS[s]:
+            mi = mats.index(m)
+            c = remote(spot(m, *place.moved(**{q: -i, p: -j, "z": -k, "core": 1})), sib[m].at[slot], csend.at[mi, slot], crecv.at[mi, slot], core=1)
+            c.start()
+            sent.append(c)
+            loads[m, slot] = pltpu.make_async_copy(spot(m, *place.moved(**{q: -i, p: -j, "z": -k})), acc[m].at[slot], lsem.at[mi, slot])
+            loads[m, slot].start()
+    for _, s, i, j, k in steps:
+        p, q = ORDER[s]
+        npp, nq = place.n[p], place.n[q]
+        slot = (i * npp + j) * nz + k
+        for m in RSTREAMS[s]:
+            mi = mats.index(m)
+            loads[m, slot].wait()
+            remote(sib[m].at[slot], sib[m].at[slot], csend.at[mi, slot], crecv.at[mi, slot], core=1).wait_recv()
+            terms = [(acc[m], slot), (sib[m], slot)]
+            if i < nq - 1:
+                remote(rq[m].at[slot], rq[m].at[slot], send.at[mi, slot], qrecv.at[mi, slot], core=1).wait_recv()
+                terms.append((rq[m], slot))
+            if i == 0 and j < npp - 1:
+                remote(rp[m].at[slot], rp[m].at[slot], send.at[mi, slot], prec.at[mi, slot], core=1).wait_recv()
+                terms.append((rp[m], slot))
+            if i == j == 0 and k < nz - 1:
+                remote(rz[m].at[slot], rz[m].at[slot], send.at[mi, slot], zrecv.at[mi, slot], core=1).wait_recv()
+                terms.append((rz[m], slot))
+            last = i == j == k == 0
+            total = acc[m].shape[1]
+            size = 8 if m == "E" else 16
+
+            def add(r, m=m, terms=terms, last=last, slot=slot):
+                v = terms[0][0][slot, r, :].astype(f32)
+                for ref, at in terms[1:]:
+                    v = v + ref[at, r, :].astype(f32)
+                if not last:
+                    acc[m][slot, r, :] = v.astype(acc[m].dtype)
+                elif m == "E":
+                    ge[pl.ds(0, total), :] = v
+                else:
+                    outs[m][r, :] = v
+            if m == "E":
+                add(slice(None))
+            else:
+                rows(total, size, add)
+            if last:
+                continue
+            if i > 0:
+                c = remote(acc[m].at[slot], rq[m].at[slot - npp * nz], send.at[mi, slot], qrecv.at[mi, slot - npp * nz], **{q: -1})
+            elif j > 0:
+                c = remote(acc[m].at[slot], rp[m].at[slot - nz], send.at[mi, slot], prec.at[mi, slot - nz], **{p: -1})
+            else:
+                c = remote(acc[m].at[slot], rz[m].at[slot - 1], send.at[mi, slot], zrecv.at[mi, slot - 1], z=-1)
+            c.start()
+            sent.append(c)
+
+
+    row, col = place.moved()
+    la = lax.broadcasted_iota(jnp.int32, (1, sh.alanes), 1) + (sh.start("A", col) - col * sh.awide)
+    lb = lax.broadcasted_iota(jnp.int32, (1, sh.blanes), 1) + (sh.start("B", row) - row * sh.bwide)
+    va = jnp.where((la >= 0) & (la < sh.awide), ga[...], 0.0)
+    vb = jnp.where((lb >= 0) & (lb < sh.bwide), gb[...], 0.0)
+    er = sh.erows
+    sq = jnp.zeros((1, 128), f32)
+    for v in (va, vb, gc[...], gd[...], ge[0:er, :]):
+        w = rsum(v * v)
+        for c0 in range(0, w.shape[1], 128):
+            sq = sq + w[:, c0 : c0 + 128]
+    ge[er : er + 8, :] = jnp.concatenate([jnp.broadcast_to(sq, (8, 128)), jnp.broadcast_to(loss[...], (8, 128))], axis=1)
+
+    def espot(**by):
+        r, c = place.moved(**by)
+        return eall.at[r * ncol + c]
+
+    eall[row * ncol + col] = ge[...]
+    npp, nq = place.n["x"], place.n["y"]
+    esteps = sorted((i + j + k, k, i, j) for i in range(nq) for j in range(npp) for k in range(nz))
+    late = []
+    for _, k, i, j in esteps:
+        slot = (i * npp + j) * nz + k
+        own = i == j == k == 0
+        dst = espot(y=-i, x=-j, z=-k)
+        src = ge if own else dst
+        if not own:
+            remote(dst, dst, esend.at[slot], erecv.at[slot], core=1).wait_recv()
+        plan = []
+        if i == j == 0 and k < nz - 1:
+            plan.append(({"z": 1}, slot + 1))
+        if i == 0 and j < npp - 1:
+            plan.append(({"x": 1}, slot + nz))
+        if i < nq - 1:
+            plan.append(({"y": 1}, slot + nz * npp))
+        for by, there in plan:
+            c = remote(src, dst, esend.at[there], erecv.at[there], **by)
+            c.start()
+            sent.append(c)
+        c = remote(src, dst, ecs.at[slot], ecr.at[slot], core=1)
+        c.start()
+        sent.append(c)
+        other = espot(y=-i, x=-j, z=-k, core=1)
+        late.append(remote(other, other, ecs.at[slot], ecr.at[slot], core=1))
+    for c in late:
+        c.wait_recv()
+    for c in sent:
+        c.wait_send()
+
+
+def reduce_grads(nrow, ncol, da, db, dc, dd, de, loss):
+    sh = Shapes(nrow, ncol)
+    half = nrow * ncol // 2
+    side = math.isqrt(nrow)
+    n = {"x": side, "y": nrow // side, "z": ncol // 2}
+    S = jax.ShapeDtypeStruct
+    V = pltpu.VMEM
+    anyspec = pl.BlockSpec(memory_space=pl.ANY)
+    vm = pl.BlockSpec(memory_space=pltpu.VMEM)
+    sem = pltpu.SemaphoreType.DMA
+    kinds = [sh.blocks[m] + (bf,) for m in "ABCD"] + [(sh.erows, 256, f32)]
+    order = [ORDER[s] for s in (0, 1, 1, 1, 1)]
+    nz = n["z"]
+    scratch = []
+    for count in (
+        lambda p, q: half, lambda p, q: half, lambda p, q: (n[q] - 1) * n[p] * nz,
+        lambda p, q: (n[p] - 1) * nz, lambda p, q: nz - 1,
+    ):
+        scratch += [V((count(p, q), r, l), t) for (r, l, t), (p, q) in zip(kinds, order)]
+    scratch += [V((sh.erows + 8, 256), f32)]
+    big = n["x"] * n["y"] * nz - min(n["x"], n["y"]) * nz
+    scratch += [sem((5, half))] * 4 + [sem((5, big)), sem((5, max(n["x"], n["y"]) * nz)), sem((5, nz))] + [sem((half,))] * 4
+    return pl.pallas_call(
+        functools.partial(reduce_kernel, nrow, ncol),
+        in_specs=[anyspec] * 5 + [vm], out_specs=[vm] * 5,
+        out_shape=[S(sh.blocks[m], f32) for m in "ABCD"] + [S((nrow * ncol, sh.erows + 8, 256), f32)],
+        scratch_shapes=scratch,
+        compiler_params=pltpu.CompilerParams(collective_id=1, has_side_effects=True, vmem_limit_bytes=60 << 20),
+        name="reduce_grads",
+    )(da, db, dc, dd, de, loss)
+
+
+def windows(nrow, ncol, weights):
+    sh = Shapes(nrow, ncol)
+    row, col = lax.axis_index("row"), lax.axis_index("col")
+
+    def put(v, which, index, wide, lanes):
+        if wide == lanes:
+            return v
+        shift = index * wide - sh.start(which, index)
+        return lax.dynamic_update_slice(jnp.zeros((v.shape[0], lanes), v.dtype), v, (0, shift))
+    a, b, c, d = (w.astype(bf) for w in weights)
+    return put(a, "A", col, sh.awide, sh.alanes), put(b.T, "B", row, sh.bwide, sh.blanes), c, d.T
+
+
+def unwindow(nrow, ncol, ga, gb, gc, gd):
+    sh = Shapes(nrow, ncol)
+    row, col = lax.axis_index("row"), lax.axis_index("col")
+
+    def take(v, which, index, wide, lanes):
+        if wide == lanes:
+            return v
+        return lax.dynamic_slice(v, (0, index * wide - sh.start(which, index)), (v.shape[0], wide))
+    return take(ga, "A", col, sh.awide, sh.alanes), take(gb, "B", row, sh.bwide, sh.blanes).T, gc, gd.T
+
+
+def tile_plan(sh, which):
+    wide, count = (sh.awide, sh.ncol) if which == "A" else (sh.bwide, sh.nrow)
+    alone, shared = [], []
+    for c in range(count):
+        first, end = wide * c // 128, -(-(wide * (c + 1)) // 128)
+        base = sh.start(which, c) // 128
+        lo = first + 1 if (wide * c) % 128 else first
+        hi = end - 1 if (wide * (c + 1)) % 128 else end
+        alone.append((c, lo, hi, base))
+        if hi < end:
+            shared.append((c, hi, base, sh.start(which, c + 1) // 128))
+    return alone, shared
+
+
+def joiner(sh, which, src, dst, tmp, sem, base=0):
+    alone, shared = tile_plan(sh, which)
+    copies = []
+    for c, lo, hi, at in alone:
+        copies.append((src.at[c, :, pl.ds((lo - at) * 128, (hi - lo) * 128)], dst.at[:, pl.ds(lo * 128, (hi - lo) * 128)]))
+    for u, (c, t, at, nxt) in enumerate(shared):
+        copies.append((src.at[c, :, pl.ds((t - at) * 128, 128)], dst.at[:, pl.ds(t * 128, 128)]))
+        copies.append((src.at[c + 1, :, pl.ds((t - nxt) * 128, 128)], tmp.at[u]))
+    made = [pltpu.make_async_copy(a, b, sem.at[base + i]) for i, (a, b) in enumerate(copies)]
+    for m in made:
+        m.start()
+
+    def end():
+        for m in made:
+            m.wait()
+        for u, (c, t, at, nxt) in enumerate(shared):
+            dst[:, t * 128 : (t + 1) * 128] += tmp[u]
+    return end
+
+
+def joiner_scratch(sh):
+    V = pltpu.VMEM
+    counts = [(len(a), len(s)) for a, s in (tile_plan(sh, "A"), tile_plan(sh, "B"))]
+    return [V((D, 5 * D + FF + DD), bf), V((D, FF), bf)] + [V((max(s, 1), D, 128), bf) for _, s in counts] + [
+        pltpu.SemaphoreType.DMA((a + 2 * s,)) for a, s in counts]
+
+
 EG = 4 * ES
 O_Q, O_P, O_F, O_E = D, 4 * D, 5 * D, 5 * D + FF
 
 
-def enc_fwd_kernel(pix, keepc, pos3, sv, win, wout,
-                   y, kept, xh1, xh2, xhf, rs1, rs2, rsf, a1, a2, e16, o, qkv, p, hid, gp, x, bias):
+def enc_fwd_kernel(sh, pix, keepc, pos3, sv, awin, bwin,
+                   y, kept, xh1, xh2, xhf, rs1, rs2, rsf, a1, a2, e16, o, qkv, p, hid, gp, x, bias, win, wout, atmp, btmp, asem, bsem):
+    enda = joiner(sh, "A", awin, win, atmp, asem)
+    endb = joiner(sh, "B", bwin, wout, btmp, bsem)
     n = pix.shape[0]
     M = n * ES
     R = 32
@@ -372,6 +759,7 @@
             pick = (kc == lax.broadcasted_iota(jnp.int32, (ES, DS), 1)).astype(f32).astype(bf)
             two.append(nn(pick, pix[b]))
         kept[i * ES : (i + 2) * ES, :] = jnp.concatenate(two, axis=0).astype(bf)
+    enda()
     for lo in range(0, M, EG):
         sl = slice(lo, lo + EG)
         kc = keepc[sl, :]
@@ -417,6 +805,7 @@
         hid[:, pl.ds(c, 256)] = g.astype(bf)
         gp[:, pl.ds(c, 256)] = dg_.astype(bf)
     cols(FF, 256, fc1)
+    endb()
     x[...] += nt(hid[...], wout[...]) + part(sv, 7)
 
     def lnf(r):
@@ -432,7 +821,7 @@
     return [pl.BlockSpec(memory_space=pltpu.VMEM)] * k
 
 
-def encoder_fwd(pix, keepc, pos3, sv, win, wout):
+def encoder_fwd(sh, pix, keepc, pos3, sv, awin, bwin):
     n = pix.shape[0]
     M = n * ES
     S = jax.ShapeDtypeStruct
@@ -441,16 +830,18 @@
             S((M, 1), f32), S((M, 1), f32), S((M, 1), f32), S((M, D), bf), S((M, D), bf), S((M, D), bf), S((M, D), bf),
             S((M, 3 * D), bf), S((n // 4 * HEADS, EG, EG), bf), S((M, FF), bf), S((M, FF), bf)]
     return pl.pallas_call(
-        enc_fwd_kernel,
-        in_specs=vspec(6), out_specs=vspec(len(outs)), out_shape=outs,
-        scratch_shapes=[V((M, D), f32), V((EG, EG), f32)],
+        functools.partial(enc_fwd_kernel, sh),
+        in_specs=vspec(4) + [pl.BlockSpec(memory_space=pl.ANY)] * 2, out_specs=vspec(len(outs)), out_shape=outs,
+        scratch_shapes=[V((M, D), f32), V((EG, EG), f32)] + joiner_scratch(sh),
         compiler_params=pltpu.CompilerParams(vmem_limit_bytes=60 << 20),
         name="encoder_fwd",
-    )(pix, keepc, pos3, sv, win, wout)
-
-
-def enc_bwd_kernel(dy, keepc, sv, win, wout, kept, xh1, xh2, xhf, rs1, rs2, rsf, a1, a2, e16, o, qkv, p, hid, gp,
-                   dwin, dwout, dsm, x, t, d16, dqkv, stage, sem):
+    )(pix, keepc, pos3, sv, awin, bwin)
+
+
+def enc_bwd_kernel(sh, dy, keepc, sv, awin, bwin, kept, xh1, xh2, xhf, rs1, rs2, rsf, a1, a2, e16, o, qkv, p, hid, gp,
+                   dwin, dwout, dsm, x, t, d16, dqkv, stage, sem, win, wout, atmp, btmp, asem, bsem):
+    enda = joiner(sh, "A", awin, win, atmp, asem)
+    endb = joiner(sh, "B", bwin, wout, btmp, bsem)
     M = dy.shape[0]
     R = 32
     W = D
@@ -484,6 +875,8 @@
         d16[r, 0:DD] = v.astype(bf)
     rows(M, R, emb)
     put(dwin, DD // CW, O_E, lambda c: dg(e16[...], d16[:, pl.ds(c, CW)], 0, 0))
+    enda()
+    endb()
     t[...] = nt(d16[:, 0:DD], win[:, O_E:])
 
     def lnfb(r):
@@ -547,21 +940,21 @@
     put(dwin, D // CW, 0, lambda c: dg(kept[...], d16[:, pl.ds(c, CW)], 0, 0))
 
 
-def encoder_bwd(dy, keepc, sv, win, wout, saved):
+def encoder_bwd(sh, dy, keepc, sv, awin, bwin, saved):
     M = dy.shape[0]
     S = jax.ShapeDtypeStruct
     V = pltpu.VMEM
     anyspec = pl.BlockSpec(memory_space=pl.ANY)
     return pl.pallas_call(
-        enc_bwd_kernel,
-        in_specs=vspec(5 + len(saved)),
+        functools.partial(enc_bwd_kernel, sh),
+        in_specs=vspec(3) + [pl.BlockSpec(memory_space=pl.ANY)] * 2 + vspec(len(saved)),
         out_specs=[anyspec, anyspec, pl.BlockSpec(memory_space=pltpu.VMEM)],
-        out_shape=[S(win.shape, bf), S(wout.shape, bf), S((1, SMALL), f32)],
+        out_shape=[S((D, 5 * D + FF + DD), bf), S((D, FF), bf), S((1, SMALL), f32)],
         scratch_shapes=[V((M, D), f32), V((M, D), f32), V((M, D), bf), V((M, 3 * D), bf), V((2, D, 256), bf),
-                        pltpu.SemaphoreType.DMA((2,))],
+                        pltpu.SemaphoreType.DMA((2,))] + joiner_scratch(sh),
         compiler_params=pltpu.CompilerParams(vmem_limit_bytes=62 << 20),
         name="encoder_bwd",
-    )(dy, keepc, sv, win, wout, *saved)
+    )(dy, keepc, sv, awin, bwin, *saved)
 
 
 def sincos_np(width):
@@ -585,20 +978,6 @@
     return dec, np.concatenate([hi, mid, lo], axis=0)
 
 
-def step(pixels, keep, restore, A, BT, C, DT, hw, small, denom):
-    n = pixels.shape[0]
-    dec_pos, enc_pos = tables()
-    pix = jnp.pad(pixels, ((0, 0), (0, DS - PATCHES), (0, 0)))
-    keepc = jnp.concatenate([keep, jnp.full((n, 1), NOROW - 1, jnp.int32), jnp.full((n, ES - KEEP - 1), NOROW, jnp.int32)], axis=1).reshape(n * ES, 1)
-    code = jnp.concatenate([jnp.where(restore < KEEP, restore, 64), jnp.full((n, 1), KEEP, jnp.int32), jnp.full((n, DS - PATCHES - 1), NOROW, jnp.int32)], axis=1)
-    sv = small.reshape(1, SMALL)
-    fw = encoder_fwd(pix, keepc, jnp.asarray(enc_pos), sv, A, BT)
-    y, saved = fw[0], fw[1:]
-    dy, dC, dDT, dhw, dsm_d, loss = decoder(y.reshape(n, ES, DD), code.reshape(n, DS, 1), code.reshape(n, 1, DS), pix, jnp.asarray(dec_pos), sv, C, DT, hw, 1.0 / denom)
-    dA, dBT, dsm_e = encoder_bwd(dy.reshape(n * ES, DD), keepc, sv, A, BT, saved)
-    return dA, dBT, dC, dDT, dhw, (dsm_d + dsm_e).reshape(SMALL), loss[0, 0]
-
-
 def adamw(weight, first, second, grad):
     first = 0.9 * first + (1.0 - 0.9) * grad
     second = 0.999 * second + (1.0 - 0.999) * grad * grad
@@ -610,29 +989,32 @@
 
 def local(pixels, keep_idx, restore, *state):
     weights, firsts, seconds = state[0:6], state[6:12], state[12:18]
-    devices = lax.axis_size("row") * lax.axis_size("col")
-    denom = 1.0 * pixels.shape[0] * devices * (PATCHES - KEEP)
-
-    def gather(v, flip):
-        v = v.astype(bf)
-        v = lax.all_gather(v, "row", axis=0, tiled=True)
-        v = lax.all_gather(v, "col", axis=1, tiled=True)
-        return v.T if flip else v
-
-    A, BT, C, DT = (gather(w, f) for w, f in zip(weights[0:4], (False, True, False, True)))
-    dA, dBT, dC, dDT, dhw, dsm, loss = step(pixels, keep_idx, restore, A, BT, C, DT, weights[4], weights[5], denom)
-
-    def scatter(v, flip):
-        v = v.astype(bf)
-        v = v.T if flip else v
-        v = lax.psum_scatter(v, "col", scatter_dimension=1, tiled=True)
-        return lax.psum_scatter(v, "row", scatter_dimension=0, tiled=True).astype(f32)
-
-    grads = [scatter(g, f) for g, f in zip((dA, dBT, dC, dDT), (False, True, False, True))]
-    squares = sum(jnp.sum(g * g) for g in grads)
-    dhw, dsm, loss, squares = lax.psum((dhw, dsm, loss, squares), ("row", "col"))
-    grads += [dhw, dsm]
-    norm = jnp.sqrt(squares + jnp.sum(dhw * dhw) + jnp.sum(dsm * dsm))
+    nrow, ncol = lax.axis_size("row"), lax.axis_size("col")
+    sh = Shapes(nrow, ncol)
+    n = pixels.shape[0]
+    denom = 1.0 * n * nrow * ncol * (PATCHES - KEEP)
+
+    dec_pos, enc_pos = tables()
+    pix = jnp.pad(pixels, ((0, 0), (0, DS - PATCHES), (0, 0)))
+    fill = lambda count, value: jnp.full((n, count), value, jnp.int32)
+    keepc = jnp.concatenate([keep_idx, fill(1, NOROW - 1), fill(ES - KEEP - 1, NOROW)], axis=1).reshape(n * ES, 1)
+    code = jnp.concatenate([jnp.where(restore < KEEP, restore, 64), fill(1, KEEP), fill(DS - PATCHES - 1, NOROW)], axis=1)
+    head, sv = weights[4], weights[5].reshape(1, SMALL)
+
+    aw, bw, c, dt = gather_weights(nrow, ncol, *windows(nrow, ncol, weights[0:4]))
+    y, *saved = encoder_fwd(sh, pix, keepc, jnp.asarray(enc_pos), sv, aw, bw)
+    dy, dc, ddt, dhead, dsm_d, loss = decoder(
+        y.reshape(n, ES, DD), code.reshape(n, DS, 1), code.reshape(n, 1, DS), pix, jnp.asarray(dec_pos), sv, c, dt, head, 1.0 / denom)
+    da, dbt, dsm_e = encoder_bwd(sh, dy.reshape(n * ES, DD), keepc, sv, aw, bw, saved)
+
+    count = nrow * ncol * sh.erows * 256
+    flat = jnp.concatenate([dhead.reshape(-1), (dsm_d + dsm_e).reshape(-1), jnp.zeros((count - DD * PIX - SMALL,), f32)])
+    ga, gb, gc, gd, ge = reduce_grads(nrow, ncol, da, dbt, dc, ddt, flat.reshape(nrow * ncol, sh.erows, 256), loss)
+    flat = ge[:, : sh.erows].reshape(-1)
+    grads = [*unwindow(nrow, ncol, ga, gb, gc, gd), flat[: DD * PIX].reshape(DD, PIX), flat[DD * PIX : DD * PIX + SMALL]]
+    aux = jnp.sum(ge[:, sh.erows], axis=0)
+    norm = jnp.sqrt(jnp.sum(aux[:128]))
+    loss = aux[128]
     factor = 0.0001 / jnp.maximum(norm, 0.0001)
     done = [adamw(w, m, v, g * factor) for w, m, v, g in zip(weights, firsts, seconds, grads)]
     return tuple(d[0] for d in done) + tuple(d[1] for d in done) + tuple(d[2] for d in done) + (loss, norm)

time: 1220 us -> 782 us (0.64)
  waiting for transfers between devices: 551 us -> 0 us
  Pallas kernels: 488 us -> 734 us
  blocking collectives: 71.6 us -> 0 us
  local copies, waits for them, and re-layouts: 44.7 us -> 17.5 us
  between operations: 20.5 us -> 3.37 us
  other arithmetic: 34.4 us -> 18.9 us
    pallas_call x2 -> x4, Pallas kernels: 147 us -> 394 us  [the longest x1 137 us: reduce_grads(): pl.pallas_call(functools.partial(reduce_kernel, nrow, ncol), in_specs=[an...]
    all_gather x5 -> x0, waiting for transfers between devices: 153 us -> none  [the longest x4 118 us: gather(): v = lax.all_gather(v, 'col', axis=1, tiled=True)]
    reduce_scatter x7 -> x0, waiting for transfers between devices: 144 us -> none  [the longest x4 108 us: scatter(): lax.psum_scatter(v, 'row', scatter_dimension=0, tiled=True).astype(f32)]
    psum x1 -> x0, waiting for transfers between devices: 135 us -> none  [local(): lax.psum((dhw, dsm, loss, squares), ('row', 'col'))]
    unnamed x15 -> x0, waiting for transfers between devices: 120 us -> none
    psum x1 -> x0, blocking collectives: 39.6 us -> none  [local(): lax.psum((dhw, dsm, loss, squares), ('row', 'col'))]
    all_gather x3 -> x0, blocking collectives: 32 us -> none  [gather(): v = lax.all_gather(v, 'row', axis=0, tiled=True)]
    all_gather x2 -> x0, local copies, waits for them, and re-layouts: 17.8 us -> none  [the longest x1 15.3 us: gather(): v = lax.all_gather(v, 'col', axis=1, tiled=True)]
  transfers between devices with their start and end apart: 14 -> 0, of which waited for: 11 -> 0; matrix products, arithmetic and copies ran while one was open for 5% -> 0% of each run, Pallas kernels for 12% -> 0%
where the time goes in v2:
time: 782 us; the launch traced here: 774 us
  Pallas kernels  734 us (94%)
  other arithmetic  18.9 us (2%)
  local copies, waits for them, and re-layouts  17.5 us (2%)
    pallas_call x1, Pallas kernels, decoder(): pl.pallas_call(functools.partial(dec_kernel, scale, nb), grid=(n // nb,),...  340 us
    pallas_call x1, Pallas kernels, reduce_grads(): pl.pallas_call(functools.partial(reduce_kernel, nrow, ncol), in_specs=[an...  137 us
    pallas_call x1, Pallas kernels, gather_weights(): pl.pallas_call(functools.partial(gather_kernel, nrow, ncol), in_specs=[an...  110 us
    pallas_call x1, Pallas kernels, encoder_bwd(): pl.pallas_call(functools.partial(enc_bwd_kernel, sh), in_specs=vspec(3) +...  83.6 us
    pallas_call x1, Pallas kernels, encoder_fwd(): pl.pallas_call(functools.partial(enc_fwd_kernel, sh), in_specs=vspec(4) +...  63.4 us

profile of v2, /device:TPU:0, one launch (start us, length us, event | category | flops | bytes accessed | tf_op | source)
XLA Modules:
  0.0 773.8 jit_solution(16198846656426229785)
XLA Ops:
  0.7 1.2 convert_element_type.14
  2.0 2.3 dynamic_update_slice.3.ain
  4.3 0.7 convert_bitcast_fusion.bin_
  5.1 0.7 convert_element_type.16.cin
  5.7 0.6 convert_bitcast_fusion.1.din
  6.4 109.7 %gather_weights.1 = (bf16[8,768,1024]{2,1,0:T(8,128)(2,1)}, bf16[4,768,768]{2,1,0:T(8,128)(2,1)}, bf16[512,4096]{1,0:T(8,128)(2,1)}, bf16[512,2048]{1,0:T(8,128)(2,1)}) custom-call(bf16[192,1024]{1,0:T(8,128)(2,1)} %copy-done.3, bf16[96,768]{1,0:T(8,128)(2,1)} %convert_bitcast_fusion.bin_, bf16[128,512]{1,0:T(8,128)(2,1)} %convert_element_type.16.cin, ...), custom_call_target="tpu_custom_call" | custom-call | tf_op jit(solution)/shard_map/gather_weights/pallas_call | solution.py:488
  116.1 0.7 reshape.74.sv
  116.8 4.1 pad.4.pix
  121.1 0.9 reshape.83.keepc
  122.0 63.4 %encoder_fwd.1 = (f32[672,512]{1,0:T(8,128)}, bf16[672,768]{1,0:T(8,128)(2,1)}, f32[672,768]{1,0:T(8,128)}, f32[672,768]{1,0:T(8,128)}, f32[672,768]{1,0:T(8,128...) custom-call(bf16[12,208,768]{2,1,0:T(8,128)(2,1)} %pad.4.pix, ...), custom_call_target="tpu_custom_call" | custom-call | tf_op jit(solution)/shard_map/encoder_fwd/pallas_call | solution.py:832
  185.6 1.5 copy.45.codec
  187.1 0.6 reshape.77.coder
  187.7 340.2 %decoder.1 = (f32[12,56,512]{2,1,0:T(8,128)}, bf16[512,4096]{1,0:T(8,128)(2,1)}, bf16[512,2048]{1,0:T(8,128)(2,1)}, f32[512,768]{1,0:T(8,128)}, f32[1,21248]{1,0:T(1,128)}, /*index=5*/f32[1,128]{1,0:T(1,128)}) custom-call(f32[12,56,512]{2,1,0:T(8,128)} %bitcast.31, s32[12,208,1]{2,1,0:T(8,128)} %copy.45.codec, s32[12,1,208]{2,1,0:T(1,128)} %reshape.77.coder, ...), custom_call_target="tpu_custom_call" | custom-call | tf_op jit(solution)/shard_map/decoder/pallas_call | solution.py:340
  528.0 83.6 %encoder_bwd.1 = (bf16[768,7424]{1,0:T(8,128)(2,1)}, bf16[768,3072]{1,0:T(8,128)(2,1)}, f32[1,21248]{1,0:T(1,128)}) custom-call(f32[672,512]{1,0:T(8,128)} %bitcast.30, s32[672,1]{1,0:T(8,128)} %reshape.83.keepc, f32[1,21248]{1,0:T(1,128)} %reshape.74.sv, bf16[8,768,1024]{2,1,0:T(8,128)(2,1)} %get-tuple-element.54.awin, ...), custom_call_target="tpu_custom_call" | custom-call | tf_op jit(solution)/shard_map/encoder_bwd/pallas_call | solution.py:948
  611.6 1.8 add_reduce_fusion
  613.5 1.0 pad_maximum_fusion
  614.5 1.7 reshape.81.de
  616.3 137.1 %reduce_grads.1 = (f32[192,1024]{1,0:T(8,128)}, f32[96,768]{1,0:T(8,128)}, f32[128,512]{1,0:T(8,128)}, f32[64,512]{1,0:T(8,128)}, f32[32,64,256]{2,1,0:T(8,128)}) custom-call(bf16[768,7424]{1,0:T(8,128)(2,1)} %get-tuple-element.75.da, bf16[768,3072]{1,0:T(8,128)(2,1)} %get-tuple-element.76.db, bf16[512,4096]{1,0:T(8,128)(2,1)} %get-tuple-element.77.dc, ...), custom_call_target="tpu_custom_call" | custom-call | tf_op jit(solution)/shard_map/reduce_grads/pallas_call | solution.py:668
  753.4 1.6 slice.20
  755.1 0.9 copy.47
  756.1 1.0 slice_reduce_fusion
  757.1 0.6 slice_reduce_fusion.1
  758.4 0.7 multiply_subtract_fusion.5
  759.3 1.4 mul.357
  760.7 0.3 copy-done
  761.1 5.4 multiply_subtract_fusion
  766.5 0.8 multiply_subtract_fusion.4
  767.4 1.0 multiply_subtract_fusion.3
  768.4 1.1 multiply_subtract_fusion.2
  769.5 0.2 copy-done.10
  769.6 2.1 multiply_subtract_fusion.1
  771.7 0.5 slice.23
  (68 shorter events, 0.7 us)
Async XLA Ops:
  0.7 3.7 copy-start.4
  0.7 4.4 copy-start.6
  0.7 5.0 copy-start.11
  2.0 114.1 %copy-start.12 = (f32[21248]{0:T(1024)S(1)}, f32[21248]{0:T(1024)}, u32[]{:S(2)}) copy-start(f32[21248]{0:T(1024)} %param.31) | copy-start | bytes 254980
  4.3 2.1 copy-start.3
  116.8 4.3 copy-start.27
  122.0 63.4 %copy-start.26 = (s32[12,196]{1,0:T(8,128)S(1)}, s32[12,196]{1,0:T(8,128)}, u32[]{:S(2)}) copy-start(s32[12,196]{1,0:T(8,128)} %param.25) | copy-start | bytes 28228
  528.0 83.7 %copy-start.25 = (f32[1,21248]{1,0:T(1,128)S(1)}, f32[1,21248]{1,0:T(1,128)}, u32[]{:S(2)}) copy-start(f32[1,21248]{1,0:T(1,128)} %get-tuple-element.80) | copy-start | bytes 254980
  528.0 85.4 %copy-start.2 = (f32[512,768]{1,0:T(8,128)S(1)}, f32[512,768]{1,0:T(8,128)}, u32[]{:S(2)}) copy-start(f32[512,768]{1,0:T(8,128)} %get-tuple-element.79) | copy-start | bytes 4718596
  755.1 3.3 copy-start.13
  755.1 3.3 copy-start.23
  755.1 3.3 copy-start.24
  759.3 1.8 copy-start
  761.0 5.4 copy-start.20
  761.0 5.4 copy-start.21
  761.0 5.5 copy-start.22
  761.0 6.3 copy-start.7
  761.0 6.3 copy-start.17
  761.1 6.3 copy-start.18
  761.1 6.2 copy-start.19
  766.5 1.9 copy-start.5
  766.5 1.9 copy-start.14
  766.5 1.9 copy-start.15
  766.5 1.9 copy-start.16
  767.3 2.1 copy-start.1
  767.3 2.1 copy-start.8
  767.3 2.1 copy-start.9
  767.4 2.3 copy-start.10

commit v3 on v2

--- a/solution.py
+++ b/solution.py
@@ -60,10 +60,12 @@
         fn(pl.ds(pl.multiple_of(i * size, size), size))
 
 
-def cols(total, size, fn):
-    @pl.loop(0, total // size)
-    def _(i):
-        fn(pl.multiple_of(i * size, size))
+def rows_sum(total, size, widths, fn):
+    def body(i, carry):
+        parts = fn(pl.ds(pl.multiple_of(i * size, size), size))
+        return tuple(c + jnp.sum(v.reshape(size // 8, 8, v.shape[1]), axis=0) for c, v in zip(carry, parts))
+    carry = lax.fori_loop(0, total // size, body, tuple(jnp.zeros((8, w), f32) for w in widths))
+    return [rsum(c) for c in carry]
 
 
 def pieces(x):
@@ -110,54 +112,62 @@
     return jnp.where((lane >= h * hd) & (lane < (h + 1) * hd), x, jnp.zeros_like(x))
 
 
+def stack(x, hd):
+    return jnp.concatenate([lanes_of(x, h, hd) for h in range(128 // hd)], axis=0)
+
+
+def unstack(x, hd):
+    n = x.shape[0] * hd // 128
+    out = None
+    for h in range(128 // hd):
+        t = lanes_of(x[h * n : (h + 1) * n], h, hd)
+        out = t if out is None else out + t
+    return out
+
+
 def att_fwd(qkv, o, p, bias, rsl, width, g, slot, hd):
-    c0 = pl.multiple_of(g * 128, 128)
-    q = qkv[rsl, pl.ds(c0, 128)]
-    k = qkv[rsl, pl.ds(pl.multiple_of(c0 + width, 128), 128)]
-    v = qkv[rsl, pl.ds(pl.multiple_of(c0 + 2 * width, 128), 128)]
-    acc = None
+    c0 = g * 128
+    q = qkv[rsl, c0 : c0 + 128]
+    k = qkv[rsl, c0 + width : c0 + width + 128]
+    v = qkv[rsl, c0 + 2 * width : c0 + 2 * width + 128]
+    n = q.shape[0]
+    every = nt(stack(k, hd), q)
+    probs = []
     for h in range(128 // hd):
-        s = nt(lanes_of(k, h, hd), q) * (hd ** -0.5) + bias
-        e = jnp.exp(s - jnp.max(s, axis=0, keepdims=True))
+        s = every[h * n : (h + 1) * n] * (hd ** -0.5 * 1.4426950408889634) + bias
+        e = jnp.exp2(s - jnp.max(s, axis=0, keepdims=True))
         pr = (e * (1.0 / jnp.sum(e, axis=0, keepdims=True))).astype(bf)
         p[slot + h] = pr
-        t = dg(pr, lanes_of(v, h, hd), 0, 0)
-        acc = t if acc is None else acc + t
-    o[rsl, pl.ds(c0, 128)] = acc.astype(bf)
+        probs.append(pr)
+    o[rsl, c0 : c0 + 128] = dg(jnp.concatenate(probs, axis=0), stack(v, hd), 0, 0).astype(bf)
 
 
 def att_bwd(qkv, do, p, dqkv, rsl, width, g, slot, hd):
-    c0 = pl.multiple_of(g * 128, 128)
-    c1 = pl.multiple_of(c0 + width, 128)
-    c2 = pl.multiple_of(c0 + 2 * width, 128)
-    q = qkv[rsl, pl.ds(c0, 128)]
-    k = qkv[rsl, pl.ds(c1, 128)]
-    v = qkv[rsl, pl.ds(c2, 128)]
-    d = do[rsl, pl.ds(c0, 128)]
-    aq = ak = av = None
+    c0 = g * 128
+    c1, c2 = c0 + width, c0 + 2 * width
+    q = qkv[rsl, c0 : c0 + 128]
+    k = qkv[rsl, c1 : c1 + 128]
+    v = qkv[rsl, c2 : c2 + 128]
+    d = do[rsl, c0 : c0 + 128]
+    n = q.shape[0]
+    probs = jnp.concatenate([p[slot + h] for h in range(128 // hd)], axis=0)
+    every = nt(stack(v, hd), d)
+    back = []
     for h in range(128 // hd):
-        pr = p[slot + h]
-        dp = nt(lanes_of(v, h, hd), d).astype(bf).astype(f32)
-        pf = pr.astype(f32)
-        t = pf * dp
-        ds = ((t - pf * jnp.sum(t, axis=0, keepdims=True)) * (hd ** -0.5)).astype(bf)
-        tv = nn(pr, lanes_of(d, h, hd))
-        tk = nn(ds, lanes_of(q, h, hd))
-        tq = dg(ds, lanes_of(k, h, hd), 0, 0)
-        if h == 0:
-            aq, ak, av = tq, tk, tv
-        else:
-            aq, ak, av = aq + tq, ak + tk, av + tv
-    dqkv[rsl, pl.ds(c0, 128)] = aq.astype(bf)
-    dqkv[rsl, pl.ds(c1, 128)] = ak.astype(bf)
-    dqkv[rsl, pl.ds(c2, 128)] = av.astype(bf)
+        pf = probs[h * n : (h + 1) * n].astype(f32)
+        t = pf * every[h * n : (h + 1) * n].astype(bf).astype(f32)
+        back.append(((t - pf * jnp.sum(t, axis=0, keepdims=True)) * (hd ** -0.5)).astype(bf))
+    back = jnp.concatenate(back, axis=0)
+    dqkv[rsl, c0 : c0 + 128] = dg(back, stack(k, hd), 0, 0).astype(bf)
+    dqkv[rsl, c1 : c1 + 128] = unstack(nn(back, q), hd).astype(bf)
+    dqkv[rsl, c2 : c2 + 128] = unstack(nn(probs, d), hd).astype(bf)
 
 
 def dec_kernel(scale, nb, y, codec, coder, pix, pos, sv, win, wout, hw,
                dy, win_out, wout_out, dhw, dsm, loss,
                dwin, dwout, x, t, xh1, xh2, xhf, rs1, rs2, rsf, tm, tr, a1, a2, u, o, qkv, p, hid, gp, dpr, d16, lacc):
     M = nb * DS
-    R = 32
+    R = M
     W = DD
 
     @pl.when(pl.program_id(0) == 0)
@@ -168,10 +178,9 @@
         for ref in (dwin, dwout, dhw):
             rows(ref.shape[0], 16, lambda r: ref.__setitem__((r, slice(None)), jnp.zeros((16, ref.shape[1]), f32)))
 
-    def gsum(i, v, lo=0, n=None):
-        a = OFF[i] + lo
-        n = LENS[i] if n is None else n
-        dsm[:, pl.ds(a, n)] += rsum(v)
+    def put(where, sums):
+        for (i, lo), v in zip(where, sums):
+            dsm[:, OFF[i] + lo : OFF[i] + lo + v.shape[1]] += v
 
     for b in range(nb):
         pick = (codec[b] == lax.broadcasted_iota(jnp.int32, (DS, SEL), 1)).astype(f32).astype(bf)
@@ -195,10 +204,11 @@
 
     bias = jnp.where(lax.broadcasted_iota(jnp.int32, (DS, 1), 0) <= PATCHES, 0.0, -1e30).astype(f32)
 
-    @pl.loop(0, nb * 4)
+    @pl.loop(0, nb)
     def _(i):
-        rsl = pl.ds(pl.multiple_of((i // 4) * DS, 16), DS)
-        att_fwd(qkv, o, p, bias, rsl, W, i % 4, i * 4, 32)
+        rsl = pl.ds(pl.multiple_of(i * DS, 16), DS)
+        for g in range(4):
+            att_fwd(qkv, o, p, bias, rsl, W, g, i * 16 + g * 4, 32)
 
     x[...] += nn(o[...], win[:, 3 * W : 4 * W]) + part(sv, 17)
 
@@ -209,12 +219,12 @@
         a2[r, :] = a.astype(bf)
     rows(M, R, ln2)
 
-    def fc1(c):
-        h = nn(a2[...], win[:, pl.ds(pl.multiple_of(4 * W + c, 256), 256)])
-        g, dg_ = gelu_pair(h + sv[:, pl.ds(pl.multiple_of(OFF[20] + c, 128), 256)])
-        hid[:, pl.ds(c, 256)] = g.astype(bf)
-        gp[:, pl.ds(c, 256)] = dg_.astype(bf)
-    cols(DFF, 256, fc1)
+    CW = 512
+    for c in range(0, DFF, CW):
+        h = nn(a2[...], win[:, 4 * W + c : 4 * W + c + CW])
+        g, dg_ = gelu_pair(h + sv[:, OFF[20] + c : OFF[20] + c + CW])
+        hid[:, c : c + CW] = g.astype(bf)
+        gp[:, c : c + CW] = dg_.astype(bf)
 
     x[...] += nt(hid[...], wout[...]) + part(sv, 21)
 
@@ -226,93 +236,72 @@
     rows(M, R, lnf)
 
     for b in range(nb):
-        def tstat(r):
-            v = pix[b, r, :].astype(f32)
-            m = jnp.mean(v, axis=1, keepdims=True)
-            c = v - m
-            q = pl.ds(pl.multiple_of(b * DS + r.start, 16), 16)
-            tm[q, :] = m
-            tr[q, :] = lax.rsqrt(jnp.mean(c * c, axis=1, keepdims=True) + 1e-06)
-        rows(DS, 16, tstat)
-
-    def headc(c):
-        hwc = hw[:, pl.ds(c, 256)].astype(bf)
-        pr = nn(u[...], hwc) + sv[:, pl.ds(pl.multiple_of(OFF[24] + c, 128), 256)]
+        v = pix[b].astype(f32)
+        m = jnp.mean(v, axis=1, keepdims=True)
+        c = v - m
+        tm[b * DS : (b + 1) * DS, :] = m
+        tr[b * DS : (b + 1) * DS, :] = lax.rsqrt(jnp.mean(c * c, axis=1, keepdims=True) + 1e-06)
+
+    for c in range(0, PIX, 256):
+        pr = nn(u[...], hw[:, c : c + 256].astype(bf)) + sv[:, OFF[24] + c : OFF[24] + c + 256]
         for b in range(nb):
             sl = slice(b * DS, (b + 1) * DS)
-            tgt = (pix[b, :, pl.ds(c, 256)].astype(f32) - tm[sl, :]) * tr[sl, :]
+            tgt = (pix[b, :, c : c + 256].astype(f32) - tm[sl, :]) * tr[sl, :]
             diff = jnp.where(codec[b] == 64, pr[sl] - tgt, 0.0)
-            lacc[:, 0:256] += rsum(diff * diff)
+            lacc[...] += rsum(diff * diff)
             dp = diff * (2.0 * scale / PIX)
-            dsm[:, pl.ds(pl.multiple_of(OFF[24] + c, 128), 256)] += rsum(dp)
-            dpr[sl, pl.ds(c, 256)] = dp.astype(bf)
-    cols(PIX, 256, headc)
-
-    def hgrad(c):
-        dhw[:, pl.ds(c, 256)] += dg(u[...], dpr[:, pl.ds(c, 256)], 0, 0)
-    cols(PIX, 256, hgrad)
+            dsm[:, OFF[24] + c : OFF[24] + c + 256] += rsum(dp)
+            dpr[sl, c : c + 256] = dp.astype(bf)
+
+    dhw[...] += dg(u[...], dpr[...], 0, 0)
     t[...] = nt(dpr[...], hw[...].astype(bf))
 
     def lnfb(r):
         da = t[r, :]
         xh = xhf[r, :]
-        gsum(22, da * xh)
-        gsum(23, da)
         dx = norm_back(da, xh, rsf[r, :], part(sv, 22))
-        gsum(21, dx)
         x[r, :] = dx
         d16[r, :] = dx.astype(bf)
-    rows(M, R, lnfb)
-
-    def fc1b(c):
-        cs = pl.ds(c, 256)
-        dwout[:, cs] += dg(d16[...], hid[:, cs], 0, 0)
-        dh = nn(d16[...], wout[:, cs]) * gp[:, cs].astype(f32)
-        dsm[:, pl.ds(pl.multiple_of(OFF[20] + c, 128), 256)] += rsum(dh)
-        dh16 = dh.astype(bf)
-        gp[:, cs] = dh16
-        wc = pl.ds(pl.multiple_of(4 * W + c, 256), 256)
-        dwin[:, wc] += dg(a2[...], dh16, 0, 0)
-    cols(DFF, 256, fc1b)
+        return da * xh, da, dx
+    put([(22, 0), (23, 0), (21, 0)], rows_sum(M, R, [W] * 3, lnfb))
+
+    dwout[...] += dg(d16[...], hid[...], 0, 0)
+    for c in range(0, DFF, CW):
+        dh = nn(d16[...], wout[:, c : c + CW]) * gp[:, c : c + CW].astype(f32)
+        dsm[:, OFF[20] + c : OFF[20] + c + CW] += rsum(dh)
+        gp[:, c : c + CW] = dh.astype(bf)
+    dwin[:, 4 * W :] += dg(a2[...], gp[...], 0, 0)
     t[...] = nt(gp[...], win[:, 4 * W :])
 
     def ln2b(r):
         da = t[r, :]
         xh = xh2[r, :]
-        gsum(18, da * xh)
-        gsum(19, da)
         dx = x[r, :] + norm_back(da, xh, rs2[r, :], part(sv, 18))
-        gsum(17, dx)
         x[r, :] = dx
         d16[r, :] = dx.astype(bf)
-    rows(M, R, ln2b)
+        return da * xh, da, dx
+    put([(18, 0), (19, 0), (17, 0)], rows_sum(M, R, [W] * 3, ln2b))
 
     dwin[:, 3 * W : 4 * W] += dg(o[...], d16[...], 0, 0)
     o[...] = nt(d16[...], win[:, 3 * W : 4 * W]).astype(bf)
     dqkv = gp
 
-    @pl.loop(0, nb * 4)
+    @pl.loop(0, nb)
     def _(i):
-        rsl = pl.ds(pl.multiple_of((i // 4) * DS, 16), DS)
-        att_bwd(qkv, o, p, dqkv, rsl, W, i % 4, i * 4, 32)
-
-    def wq(c):
-        cs = pl.ds(c, 256)
-        dwin[:, cs] += dg(a1[...], dqkv[:, cs], 0, 0)
-    cols(3 * W, 256, wq)
-    def qb(r):
-        dsm[:, OFF[16] : OFF[16] + W] += rsum(dqkv[r, 0:W].astype(f32))
-        dsm[:, OFF[16] + W : OFF[17]] += rsum(dqkv[r, 2 * W : 3 * W].astype(f32))
-    rows(M, R, qb)
+        rsl = pl.ds(pl.multiple_of(i * DS, 16), DS)
+        for g in range(4):
+            att_bwd(qkv, o, p, dqkv, rsl, W, g, i * 16 + g * 4, 32)
+
+    dwin[:, 0 : 3 * W] += dg(a1[...], dqkv[:, 0 : 3 * W], 0, 0)
+    put([(16, 0), (16, W)], rows_sum(M, R, [W, W], lambda r: [dqkv[r, 0:W].astype(f32), dqkv[r, 2 * W : 3 * W].astype(f32)]))
     t[...] = nt(dqkv[:, 0 : 3 * W], win[:, 0 : 3 * W])
 
     def ln1b(r):
         da = t[r, :]
         xh = xh1[r, :]
-        gsum(14, da * xh)
-        gsum(15, da)
         x[r, :] = x[r, :] + norm_back(da, xh, rs1[r, :], part(sv, 14))
-    rows(M, R, ln1b)
+        return da * xh, da
+    put([(14, 0), (15, 0)], rows_sum(M, R, [W] * 2, ln1b))
 
     for b in range(nb):
         pick = (coder[b] == lax.broadcasted_iota(jnp.int32, (SEL, DS), 0)).astype(f32).astype(bf)
@@ -713,15 +702,20 @@
     return alone, shared
 
 
-def joiner(sh, which, src, dst, tmp, sem, base=0):
+MOST = 6
+
+
+def joiner(sh, which, src, dst, tmp, sem):
     alone, shared = tile_plan(sh, which)
     copies = []
     for c, lo, hi, at in alone:
         copies.append((src.at[c, :, pl.ds((lo - at) * 128, (hi - lo) * 128)], dst.at[:, pl.ds(lo * 128, (hi - lo) * 128)]))
     for u, (c, t, at, nxt) in enumerate(shared):
         copies.append((src.at[c, :, pl.ds((t - at) * 128, 128)], dst.at[:, pl.ds(t * 128, 128)]))
-        copies.append((src.at[c + 1, :, pl.ds((t - nxt) * 128, 128)], tmp.at[u]))
-    made = [pltpu.make_async_copy(a, b, sem.at[base + i]) for i, (a, b) in enumerate(copies)]
+        copies.append((src.at[c + 1, :, pl.ds((t - nxt) * 128, 128)], tmp.at[u % MOST]))
+    late = {len(alone) + 2 * u + 1 for u in range(MOST, len(shared))}
+    make = lambda i: pltpu.make_async_copy(*copies[i], sem.at[i])
+    made = [make(i) for i in range(len(copies)) if i not in late]
     for m in made:
         m.start()
 
@@ -729,14 +723,18 @@
         for m in made:
             m.wait()
         for u, (c, t, at, nxt) in enumerate(shared):
-            dst[:, t * 128 : (t + 1) * 128] += tmp[u]
+            if u >= MOST:
+                m = make(len(alone) + 2 * u + 1)
+                m.start()
+                m.wait()
+            dst[:, t * 128 : (t + 1) * 128] += tmp[u % MOST]
     return end
 
 
 def joiner_scratch(sh):
     V = pltpu.VMEM
     counts = [(len(a), len(s)) for a, s in (tile_plan(sh, "A"), tile_plan(sh, "B"))]
-    return [V((D, 5 * D + FF + DD), bf), V((D, FF), bf)] + [V((max(s, 1), D, 128), bf) for _, s in counts] + [
+    return [V((D, 5 * D + FF + DD), bf), V((D, FF), bf)] + [V((min(max(s, 1), MOST), D, 128), bf) for _, s in counts] + [
         pltpu.SemaphoreType.DMA((a + 2 * s,)) for a, s in counts]
 
 
@@ -750,7 +748,7 @@
     endb = joiner(sh, "B", bwin, wout, btmp, bsem)
     n = pix.shape[0]
     M = n * ES
-    R = 32
+    R = M // 2
     W = D
     for i in range(0, n, 2):
         two = []
@@ -785,10 +783,11 @@
         same = same | ((ki >= j * ES) & (ki < j * ES + KEEP + 1) & (qi >= j * ES) & (qi < (j + 1) * ES))
     bias[...] = jnp.where(same, 0.0, -1e30).astype(f32)
 
-    @pl.loop(0, (n // 4) * 6)
+    @pl.loop(0, n // 4)
     def _(i):
-        rsl = pl.ds(pl.multiple_of((i // 6) * EG, 16), EG)
-        att_fwd(qkv, o, p, bias[...], rsl, W, i % 6, i * 2, 64)
+        rsl = pl.ds(pl.multiple_of(i * EG, 16), EG)
+        for g in range(6):
+            att_fwd(qkv, o, p, bias[...], rsl, W, g, i * 12 + g * 2, 64)
 
     x[...] += nn(o[...], win[:, O_P : O_P + W]) + part(sv, 3)
 
@@ -799,12 +798,11 @@
         a2[r, :] = a.astype(bf)
     rows(M, R, ln2)
 
-    def fc1(c):
-        h = nn(a2[...], win[:, pl.ds(pl.multiple_of(O_F + c, 256), 256)])
-        g, dg_ = gelu_pair(h + sv[:, pl.ds(pl.multiple_of(OFF[6] + c, 128), 256)])
-        hid[:, pl.ds(c, 256)] = g.astype(bf)
-        gp[:, pl.ds(c, 256)] = dg_.astype(bf)
-    cols(FF, 256, fc1)
+    for c in range(0, FF, 512):
+        h = nn(a2[...], win[:, O_F + c : O_F + c + 512])
+        g, dg_ = gelu_pair(h + sv[:, OFF[6] + c : OFF[6] + c + 512])
+        hid[:, c : c + 512] = g.astype(bf)
+        gp[:, c : c + 512] = dg_.astype(bf)
     endb()
     x[...] += nt(hid[...], wout[...]) + part(sv, 7)
 
@@ -838,106 +836,105 @@
     )(pix, keepc, pos3, sv, awin, bwin)
 
 
-def enc_bwd_kernel(sh, dy, keepc, sv, awin, bwin, kept, xh1, xh2, xhf, rs1, rs2, rsf, a1, a2, e16, o, qkv, p, hid, gp,
-                   dwin, dwout, dsm, x, t, d16, dqkv, stage, sem, win, wout, atmp, btmp, asem, bsem):
+def enc_bwd_kernel(sh, dy, keepc, sv, awin, bwin, kept, xh1_in, xh2, xhf_in, rs1, rs2, rsf, a1_in, a2, e16_in, o, qkv, p, hid, gp,
+                   dwin, dwout, dsm, x, t, d16, dh16, stage, xb, ab, sem, lsem, win, wout, atmp, btmp, asem, bsem):
+    def fetch(i, src, dst):
+        copy = pltpu.make_async_copy(src, dst, lsem.at[i])
+        copy.start()
+        return copy
+
+    at_e, at_xhf = fetch(0, e16_in, ab), fetch(1, xhf_in, xb)
     enda = joiner(sh, "A", awin, win, atmp, asem)
     endb = joiner(sh, "B", bwin, wout, btmp, bsem)
     M = dy.shape[0]
-    R = 32
+    R = M // 2
     W = D
-    CW = 256
     dsm[...] = jnp.zeros_like(dsm)
 
-    def gsum(i, v, lo=0, n=None):
-        a = OFF[i] + lo
-        n = LENS[i] if n is None else n
-        dsm[:, pl.ds(a, n)] += rsum(v)
-
-    def put(out, count, base, value):
-        def copy(i, slot):
-            return pltpu.make_async_copy(stage.at[slot], out.at[:, pl.ds(pl.multiple_of(base + i * CW, 128), CW)], sem.at[slot])
-
-        @pl.loop(0, count)
-        def _(i):
-            slot = lax.rem(i, 2)
-
-            @pl.when(i >= 2)
-            def _():
-                copy(i - 2, slot).wait()
-            stage[slot] = value(pl.multiple_of(i * CW, CW)).astype(bf)
-            copy(i, slot).start()
-        for i in range(max(count - 2, 0), count):
-            copy(i, i % 2).wait()
+    def save(where, sums):
+        for (i, lo), v in zip(where, sums):
+            dsm[:, OFF[i] + lo : OFF[i] + lo + v.shape[1]] += v
+
+    shots = []
+
+    def put(out, base, value):
+        width = value.shape[1]
+        slot = len(shots) % 2
+        if len(shots) >= 2:
+            shots[-2].wait()
+        stage[slot, :, 0:width] = value.astype(bf)
+        copy = pltpu.make_async_copy(stage.at[slot, :, pl.ds(0, width)], out.at[:, pl.ds(base, width)], sem.at[slot])
+        copy.start()
+        shots.append(copy)
 
     def emb(r):
         v = dy[r, :]
-        gsum(12, v)
         d16[r, 0:DD] = v.astype(bf)
-    rows(M, R, emb)
-    put(dwin, DD // CW, O_E, lambda c: dg(e16[...], d16[:, pl.ds(c, CW)], 0, 0))
+        return [v]
+    save([(12, 0)], rows_sum(M, R, [DD], emb))
+    at_e.wait()
+    put(dwin, O_E, dg(ab[...], d16[:, 0:DD], 0, 0))
+    at_a = fetch(2, a1_in, ab)
     enda()
     endb()
     t[...] = nt(d16[:, 0:DD], win[:, O_E:])
 
+    at_xhf.wait()
+
     def lnfb(r):
         da = t[r, :]
-        xh = xhf[r, :]
-        gsum(8, da * xh)
-        gsum(9, da)
+        xh = xb[r, :]
         dx = norm_back(da, xh, rsf[r, :], part(sv, 8))
-        gsum(7, dx)
         x[r, :] = dx
         d16[r, :] = dx.astype(bf)
-    rows(M, R, lnfb)
-    put(dwout, FF // CW, 0, lambda c: dg(d16[...], hid[:, pl.ds(c, CW)], 0, 0))
-
-    def fc1b(c):
-        cs = pl.ds(c, CW)
-        dh = nn(d16[...], wout[:, cs]) * gp[:, cs].astype(f32)
-        dsm[:, pl.ds(pl.multiple_of(OFF[6] + c, 128), CW)] += rsum(dh)
-        gp[:, cs] = dh.astype(bf)
-        return dg(a2[...], gp[:, cs], 0, 0)
-    put(dwin, FF // CW, O_F, fc1b)
-    t[...] = nt(gp[...], win[:, O_F:O_E])
+        return da * xh, da, dx
+    save([(8, 0), (9, 0), (7, 0)], rows_sum(M, R, [W] * 3, lnfb))
+    at_xh1 = fetch(3, xh1_in, xb)
+    for c in range(0, FF, W):
+        put(dwout, c, dg(d16[...], hid[:, c : c + W], 0, 0))
+        dh = nn(d16[...], wout[:, c : c + W]) * gp[:, c : c + W].astype(f32)
+        dsm[:, OFF[6] + c : OFF[6] + c + W] += rsum(dh)
+        dh16[:, c : c + W] = dh.astype(bf)
+        put(dwin, O_F + c, dg(a2[...], dh16[:, c : c + W], 0, 0))
+    t[...] = nt(dh16[...], win[:, O_F:O_E])
+    dqkv = dh16
 
     def ln2b(r):
         da = t[r, :]
         xh = xh2[r, :]
-        gsum(4, da * xh)
-        gsum(5, da)
         dx = x[r, :] + norm_back(da, xh, rs2[r, :], part(sv, 4))
-        gsum(3, dx)
         x[r, :] = dx
         d16[r, :] = dx.astype(bf)
-    rows(M, R, ln2b)
-    put(dwin, D // CW, O_P, lambda c: dg(o[...], d16[:, pl.ds(c, CW)], 0, 0))
+        return da * xh, da, dx
+    save([(4, 0), (5, 0), (3, 0)], rows_sum(M, R, [W] * 3, ln2b))
+    put(dwin, O_P, dg(o[...], d16[...], 0, 0))
     d16[...] = nt(d16[...], win[:, O_P:O_F]).astype(bf)
 
-    @pl.loop(0, (M // EG) * 6)
+    @pl.loop(0, M // EG)
     def _(i):
-        rsl = pl.ds(pl.multiple_of((i // 6) * EG, 16), EG)
-        att_bwd(qkv, d16, p, dqkv, rsl, W, i % 6, i * 2, 64)
-
-    put(dwin, 3 * D // CW, O_Q, lambda c: dg(a1[...], dqkv[:, pl.ds(c, CW)], 0, 0))
-    def qb(r):
-        dsm[:, OFF[2] : OFF[2] + W] += rsum(dqkv[r, 0:W].astype(f32))
-        dsm[:, OFF[2] + W : OFF[3]] += rsum(dqkv[r, 2 * W : 3 * W].astype(f32))
-    rows(M, R, qb)
-    t[...] = nt(dqkv[...], win[:, O_Q:O_P])
+        rsl = pl.ds(pl.multiple_of(i * EG, 16), EG)
+        for g in range(6):
+            att_bwd(qkv, d16, p, dqkv, rsl, W, g, i * 12 + g * 2, 64)
+
+    at_a.wait()
+    for c in range(0, 3 * D, W):
+        put(dwin, O_Q + c, dg(ab[...], dqkv[:, c : c + W], 0, 0))
+    save([(2, 0), (2, W)], rows_sum(M, R, [W, W], lambda r: [dqkv[r, 0:W].astype(f32), dqkv[r, 2 * W : 3 * W].astype(f32)]))
+    t[...] = nt(dqkv[:, 0 : 3 * W], win[:, O_Q:O_P])
+    at_xh1.wait()
 
     def ln1b(r):
         da = t[r, :]
-        xh = xh1[r, :]
-        gsum(0, da * xh)
-        gsum(1, da)
+        xh = xb[r, :]
         dx = x[r, :] + norm_back(da, xh, rs1[r, :], part(sv, 0))
         kc = keepc[r, :]
-        gsum(11, jnp.where(kc == NOROW - 1, dx, 0.0))
-        dx = jnp.where(kc < PATCHES, dx, 0.0)
-        gsum(10, dx)
-        d16[r, :] = dx.astype(bf)
-    rows(M, R, ln1b)
-    put(dwin, D // CW, 0, lambda c: dg(kept[...], d16[:, pl.ds(c, CW)], 0, 0))
+        only = jnp.where(kc < PATCHES, dx, 0.0)
+        d16[r, :] = only.astype(bf)
+        return da * xh, da, jnp.where(kc == NOROW - 1, dx, 0.0), only
+    save([(0, 0), (1, 0), (11, 0), (10, 0)], rows_sum(M, R, [W] * 4, ln1b))
+    put(dwin, 0, dg(kept[...], d16[...], 0, 0))
+    for c in shots[-2:]:
+        c.wait()
 
 
 def encoder_bwd(sh, dy, keepc, sv, awin, bwin, saved):
@@ -947,12 +944,12 @@
     anyspec = pl.BlockSpec(memory_space=pl.ANY)
     return pl.pallas_call(
         functools.partial(enc_bwd_kernel, sh),
-        in_specs=vspec(3) + [pl.BlockSpec(memory_space=pl.ANY)] * 2 + vspec(len(saved)),
+        in_specs=[anyspec if i in (3, 4, 6, 8, 12, 14) else spec for i, spec in enumerate(vspec(5 + len(saved)))],
         out_specs=[anyspec, anyspec, pl.BlockSpec(memory_space=pltpu.VMEM)],
         out_shape=[S((D, 5 * D + FF + DD), bf), S((D, FF), bf), S((1, SMALL), f32)],
-        scratch_shapes=[V((M, D), f32), V((M, D), f32), V((M, D), bf), V((M, 3 * D), bf), V((2, D, 256), bf),
-                        pltpu.SemaphoreType.DMA((2,))] + joiner_scratch(sh),
-        compiler_params=pltpu.CompilerParams(vmem_limit_bytes=62 << 20),
+        scratch_shapes=[V((M, D), f32), V((M, D), f32), V((M, D), bf), V((M, FF), bf), V((2, D, D), bf), V((M, D), f32), V((M, D), bf),
+                        pltpu.SemaphoreType.DMA((2,)), pltpu.SemaphoreType.DMA((4,))] + joiner_scratch(sh),
+        compiler_params=pltpu.CompilerParams(vmem_limit_bytes=63 << 20),
         name="encoder_bwd",
     )(dy, keepc, sv, awin, bwin, *saved)
 

time: 782 us -> 573 us (0.73)
  Pallas kernels: 734 us -> 528 us
    pallas_call x1, Pallas kernels: 340 us -> 163 us  [decoder(): pl.pallas_call(functools.partial(dec_kernel, scale, nb), grid=(n // nb,),...]
    pallas_call x1, Pallas kernels: 83.6 us -> 61.3 us  [encoder_bwd(): pl.pallas_call(functools.partial(enc_bwd_kernel, sh), in_specs=[anyspec i...]
where the time goes in v3:
time: 573 us; the launch traced here: 569 us
  Pallas kernels  528 us (92%)
  local copies, waits for them, and re-layouts  18.8 us (3%)
  other arithmetic  18.8 us (3%)
    pallas_call x1, Pallas kernels, decoder(): pl.pallas_call(functools.partial(dec_kernel, scale, nb), grid=(n // nb,),...  163 us
    pallas_call x1, Pallas kernels, reduce_grads(): pl.pallas_call(functools.partial(reduce_kernel, nrow, ncol), in_specs=[an...  137 us
    pallas_call x1, Pallas kernels, gather_weights(): pl.pallas_call(functools.partial(gather_kernel, nrow, ncol), in_specs=[an...  110 us
    pallas_call x1, Pallas kernels, encoder_bwd(): pl.pallas_call(functools.partial(enc_bwd_kernel, sh), in_specs=[anyspec i...  61.3 us
    pallas_call x1, Pallas kernels, encoder_fwd(): pl.pallas_call(functools.partial(enc_fwd_kernel, sh), in_specs=vspec(4) +...  56.4 us

profile of v3, /device:TPU:0, one launch (start us, length us, event | category | flops | bytes accessed | tf_op | source)
XLA Modules:
  0.0 568.7 jit_solution(12049753935388036516)
XLA Ops:
  0.7 1.2 convert_element_type.14
  2.0 2.3 dynamic_update_slice.3.ain
  4.3 0.7 convert_bitcast_fusion.bin_
  5.1 0.7 convert_element_type.16.cin
  5.7 0.6 convert_bitcast_fusion.1.din
  6.4 109.7 %gather_weights.1 = (bf16[8,768,1024]{2,1,0:T(8,128)(2,1)}, bf16[4,768,768]{2,1,0:T(8,128)(2,1)}, bf16[512,4096]{1,0:T(8,128)(2,1)}, bf16[512,2048]{1,0:T(8,128)(2,1)}) custom-call(bf16[192,1024]{1,0:T(8,128)(2,1)} %copy-done.2, bf16[96,768]{1,0:T(8,128)(2,1)} %convert_bitcast_fusion.bin_, bf16[128,512]{1,0:T(8,128)(2,1)} %convert_element_type.16.cin, ...), custom_call_target="tpu_custom_call" | custom-call | tf_op jit(solution)/shard_map/gather_weights/pallas_call | solution.py:477
  116.1 0.7 reshape.74.sv
  116.8 4.1 pad.4.pix
  121.1 0.9 reshape.83.keepc
  122.0 56.4 %encoder_fwd.1 = (f32[672,512]{1,0:T(8,128)}, bf16[672,768]{1,0:T(8,128)(2,1)}, f32[672,768]{1,0:T(8,128)}, f32[672,768]{1,0:T(8,128)}, f32[672,768]{1,0:T(8,128...) custom-call(bf16[12,208,768]{2,1,0:T(8,128)(2,1)} %pad.4.pix, ...), custom_call_target="tpu_custom_call" | custom-call | tf_op jit(solution)/shard_map/encoder_fwd/pallas_call | solution.py:830
  178.6 1.5 copy.45.codec
  180.1 0.6 reshape.77.coder
  180.7 163.5 %decoder.1 = (f32[12,56,512]{2,1,0:T(8,128)}, bf16[512,4096]{1,0:T(8,128)(2,1)}, bf16[512,2048]{1,0:T(8,128)(2,1)}, f32[512,768]{1,0:T(8,128)}, f32[1,21248]{1,0:T(1,128)}, /*index=5*/f32[1,128]{1,0:T(1,128)}) custom-call(f32[12,56,512]{2,1,0:T(8,128)} %bitcast.31, s32[12,208,1]{2,1,0:T(8,128)} %copy.45.codec, s32[12,1,208]{2,1,0:T(1,128)} %reshape.77.coder, ...), custom_call_target="tpu_custom_call" | custom-call | tf_op jit(solution)/shard_map/decoder/pallas_call | solution.py:329
  344.2 61.3 %encoder_bwd.1 = (bf16[768,7424]{1,0:T(8,128)(2,1)}, bf16[768,3072]{1,0:T(8,128)(2,1)}, f32[1,21248]{1,0:T(1,128)}) custom-call(f32[672,512]{1,0:T(8,128)} %bitcast.30, s32[672,1]{1,0:T(8,128)} %reshape.83.keepc, f32[1,21248]{1,0:T(1,128)} %reshape.74.sv, bf16[8,768,1024]{2,1,0:T(8,128)(2,1)} %get-tuple-element.54.awin, ...), custom_call_target="tpu_custom_call" | custom-call | tf_op jit(solution)/shard_map/encoder_bwd/pallas_call | solution.py:945
  405.5 1.8 add_reduce_fusion
  407.3 1.4 reshape.79
  408.8 1.0 pad_maximum_fusion
  409.8 1.7 reshape.81.de
  411.5 137.1 %reduce_grads.1 = (f32[192,1024]{1,0:T(8,128)}, f32[96,768]{1,0:T(8,128)}, f32[128,512]{1,0:T(8,128)}, f32[64,512]{1,0:T(8,128)}, f32[32,64,256]{2,1,0:T(8,128)}) custom-call(bf16[768,7424]{1,0:T(8,128)(2,1)} %get-tuple-element.75.da, bf16[768,3072]{1,0:T(8,128)(2,1)} %get-tuple-element.76.db, bf16[512,4096]{1,0:T(8,128)(2,1)} %get-tuple-element.77.dc, ...), custom_call_target="tpu_custom_call" | custom-call | tf_op jit(solution)/shard_map/reduce_grads/pallas_call | solution.py:657
  548.6 1.6 slice.20
  550.3 0.9 copy.47
  551.3 1.0 slice_reduce_fusion
  552.3 0.6 slice_reduce_fusion.1
  553.6 0.7 multiply_subtract_fusion.5
  554.5 1.4 mul.357
  555.9 0.3 copy-done
  556.3 5.4 multiply_subtract_fusion
  561.7 0.8 multiply_subtract_fusion.4
  562.6 1.0 multiply_subtract_fusion.3
  563.6 1.1 multiply_subtract_fusion.2
  564.8 2.1 multiply_subtract_fusion.1
  566.9 0.5 slice.23
  (66 shorter events, 0.8 us)
Async XLA Ops:
  0.7 3.7 copy-start.3
  0.7 4.4 copy-start.5
  0.7 5.0 copy-start.10
  2.0 114.1 %copy-start.11 = (f32[21248]{0:T(1024)S(1)}, f32[21248]{0:T(1024)}, u32[]{:S(2)}) copy-start(f32[21248]{0:T(1024)} %param.31) | copy-start | bytes 254980
  4.3 2.0 copy-start.2
  116.8 4.3 copy-start.26
  122.0 56.4 %copy-start.25 = (s32[12,196]{1,0:T(8,128)S(1)}, s32[12,196]{1,0:T(8,128)}, u32[]{:S(2)}) copy-start(s32[12,196]{1,0:T(8,128)} %param.25) | copy-start | bytes 28228
  344.2 61.3 %copy-start.24 = (f32[1,21248]{1,0:T(1,128)S(1)}, f32[1,21248]{1,0:T(1,128)}, u32[]{:S(2)}) copy-start(f32[1,21248]{1,0:T(1,128)} %get-tuple-element.80) | copy-start | bytes 254980
  550.3 3.3 copy-start.12
  550.3 3.3 copy-start.22
  550.3 3.3 copy-start.23
  554.5 1.8 copy-start
  556.2 5.4 copy-start.19
  556.2 5.4 copy-start.20
  556.2 5.5 copy-start.21
  556.2 6.3 %copy-start.6 = (f32[128,512]{1,0:T(8,128)S(1)}, f32[128,512]{1,0:T(8,128)}, u32[]{:S(2)}) copy-start(f32[128,512]{1,0:T(8,128)} %param.28) | copy-start | bytes 786436
  556.2 6.3 %copy-start.16 = (f32[128,512]{1,0:T(8,128)S(1)}, f32[128,512]{1,0:T(8,128)}, u32[]{:S(2)}) copy-start(f32[128,512]{1,0:T(8,128)} %param.34) | copy-start | bytes 786436
  556.3 6.3 %copy-start.17 = (f32[128,512]{1,0:T(8,128)S(1)}, f32[128,512]{1,0:T(8,128)}, u32[]{:S(2)}) copy-start(f32[128,512]{1,0:T(8,128)} %param.40) | copy-start | bytes 786436
  556.3 6.2 %copy-start.18 = (f32[128,512]{1,0:T(8,128)S(1)}, f32[128,512]{1,0:T(8,128)}, u32[]{:S(2)}) copy-start(f32[128,512]{1,0:T(8,128)} %get-tuple-element.86) | copy-start | bytes 786436
  561.6 1.9 copy-start.4
  561.7 1.9 copy-start.13
  561.7 1.9 copy-start.14
  561.7 1.9 copy-start.15
  562.5 2.1 copy-start.1
  562.5 2.1 copy-start.7
  562.5 2.1 copy-start.8
  562.6 2.3 copy-start.9

commit v4 on v3

--- a/solution.py
+++ b/solution.py
@@ -163,9 +163,9 @@
     dqkv[rsl, c2 : c2 + 128] = unstack(nn(probs, d), hd).astype(bf)
 
 
-def dec_kernel(scale, nb, y, codec, coder, pix, pos, sv, win, wout, hw,
+def dec_kernel(scale, nb, y, coder, pix, pos, sv, win, wout, hw,
                dy, win_out, wout_out, dhw, dsm, loss,
-               dwin, dwout, x, t, xh1, xh2, xhf, rs1, rs2, rsf, tm, tr, a1, a2, u, o, qkv, p, hid, gp, dpr, d16, lacc):
+               dwin, dwout, x, t, xh1, xh2, xhf, rs1, rs2, rsf, tm, tr, a1, a2, u, o, qkv, p, hid, gp, dpr, d16, hide, lacc):
     M = nb * DS
     R = M
     W = DD
@@ -175,6 +175,7 @@
         dsm[...] = jnp.zeros_like(dsm)
         loss[...] = jnp.zeros_like(loss)
         lacc[...] = jnp.zeros_like(lacc)
+        dpr[...] = jnp.zeros_like(dpr)
         for ref in (dwin, dwout, dhw):
             rows(ref.shape[0], 16, lambda r: ref.__setitem__((r, slice(None)), jnp.zeros((16, ref.shape[1]), f32)))
 
@@ -183,13 +184,15 @@
             dsm[:, OFF[i] + lo : OFF[i] + lo + v.shape[1]] += v
 
     for b in range(nb):
-        pick = (codec[b] == lax.broadcasted_iota(jnp.int32, (DS, SEL), 1)).astype(f32).astype(bf)
+        pick = (coder[b] == lax.broadcasted_iota(jnp.int32, (SEL, DS), 0)).astype(f32).astype(bf)
         tok = jnp.where(lax.broadcasted_iota(jnp.int32, (8, W), 0) == 0, part(sv, 13), 0.0)
         table = jnp.concatenate([y[b], jnp.zeros((8, W), f32), tok, jnp.zeros((8, W), f32)], axis=0)
         z = pos[...]
         for piece in pieces(table):
-            z = z + nn(pick, piece)
+            z = z + dg(pick, piece, 0, 0)
         x[b * DS : (b + 1) * DS, :] = z
+        mark = (lax.broadcasted_iota(jnp.int32, (SEL, 128), 0) == 64).astype(f32).astype(bf)
+        hide[b * DS : (b + 1) * DS, :] = dg(pick, mark, 0, 0)[:, 0:1]
 
     def ln1(r):
         xh, rs, a = norm_rows(x[r, :], part(sv, 14), part(sv, 15))
@@ -239,21 +242,22 @@
         v = pix[b].astype(f32)
         m = jnp.mean(v, axis=1, keepdims=True)
         c = v - m
-        tm[b * DS : (b + 1) * DS, :] = m
-        tr[b * DS : (b + 1) * DS, :] = lax.rsqrt(jnp.mean(c * c, axis=1, keepdims=True) + 1e-06)
+        tm[b * DS : b * DS + PATCHES, :] = m
+        tr[b * DS : b * DS + PATCHES, :] = lax.rsqrt(jnp.mean(c * c, axis=1, keepdims=True) + 1e-06)
 
     for c in range(0, PIX, 256):
         pr = nn(u[...], hw[:, c : c + 256].astype(bf)) + sv[:, OFF[24] + c : OFF[24] + c + 256]
         for b in range(nb):
-            sl = slice(b * DS, (b + 1) * DS)
+            sl = slice(b * DS, b * DS + PATCHES)
             tgt = (pix[b, :, c : c + 256].astype(f32) - tm[sl, :]) * tr[sl, :]
-            diff = jnp.where(codec[b] == 64, pr[sl] - tgt, 0.0)
+            diff = jnp.where(hide[sl, :] > 0.5, pr[sl] - tgt, 0.0)
             lacc[...] += rsum(diff * diff)
             dp = diff * (2.0 * scale / PIX)
             dsm[:, OFF[24] + c : OFF[24] + c + 256] += rsum(dp)
             dpr[sl, c : c + 256] = dp.astype(bf)
 
-    dhw[...] += dg(u[...], dpr[...], 0, 0)
+    for c in range(0, PIX, 256):
+        dhw[2 * c : 2 * c + DD, :] += dg(u[...], dpr[:, c : c + 256], 0, 0)
     t[...] = nt(dpr[...], hw[...].astype(bf))
 
     def lnfb(r):
@@ -319,7 +323,7 @@
             rows(DD, 16, lambda r: dst.__setitem__((r, slice(None)), src[r, :].astype(bf)))
 
 
-def decoder(y, codec, coder, pix, pos, sv, win, wout, hw, scale, nb=2):
+def decoder(y, coder, pix, pos, sv, win, wout, hw, scale, nb=2):
     n = y.shape[0]
     M = nb * DS
     whole = lambda a: pl.BlockSpec(a.shape, lambda i: (0,) * a.ndim, pipeline_mode=pl.Buffered(1))
@@ -329,22 +333,22 @@
     return pl.pallas_call(
         functools.partial(dec_kernel, scale, nb),
         grid=(n // nb,),
-        in_specs=[blk((ES, DD)), blk((DS, 1)), blk((1, DS)), blk((DS, PIX)), whole(pos), whole(sv), whole(win), whole(wout), whole(hw)],
-        out_specs=[blk((ES, DD)), fixed(win.shape), fixed(wout.shape), fixed(hw.shape), fixed((1, SMALL)), fixed((1, 128))],
+        in_specs=[blk((ES, DD)), blk((1, DS)), blk((PATCHES, PIX)), whole(pos), whole(sv), whole(win), whole(wout), whole(hw)],
+        out_specs=[blk((ES, DD)), fixed(win.shape), fixed(wout.shape), fixed((3 * DD, 256)), fixed((1, SMALL)), fixed((1, 128))],
         out_shape=[
             jax.ShapeDtypeStruct((n, ES, DD), f32), jax.ShapeDtypeStruct(win.shape, bf),
-            jax.ShapeDtypeStruct(wout.shape, bf), jax.ShapeDtypeStruct(hw.shape, f32),
+            jax.ShapeDtypeStruct(wout.shape, bf), jax.ShapeDtypeStruct((3 * DD, 256), f32),
             jax.ShapeDtypeStruct((1, SMALL), f32), jax.ShapeDtypeStruct((1, 128), f32)],
         scratch_shapes=[
             V(win.shape, f32), V(wout.shape, f32),
             V((M, DD), f32), V((M, DD), f32), V((M, DD), f32), V((M, DD), f32), V((M, DD), f32),
             V((M, 1), f32), V((M, 1), f32), V((M, 1), f32), V((M, 1), f32), V((M, 1), f32),
             V((M, DD), bf), V((M, DD), bf), V((M, DD), bf), V((M, DD), bf), V((M, 3 * DD), bf),
-            V((nb * DHEADS, DS, DS), bf), V((M, DFF), bf), V((M, DFF), bf), V((M, PIX), bf), V((M, DD), bf),
+            V((nb * DHEADS, DS, DS), bf), V((M, DFF), bf), V((M, DFF), bf), V((M, PIX), bf), V((M, DD), bf), V((M, 1), f32),
             V((1, 256), f32)],
         compiler_params=pltpu.CompilerParams(vmem_limit_bytes=60 << 20),
         name="decoder",
-    )(y, codec, coder, pix, pos, sv, win, wout, hw)
+    )(y, coder, pix, pos, sv, win, wout, hw)
 
 
 class Place:
@@ -360,7 +364,7 @@
         for k, v in self.at.items():
             step = by.get(k, 0)
             size = 2 if k == "core" else self.n[k]
-            at[k] = v if step == 0 else lax.rem(v + (step % size), size)
+            at[k] = v if step % size == 0 else lax.rem(v + (step % size), size)
         return at["y"] * self.n["x"] + at["x"], at["z"] * 2 + at["core"]
 
     def greet(self):
@@ -368,22 +372,38 @@
         count = 0
         for axis in ("x", "y", "z", "core"):
             size = 2 if axis == "core" else self.n[axis]
-            for step in sorted({1 % size, (size - 1) % size} - {0}):
+            for step in range(1, size):
                 pl.semaphore_signal(sem, inc=1, device_id=self.moved(**{axis: step}), device_id_type=pl.DeviceIdType.MESH)
                 count += 1
         pl.semaphore_wait(sem, count)
 
+    def remote(self, src, dst, ssem, rsem, **by):
+        return pltpu.make_async_remote_copy(src, dst, ssem, rsem, device_id=self.moved(**by), device_id_type=pl.DeviceIdType.MESH)
+
+
+ORDER = {
+    "A0": ("z", "x", "y"), "A1": ("z", "y", "x"), "B": ("y", "x", "z"),
+    "C": ("z", "x", "y"), "D": ("z", "y", "x"), "E": ("z", "y", "x"),
+}
+DIRECT = ("E",)
+
 
 class Shapes:
     def __init__(self, nrow, ncol):
         self.nrow, self.ncol = nrow, ncol
+        self.half = nrow * ncol // 2
+        side = math.isqrt(nrow)
+        self.n = {"x": side, "y": nrow // side, "z": ncol // 2}
         self.awide, self.bwide = (5 * D + FF + DD) // ncol, FF // nrow
         self.alanes, self.blanes = self.window(self.awide, ncol), self.window(self.bwide, nrow)
         self.arows, self.brows = D // nrow, D // ncol
-        self.crows, self.clanes = DD // nrow, 4 * DD // ncol + DFF // ncol
+        self.acut = self.arows // 32 * 16
+        self.crows, self.clanes = DD // nrow, (4 * DD + DFF) // ncol
         self.drows, self.dlanes = DD // ncol, DFF // nrow
         self.erows = -(-(DD * PIX + SMALL) // (nrow * ncol * 256 * 8)) * 8
-        self.blocks = {"A": (self.arows, self.alanes), "B": (self.brows, self.blanes), "C": (self.crows, self.clanes), "D": (self.drows, self.dlanes)}
+        self.blocks = {
+            "A0": (self.acut, self.alanes), "A1": (self.arows - self.acut, self.alanes), "B": (self.brows, self.blanes),
+            "C": (self.crows, self.clanes), "D": (self.drows, self.dlanes), "E": (self.erows, 256)}
 
     @staticmethod
     def window(wide, count):
@@ -397,275 +417,242 @@
             return min(first, last) * 128
         return jnp.minimum(first, last) * 128
 
-
-STREAMS = (("A",), ("B", "C", "D"))
-ORDER = (("x", "y"), ("y", "x"))
-
-
-def gather_kernel(nrow, ncol, ain, bin_, cin, din, aout, bout, cout, dout, send, recv, csend, crecv, lsem):
-    place = Place(nrow, ncol)
-    sh = Shapes(nrow, ncol)
-    ins = {"A": ain, "B": bin_, "C": cin, "D": din}
-    mats = "ABCD"
+    def axes(self, m):
+        return ORDER[m], tuple(self.n[a] for a in ORDER[m])
+
+    def steps(self, mats, back):
+        out = []
+        for pos, m in enumerate(mats):
+            _, (na, nb, nc) = self.axes(m)
+            for i in range(nc):
+                for j in range(nb):
+                    for k in range(na):
+                        key = (na - 1 - k) + (nb - 1 - j) + (nc - 1 - i) if back else i + j + (min(k, 1) if m in DIRECT else k)
+                        out.append((key, pos, m, i, j, k))
+        return [t[2:] for t in sorted(out)]
+
+    def onward(self, m, i, j, k):
+        (a, b, c), (na, nb, nc) = self.axes(m)
+        slot = (i * nb + j) * na + k
+        out = []
+        if m in DIRECT and i == j == k == 0:
+            out += [(a, t, t) for t in range(1, na)]
+        if m not in DIRECT and i == j == 0 and k < na - 1:
+            out.append((a, 1, slot + 1))
+        if i == 0 and j < nb - 1:
+            out.append((b, 1, slot + na))
+        if i < nc - 1:
+            out.append((c, 1, slot + na * nb))
+        return slot, out
+
+
+def spread(place, sh, mats, first, spot, send, recv, csend, crecv):
+    sent, late = [], []
+    for m, i, j, k in sh.steps(mats, False):
+        (a, b, c), _ = sh.axes(m)
+        slot, onward = sh.onward(m, i, j, k)
+        by = {c: -i, b: -j, a: -k}
+        dst = spot(m, *place.moved(**by))
+        own = i == j == k == 0
+        src = first(m) if own else dst
+        if not own:
+            place.remote(dst, dst, send[m].at[slot], recv[m].at[slot], core=1).wait_recv()
+        for axis, far, there in onward:
+            copy = place.remote(src, dst, send[m].at[there], recv[m].at[there], **{axis: far})
+            copy.start()
+            sent.append(copy)
+        copy = place.remote(src, dst, csend[m].at[slot], crecv[m].at[slot], core=1)
+        copy.start()
+        sent.append(copy)
+        other = spot(m, *place.moved(core=1, **by))
+        late.append(place.remote(other, other, csend[m].at[slot], crecv[m].at[slot], core=1))
+    for copy in late:
+        copy.wait_recv()
+    for copy in sent:
+        copy.wait_send()
+
+
+def block_at(sh, m, ref, row, col, gathered):
+    mul = pl.multiple_of
+    if m in ("A0", "A1"):
+        skip = 0 if m == "A0" else sh.acut
+        r = pl.ds(mul(row * sh.arows + skip, 16), sh.blocks[m][0])
+        return ref.at[col, r, :] if gathered else ref.at[r, pl.ds(mul(sh.start("A", col), 128), sh.alanes)]
+    if m == "B":
+        r = pl.ds(mul(col * sh.brows, 16), sh.brows)
+        return ref.at[row, r, :] if gathered else ref.at[r, pl.ds(mul(sh.start("B", row), 128), sh.blanes)]
+    if m == "C":
+        return ref.at[pl.ds(mul(row * sh.crows, 16), sh.crows), pl.ds(mul(col * sh.clanes, 128), sh.clanes)]
+    if m == "D":
+        return ref.at[pl.ds(mul(col * sh.drows, 16), sh.drows), pl.ds(mul(row * sh.dlanes, 128), sh.dlanes)]
+    return ref.at[row * sh.ncol + col]
+
+
+def gather_kernel(sh, mats, *refs):
+    place = Place(sh.nrow, sh.ncol)
+    whole = sorted({m[0] for m in mats})
+    n = len(whole)
+    ins, outs = dict(zip(whole, refs[:n])), dict(zip(whole, refs[n : 2 * n]))
+    sems = refs[2 * n :]
+    send, recv, csend, crecv = (dict(zip(mats, sems[t * len(mats) :])) for t in range(4))
+    lsem = sems[4 * len(mats)]
 
     def spot(m, row, col):
-        if m == "A":
-            return aout.at[col, pl.ds(pl.multiple_of(row * sh.arows, 16), sh.arows), :]
-        if m == "B":
-            return bout.at[row, pl.ds(pl.multiple_of(col * sh.brows, 16), sh.brows), :]
-        if m == "C":
-            return cout.at[pl.ds(pl.multiple_of(row * sh.crows, 16), sh.crows), pl.ds(pl.multiple_of(col * sh.clanes, 128), sh.clanes)]
-        return dout.at[pl.ds(pl.multiple_of(col * sh.drows, 16), sh.drows), pl.ds(pl.multiple_of(row * sh.dlanes, 128), sh.dlanes)]
-
-    nz = place.n["z"]
+        return block_at(sh, m, outs[m[0]], row, col, True)
+
+    def first(m):
+        if m == "A0":
+            return ins["A"].at[pl.ds(0, sh.acut), :]
+        if m == "A1":
+            return ins["A"].at[pl.ds(sh.acut, sh.arows - sh.acut), :]
+        return ins[m]
+
     place.greet()
-    me = place.moved()
-    locals_ = [pltpu.make_async_copy(ins[m], spot(m, *me), lsem.at[i]) for i, m in enumerate(mats)]
-    for c in locals_:
-        c.start()
-    steps = []
-    for s in (0, 1):
-        p, q = ORDER[s]
-        for i in range(place.n[q]):
-            for j in range(place.n[p]):
-                for k in range(nz):
-                    steps.append((i + j + k, k, s, i, j, k))
-    steps.sort()
-    sent = []
-    late = []
-    for _, _, s, i, j, k in steps:
-        p, q = ORDER[s]
-        npp, nq = place.n[p], place.n[q]
-        slot = (i * npp + j) * nz + k
-        own = i == j == k == 0
-        for m in STREAMS[s]:
-            mi = mats.index(m)
-            dst = spot(m, *place.moved(**{q: -i, p: -j, "z": -k}))
-            src = ins[m] if own else dst
-            if not own:
-                pltpu.make_async_remote_copy(dst, dst, send.at[mi, slot], recv.at[mi, slot], device_id=place.moved(core=1), device_id_type=pl.DeviceIdType.MESH).wait_recv()
-            plan = []
-            if i == j == 0 and k < nz - 1:
-                plan.append(({"z": 1}, slot + 1))
-            if i == 0 and j < npp - 1:
-                plan.append(({p: 1}, slot + nz))
-            if i < nq - 1:
-                plan.append(({q: 1}, slot + nz * npp))
-            for by, there in plan:
-                c = pltpu.make_async_remote_copy(src, dst, send.at[mi, there], recv.at[mi, there], device_id=place.moved(**by), device_id_type=pl.DeviceIdType.MESH)
-                c.start()
-                sent.append(c)
-            c = pltpu.make_async_remote_copy(src, dst, csend.at[mi, slot], crecv.at[mi, slot], device_id=place.moved(core=1), device_id_type=pl.DeviceIdType.MESH)
-            c.start()
-            sent.append(c)
-            other = spot(m, *place.moved(**{q: -i, p: -j, "z": -k, "core": 1}))
-            late.append(pltpu.make_async_remote_copy(other, other, csend.at[mi, slot], crecv.at[mi, slot], device_id=place.moved(core=1), device_id_type=pl.DeviceIdType.MESH))
-    for c in late:
-        c.wait_recv()
-    for c in sent:
-        c.wait_send()
-    for c in locals_:
-        c.wait()
-
-
-def gather_weights(nrow, ncol, ain, bin_, cin, din):
-    sh = Shapes(nrow, ncol)
-    half = nrow * ncol // 2
+    own = [pltpu.make_async_copy(first(m), spot(m, *place.moved()), lsem.at[i]) for i, m in enumerate(mats)]
+    for copy in own:
+        copy.start()
+    spread(place, sh, mats, first, spot, send, recv, csend, crecv)
+    for copy in own:
+        copy.wait()
+
+
+def gather_weights(sh, mats, *blocks):
     S = jax.ShapeDtypeStruct
     anyspec = pl.BlockSpec(memory_space=pl.ANY)
     sem = pltpu.SemaphoreType.DMA
+    out = {"A": S((sh.ncol, D, sh.alanes), bf), "B": S((sh.nrow, D, sh.blanes), bf), "C": S((DD, 4 * DD + DFF), bf), "D": S((DD, DFF), bf)}
+    out = [out[m] for m in sorted({m[0] for m in mats})]
     return pl.pallas_call(
-        functools.partial(gather_kernel, nrow, ncol),
-        in_specs=[anyspec] * 4, out_specs=[anyspec] * 4,
-        out_shape=[S((ncol, D, sh.alanes), bf), S((nrow, D, sh.blanes), bf), S((DD, 4 * DD + DFF), bf), S((DD, DFF), bf)],
-        scratch_shapes=[sem((4, half)), sem((4, half)), sem((4, half)), sem((4, half)), sem((4,))],
+        functools.partial(gather_kernel, sh, mats),
+        in_specs=[anyspec] * len(out), out_specs=[anyspec] * len(out), out_shape=out,
+        scratch_shapes=[sem((sh.half,))] * (4 * len(mats)) + [sem((len(mats),))],
         compiler_params=pltpu.CompilerParams(collective_id=0, has_side_effects=True),
         name="gather_weights",
-    )(ain, bin_, cin, din)
-
-
-RSTREAMS = (("A",), ("B", "C", "D", "E"))
-
-
-def reduce_kernel(nrow, ncol, da, db, dc, dd, de, loss,
-                  ga, gb, gc, gd, eall, *scratch):
-    mats = "ABCDE"
-    acc, sib, rq, rp, rz = (dict(zip(mats, scratch[5 * t : 5 * t + 5])) for t in range(5))
-    ge, lsem, csend, crecv, send, qrecv, prec, zrecv, esend, erecv, ecs, ecr = scratch[25:]
-    place = Place(nrow, ncol)
-    sh = Shapes(nrow, ncol)
-    nz = place.n["z"]
-    ins = {"A": da, "B": db, "C": dc, "D": dd, "E": de}
-    outs = {"A": ga, "B": gb, "C": gc, "D": gd}
+    )(*blocks)
+
+
+def reduce_kernel(sh, mats, *refs):
+    refs = list(refs)
+
+    def take(names):
+        return {m: refs.pop(0) for m in names}
+    whole = sorted({m[0] for m in mats})
+    ins = take(whole)
+    aux = refs.pop(0)
+    outs = take([m for m in whole if m != "E"])
+    eall = refs.pop(0)
+    acc, sib, rc, rb, ra = (take(mats) for _ in range(5))
+    csend, crecv, send, recv = (take(mats) for _ in range(4))
+    ge, lsem, erecv, ecr = refs
+    place = Place(sh.nrow, sh.ncol)
 
     def spot(m, row, col):
-        if m == "A":
-            return da.at[pl.ds(pl.multiple_of(row * sh.arows, 16), sh.arows), pl.ds(pl.multiple_of(sh.start("A", col), 128), sh.alanes)]
-        if m == "B":
-            return db.at[pl.ds(pl.multiple_of(col * sh.brows, 16), sh.brows), pl.ds(pl.multiple_of(sh.start("B", row), 128), sh.blanes)]
-        if m == "C":
-            return dc.at[pl.ds(pl.multiple_of(row * sh.crows, 16), sh.crows), pl.ds(pl.multiple_of(col * sh.clanes, 128), sh.clanes)]
-        if m == "D":
-            return dd.at[pl.ds(pl.multiple_of(col * sh.drows, 16), sh.drows), pl.ds(pl.multiple_of(row * sh.dlanes, 128), sh.dlanes)]
-        return de.at[row * ncol + col]
+        return block_at(sh, m, ins[m[0]], row, col, False)
 
     place.greet()
-
-    def remote(src, dst, ssem, rsem, **by):
-        return pltpu.make_async_remote_copy(src, dst, ssem, rsem, device_id=place.moved(**by), device_id_type=pl.DeviceIdType.MESH)
-
-    steps = []
-    for s in (0, 1):
-        p, q = ORDER[s]
-        for i in range(place.n[q]):
-            for j in range(place.n[p]):
-                for k in range(nz):
-                    steps.append(((place.n[q] - 1 - i) + (place.n[p] - 1 - j) + (nz - 1 - k), s, i, j, k))
-    steps.sort()
+    steps = sh.steps(mats, True)
     sent = []
-    loads = {}
-    for _, s, i, j, k in steps:
-        p, q = ORDER[s]
-        slot = (i * place.n[p] + j) * nz + k
-        for m in RSTREAMS[s]:
-            mi = mats.index(m)
-            c = remote(spot(m, *place.moved(**{q: -i, p: -j, "z": -k, "core": 1})), sib[m].at[slot], csend.at[mi, slot], crecv.at[mi, slot], core=1)
-            c.start()
-            sent.append(c)
-            loads[m, slot] = pltpu.make_async_copy(spot(m, *place.moved(**{q: -i, p: -j, "z": -k})), acc[m].at[slot], lsem.at[mi, slot])
-            loads[m, slot].start()
-    for _, s, i, j, k in steps:
-        p, q = ORDER[s]
-        npp, nq = place.n[p], place.n[q]
-        slot = (i * npp + j) * nz + k
-        for m in RSTREAMS[s]:
-            mi = mats.index(m)
-            loads[m, slot].wait()
-            remote(sib[m].at[slot], sib[m].at[slot], csend.at[mi, slot], crecv.at[mi, slot], core=1).wait_recv()
-            terms = [(acc[m], slot), (sib[m], slot)]
-            if i < nq - 1:
-                remote(rq[m].at[slot], rq[m].at[slot], send.at[mi, slot], qrecv.at[mi, slot], core=1).wait_recv()
-                terms.append((rq[m], slot))
-            if i == 0 and j < npp - 1:
-                remote(rp[m].at[slot], rp[m].at[slot], send.at[mi, slot], prec.at[mi, slot], core=1).wait_recv()
-                terms.append((rp[m], slot))
-            if i == j == 0 and k < nz - 1:
-                remote(rz[m].at[slot], rz[m].at[slot], send.at[mi, slot], zrecv.at[mi, slot], core=1).wait_recv()
-                terms.append((rz[m], slot))
-            last = i == j == k == 0
-            total = acc[m].shape[1]
-            size = 8 if m == "E" else 16
-
-            def add(r, m=m, terms=terms, last=last, slot=slot):
-                v = terms[0][0][slot, r, :].astype(f32)
-                for ref, at in terms[1:]:
-                    v = v + ref[at, r, :].astype(f32)
-                if not last:
-                    acc[m][slot, r, :] = v.astype(acc[m].dtype)
-                elif m == "E":
-                    ge[pl.ds(0, total), :] = v
-                else:
-                    outs[m][r, :] = v
-            if m == "E":
-                add(slice(None))
+    for m, i, j, k in steps:
+        (a, b, c), _ = sh.axes(m)
+        slot, _ = sh.onward(m, i, j, k)
+        by = {c: -i, b: -j, a: -k}
+        copy = place.remote(spot(m, *place.moved(core=1, **by)), sib[m].at[slot], csend[m].at[slot], crecv[m].at[slot], core=1)
+        copy.start()
+        sent.append((m, copy))
+        pltpu.make_async_copy(spot(m, *place.moved(**by)), acc[m].at[slot], lsem.at[mats.index(m)]).start()
+    for m in mats:
+        pltpu.make_async_copy(acc[m], acc[m], lsem.at[mats.index(m)]).wait()
+    for m, i, j, k in steps:
+        (a, b, c), (na, nb, nc) = sh.axes(m)
+        slot, onward = sh.onward(m, i, j, k)
+        place.remote(sib[m].at[slot], sib[m].at[slot], csend[m].at[slot], crecv[m].at[slot], core=1).wait_recv()
+        terms = [(sib[m], slot)]
+        for axis, far, from_slot in onward:
+            buf = {a: ra, b: rb, c: rc}[axis][m]
+            here = from_slot - {a: 1, b: na, c: na * nb}[axis]
+            place.remote(buf.at[here], buf.at[here], send[m].at[slot], recv[m].at[from_slot], core=1).wait_recv()
+            terms.append((buf, here))
+        last = i == j == k == 0
+        total, lanes = sh.blocks[m]
+
+        def add(r, m=m, terms=terms, last=last, slot=slot):
+            v = acc[m][slot, r, :].astype(f32)
+            for ref, here in terms:
+                v = v + ref[here, r, :].astype(f32)
+            if not last:
+                acc[m][slot, r, :] = v.astype(acc[m].dtype)
+            elif m == "E":
+                ge[r, :] = v
+            elif m == "A1":
+                outs["A"][pl.ds(pl.multiple_of(r.start + sh.acut, 16), r.size), :] = v
             else:
-                rows(total, size, add)
-            if last:
-                continue
-            if i > 0:
-                c = remote(acc[m].at[slot], rq[m].at[slot - npp * nz], send.at[mi, slot], qrecv.at[mi, slot - npp * nz], **{q: -1})
-            elif j > 0:
-                c = remote(acc[m].at[slot], rp[m].at[slot - nz], send.at[mi, slot], prec.at[mi, slot - nz], **{p: -1})
-            else:
-                c = remote(acc[m].at[slot], rz[m].at[slot - 1], send.at[mi, slot], zrecv.at[mi, slot - 1], z=-1)
-            c.start()
-            sent.append(c)
-
+                outs[m[0]][r, :] = v
+        rows(total, 8 if m == "E" else (32 if total % 32 == 0 else 16), add)
+        if last:
+            continue
+        if i > 0:
+            axis, buf, there = c, rc, slot - na * nb
+        elif j > 0:
+            axis, buf, there = b, rb, slot - na
+        else:
+            axis, buf, there = a, ra, slot - 1
+        far = k if m in DIRECT and buf is ra else 1
+        copy = place.remote(acc[m].at[slot], buf[m].at[there], send[m].at[slot], recv[m].at[slot], **{axis: -far})
+        copy.start()
+        sent.append((m, copy))
 
     row, col = place.moved()
     la = lax.broadcasted_iota(jnp.int32, (1, sh.alanes), 1) + (sh.start("A", col) - col * sh.awide)
     lb = lax.broadcasted_iota(jnp.int32, (1, sh.blanes), 1) + (sh.start("B", row) - row * sh.bwide)
-    va = jnp.where((la >= 0) & (la < sh.awide), ga[...], 0.0)
-    vb = jnp.where((lb >= 0) & (lb < sh.bwide), gb[...], 0.0)
     er = sh.erows
     sq = jnp.zeros((1, 128), f32)
-    for v in (va, vb, gc[...], gd[...], ge[0:er, :]):
+    values = [ge[0:er, :]]
+    for m, ref in outs.items():
+        v = ref[...]
+        if m == "A":
+            v = jnp.where((la >= 0) & (la < sh.awide), v, 0.0)
+        if m == "B":
+            v = jnp.where((lb >= 0) & (lb < sh.bwide), v, 0.0)
+        values.append(v)
+    for v in values:
         w = rsum(v * v)
         for c0 in range(0, w.shape[1], 128):
             sq = sq + w[:, c0 : c0 + 128]
-    ge[er : er + 8, :] = jnp.concatenate([jnp.broadcast_to(sq, (8, 128)), jnp.broadcast_to(loss[...], (8, 128))], axis=1)
-
-    def espot(**by):
-        r, c = place.moved(**by)
-        return eall.at[r * ncol + c]
-
-    eall[row * ncol + col] = ge[...]
-    npp, nq = place.n["x"], place.n["y"]
-    esteps = sorted((i + j + k, k, i, j) for i in range(nq) for j in range(npp) for k in range(nz))
-    late = []
-    for _, k, i, j in esteps:
-        slot = (i * npp + j) * nz + k
-        own = i == j == k == 0
-        dst = espot(y=-i, x=-j, z=-k)
-        src = ge if own else dst
-        if not own:
-            remote(dst, dst, esend.at[slot], erecv.at[slot], core=1).wait_recv()
-        plan = []
-        if i == j == 0 and k < nz - 1:
-            plan.append(({"z": 1}, slot + 1))
-        if i == 0 and j < npp - 1:
-            plan.append(({"x": 1}, slot + nz))
-        if i < nq - 1:
-            plan.append(({"y": 1}, slot + nz * npp))
-        for by, there in plan:
-            c = remote(src, dst, esend.at[there], erecv.at[there], **by)
-            c.start()
-            sent.append(c)
-        c = remote(src, dst, ecs.at[slot], ecr.at[slot], core=1)
-        c.start()
-        sent.append(c)
-        other = espot(y=-i, x=-j, z=-k, core=1)
-        late.append(remote(other, other, ecs.at[slot], ecr.at[slot], core=1))
-    for c in late:
-        c.wait_recv()
-    for c in sent:
-        c.wait_send()
-
-
-def reduce_grads(nrow, ncol, da, db, dc, dd, de, loss):
-    sh = Shapes(nrow, ncol)
-    half = nrow * ncol // 2
-    side = math.isqrt(nrow)
-    n = {"x": side, "y": nrow // side, "z": ncol // 2}
+    ge[er : er + 8, :] = jnp.concatenate([jnp.broadcast_to(sq, (8, 128)), jnp.broadcast_to(aux[...], (8, 128))], axis=1)
+    eall[row * sh.ncol + col] = ge[...]
+    for m, copy in sent:
+        copy.wait_send()
+    one = lambda v: {"E": v}
+    spread(place, sh, ["E"], lambda m: ge, lambda m, r, c: eall.at[r * sh.ncol + c], one(send["E"]), one(erecv), one(csend["E"]), one(ecr))
+
+
+def reduce_grads(sh, mats, aux, *grads):
     S = jax.ShapeDtypeStruct
     V = pltpu.VMEM
     anyspec = pl.BlockSpec(memory_space=pl.ANY)
     vm = pl.BlockSpec(memory_space=pltpu.VMEM)
     sem = pltpu.SemaphoreType.DMA
-    kinds = [sh.blocks[m] + (bf,) for m in "ABCD"] + [(sh.erows, 256, f32)]
-    order = [ORDER[s] for s in (0, 1, 1, 1, 1)]
-    nz = n["z"]
+    whole = [m for m in sorted({m[0] for m in mats}) if m != "E"]
+    outs = {"A": (sh.arows, sh.alanes)} | {m: sh.blocks[m] for m in "BCD"}
     scratch = []
     for count in (
-        lambda p, q: half, lambda p, q: half, lambda p, q: (n[q] - 1) * n[p] * nz,
-        lambda p, q: (n[p] - 1) * nz, lambda p, q: nz - 1,
+        lambda na, nb, nc: na * nb * nc, lambda na, nb, nc: na * nb * nc, lambda na, nb, nc: (nc - 1) * nb * na,
+        lambda na, nb, nc: (nb - 1) * na, lambda na, nb, nc: na - 1,
     ):
-        scratch += [V((count(p, q), r, l), t) for (r, l, t), (p, q) in zip(kinds, order)]
-    scratch += [V((sh.erows + 8, 256), f32)]
-    big = n["x"] * n["y"] * nz - min(n["x"], n["y"]) * nz
-    scratch += [sem((5, half))] * 4 + [sem((5, big)), sem((5, max(n["x"], n["y"]) * nz)), sem((5, nz))] + [sem((half,))] * 4
+        scratch += [V((count(*sh.axes(m)[1]),) + sh.blocks[m], f32 if m == "E" else bf) for m in mats]
+    scratch += [sem((sh.half,))] * (4 * len(mats))
+    scratch += [V((sh.erows + 8, 256), f32), sem((len(mats),)), sem((sh.half,)), sem((sh.half,))]
     return pl.pallas_call(
-        functools.partial(reduce_kernel, nrow, ncol),
-        in_specs=[anyspec] * 5 + [vm], out_specs=[vm] * 5,
-        out_shape=[S(sh.blocks[m], f32) for m in "ABCD"] + [S((nrow * ncol, sh.erows + 8, 256), f32)],
+        functools.partial(reduce_kernel, sh, mats),
+        in_specs=[anyspec] * (len(whole) + 1) + [vm], out_specs=[vm] * (len(whole) + 1),
+        out_shape=[S(outs[m], f32) for m in whole] + [S((sh.nrow * sh.ncol, sh.erows + 8, 256), f32)],
         scratch_shapes=scratch,
         compiler_params=pltpu.CompilerParams(collective_id=1, has_side_effects=True, vmem_limit_bytes=60 << 20),
         name="reduce_grads",
-    )(da, db, dc, dd, de, loss)
-
-
-def windows(nrow, ncol, weights):
-    sh = Shapes(nrow, ncol)
+    )(*grads, aux)
+
+
+def windows(sh, weights):
     row, col = lax.axis_index("row"), lax.axis_index("col")
 
     def put(v, which, index, wide, lanes):
@@ -677,15 +664,8 @@
     return put(a, "A", col, sh.awide, sh.alanes), put(b.T, "B", row, sh.bwide, sh.blanes), c, d.T
 
 
-def unwindow(nrow, ncol, ga, gb, gc, gd):
-    sh = Shapes(nrow, ncol)
-    row, col = lax.axis_index("row"), lax.axis_index("col")
-
-    def take(v, which, index, wide, lanes):
-        if wide == lanes:
-            return v
-        return lax.dynamic_slice(v, (0, index * wide - sh.start(which, index)), (v.shape[0], wide))
-    return take(ga, "A", col, sh.awide, sh.alanes), take(gb, "B", row, sh.bwide, sh.blanes).T, gc, gd.T
+GATHERED = ["A0", "A1", "B", "C", "D"]
+REDUCED = ["A0", "A1", "B", "C", "D", "E"]
 
 
 def tile_plan(sh, which):
@@ -742,7 +722,7 @@
 O_Q, O_P, O_F, O_E = D, 4 * D, 5 * D, 5 * D + FF
 
 
-def enc_fwd_kernel(sh, pix, keepc, pos3, sv, awin, bwin,
+def enc_fwd_kernel(sh, pix, keep, pos3, sv, awin, bwin,
                    y, kept, xh1, xh2, xhf, rs1, rs2, rsf, a1, a2, e16, o, qkv, p, hid, gp, x, bias, win, wout, atmp, btmp, asem, bsem):
     enda = joiner(sh, "A", awin, win, atmp, asem)
     endb = joiner(sh, "B", bwin, wout, btmp, bsem)
@@ -750,21 +730,20 @@
     M = n * ES
     R = M // 2
     W = D
+    kind = lax.rem(lax.broadcasted_iota(jnp.int32, (EG, 1), 0), ES)
     for i in range(0, n, 2):
         two = []
         for b in (i, i + 1):
-            kc = keepc[b * ES : (b + 1) * ES, :]
-            pick = (kc == lax.broadcasted_iota(jnp.int32, (ES, DS), 1)).astype(f32).astype(bf)
-            two.append(nn(pick, pix[b]))
+            pick = (keep[b] == lax.broadcasted_iota(jnp.int32, (PATCHES, ES), 0)).astype(f32).astype(bf)
+            two.append(dg(pick, pix[b], 0, 0))
+            at = pos3[0:PATCHES, :], pos3[DS : DS + PATCHES, :], pos3[2 * DS : 2 * DS + PATCHES, :]
+            x[b * ES : (b + 1) * ES, :] = dg(pick, at[0], 0, 0) + dg(pick, at[1], 0, 0) + dg(pick, at[2], 0, 0)
         kept[i * ES : (i + 2) * ES, :] = jnp.concatenate(two, axis=0).astype(bf)
     enda()
     for lo in range(0, M, EG):
         sl = slice(lo, lo + EG)
-        kc = keepc[sl, :]
-        pick = (kc == lax.broadcasted_iota(jnp.int32, (EG, DS), 1)).astype(f32).astype(bf)
-        v = nn(kept[sl, :], win[:, 0:W]) + part(sv, 10)
-        v = v + nn(pick, pos3[0:DS, :]) + nn(pick, pos3[DS : 2 * DS, :]) + nn(pick, pos3[2 * DS :, :])
-        x[sl, :] = jnp.where(kc < PATCHES, v, jnp.where(kc == NOROW - 1, part(sv, 11), 0.0))
+        v = x[sl, :] + nn(kept[sl, :], win[:, 0:W]) + part(sv, 10)
+        x[sl, :] = jnp.where(kind < KEEP, v, jnp.where(kind == KEEP, part(sv, 11), 0.0))
 
     def ln1(r):
         xh, rs, a = norm_rows(x[r, :], part(sv, 0), part(sv, 1))
@@ -819,7 +798,7 @@
     return [pl.BlockSpec(memory_space=pltpu.VMEM)] * k
 
 
-def encoder_fwd(sh, pix, keepc, pos3, sv, awin, bwin):
+def encoder_fwd(sh, pix, keep, pos3, sv, awin, bwin):
     n = pix.shape[0]
     M = n * ES
     S = jax.ShapeDtypeStruct
@@ -833,11 +812,11 @@
         scratch_shapes=[V((M, D), f32), V((EG, EG), f32)] + joiner_scratch(sh),
         compiler_params=pltpu.CompilerParams(vmem_limit_bytes=60 << 20),
         name="encoder_fwd",
-    )(pix, keepc, pos3, sv, awin, bwin)
-
-
-def enc_bwd_kernel(sh, dy, keepc, sv, awin, bwin, kept, xh1_in, xh2, xhf_in, rs1, rs2, rsf, a1_in, a2, e16_in, o, qkv, p, hid, gp,
-                   dwin, dwout, dsm, x, t, d16, dh16, stage, xb, ab, sem, lsem, win, wout, atmp, btmp, asem, bsem):
+    )(pix, keep, pos3, sv, awin, bwin)
+
+
+def enc_bwd_kernel(sh, dy, dsm_in, dhw, sv, awin, bwin, kept, xh1_in, xh2, xhf_in, rs1, rs2, rsf, a1_in, a2, e16_in, o, qkv, p, hid, gp,
+                   dwin, dwout, eout, dsm, etail, x, t, d16, dh16, stage, xb, ab, sem, lsem, win, wout, atmp, btmp, asem, bsem):
     def fetch(i, src, dst):
         copy = pltpu.make_async_copy(src, dst, lsem.at[i])
         copy.start()
@@ -849,7 +828,8 @@
     M = dy.shape[0]
     R = M // 2
     W = D
-    dsm[...] = jnp.zeros_like(dsm)
+    dsm[...] = dsm_in[...]
+    head = fetch(4, dhw, eout.at[pl.ds(0, 3 * DD), :])
 
     def save(where, sums):
         for (i, lo), v in zip(where, sums):
@@ -927,31 +907,36 @@
         da = t[r, :]
         xh = xb[r, :]
         dx = x[r, :] + norm_back(da, xh, rs1[r, :], part(sv, 0))
-        kc = keepc[r, :]
-        only = jnp.where(kc < PATCHES, dx, 0.0)
+        kind = lax.rem(lax.broadcasted_iota(jnp.int32, (r.size, 1), 0), ES)
+        only = jnp.where(kind < KEEP, dx, 0.0)
         d16[r, :] = only.astype(bf)
-        return da * xh, da, jnp.where(kc == NOROW - 1, dx, 0.0), only
+        return da * xh, da, jnp.where(kind == KEEP, dx, 0.0), only
     save([(0, 0), (1, 0), (11, 0), (10, 0)], rows_sum(M, R, [W] * 4, ln1b))
     put(dwin, 0, dg(kept[...], d16[...], 0, 0))
-    for c in shots[-2:]:
+    etail[...] = jnp.zeros_like(etail)
+    for i in range(SMALL // 256):
+        etail[i : i + 1, :] = dsm[:, i * 256 : (i + 1) * 256]
+    tail = fetch(5, etail, eout.at[pl.ds(3 * DD, etail.shape[0]), :])
+    for c in shots[-2:] + [head, tail]:
         c.wait()
 
 
-def encoder_bwd(sh, dy, keepc, sv, awin, bwin, saved):
+def encoder_bwd(sh, dy, dsm, dhw, sv, awin, bwin, saved):
     M = dy.shape[0]
+    count = sh.nrow * sh.ncol * sh.erows
     S = jax.ShapeDtypeStruct
     V = pltpu.VMEM
     anyspec = pl.BlockSpec(memory_space=pl.ANY)
     return pl.pallas_call(
         functools.partial(enc_bwd_kernel, sh),
-        in_specs=[anyspec if i in (3, 4, 6, 8, 12, 14) else spec for i, spec in enumerate(vspec(5 + len(saved)))],
-        out_specs=[anyspec, anyspec, pl.BlockSpec(memory_space=pltpu.VMEM)],
-        out_shape=[S((D, 5 * D + FF + DD), bf), S((D, FF), bf), S((1, SMALL), f32)],
-        scratch_shapes=[V((M, D), f32), V((M, D), f32), V((M, D), bf), V((M, FF), bf), V((2, D, D), bf), V((M, D), f32), V((M, D), bf),
-                        pltpu.SemaphoreType.DMA((2,)), pltpu.SemaphoreType.DMA((4,))] + joiner_scratch(sh),
+        in_specs=[anyspec if i in (2, 4, 5, 7, 9, 13, 15) else spec for i, spec in enumerate(vspec(6 + len(saved)))],
+        out_specs=[anyspec] * 3,
+        out_shape=[S((D, 5 * D + FF + DD), bf), S((D, FF), bf), S((count, 256), f32)],
+        scratch_shapes=[V((1, SMALL), f32), V((count - 3 * DD, 256), f32), V((M, D), f32), V((M, D), f32), V((M, D), bf), V((M, FF), bf), V((2, D, D), bf), V((M, D), f32), V((M, D), bf),
+                        pltpu.SemaphoreType.DMA((2,)), pltpu.SemaphoreType.DMA((6,))] + joiner_scratch(sh),
         compiler_params=pltpu.CompilerParams(vmem_limit_bytes=63 << 20),
         name="encoder_bwd",
-    )(dy, keepc, sv, awin, bwin, *saved)
+    )(dy, dsm, dhw, sv, awin, bwin, *saved)
 
 
 def sincos_np(width):
@@ -984,6 +969,60 @@
     return (weight, first, second)
 
 
+def update_kernel(sh, ga, gb, gc, gd, eall, *refs):
+    weights, firsts, seconds = refs[0:6], refs[6:12], refs[12:18]
+    new, mo, vo = refs[18:24], refs[24:30], refs[30:36]
+    result, e2d = refs[36], refs[37]
+    er = sh.erows
+    row, col = lax.axis_index("row"), lax.axis_index("col")
+    squares = jnp.zeros((1, 128), f32)
+    losses = jnp.zeros((1, 128), f32)
+    for i in range(sh.nrow * sh.ncol):
+        e2d[i * er : (i + 1) * er, :] = eall[i, 0:er, :]
+        squares = squares + eall[i, er : er + 1, 0:128]
+        losses = losses + eall[i, er : er + 1, 128:256]
+    norm = jnp.sqrt(jnp.sum(squares, axis=1, keepdims=True))
+    factor = 0.0001 / jnp.maximum(norm, 0.0001)
+    result[...] = jnp.where(lax.broadcasted_iota(jnp.int32, (1, 128), 1) == 0, losses, norm)
+
+    def aligned(g, which, index, wide, lanes):
+        if wide == lanes:
+            return g
+        return pltpu.roll(g, lax.rem(lanes - (index * wide - sh.start(which, index)), lanes), 1)[:, 0:wide]
+
+    def apply(i, at, grad):
+        out = adamw(weights[i][at], firsts[i][at], seconds[i][at], grad * factor)
+        new[i][at], mo[i][at], vo[i][at] = out
+
+    every = (slice(None), slice(None))
+    apply(0, every, aligned(ga[...], "A", col, sh.awide, sh.alanes))
+    apply(1, every, aligned(gb[...], "B", row, sh.bwide, sh.blanes))
+    apply(2, every, gc[...])
+    apply(3, every, gd[...])
+    for c in range(0, PIX, 256):
+        apply(4, (slice(None), slice(c, c + 256)), e2d[2 * c : 2 * c + DD, :])
+    for i in range(SMALL // 256):
+        for h in (0, 1):
+            apply(5, (slice(2 * i + h, 2 * i + h + 1), slice(None)), e2d[3 * DD + i : 3 * DD + i + 1, h * 128 : (h + 1) * 128])
+
+
+def update(sh, grads, weights, firsts, seconds):
+    S = jax.ShapeDtypeStruct
+    turn = lambda t: [v.T if i % 6 in (1, 3) else v for i, v in enumerate(t)]
+    flat = lambda t: turn([v.reshape(SMALL // 128, 128) if v.ndim == 1 else v for v in t])
+    state = flat(weights) + flat(firsts) + flat(seconds)
+    outs = pl.pallas_call(
+        functools.partial(update_kernel, sh),
+        in_specs=vspec(5 + 18), out_specs=vspec(19),
+        out_shape=[S(v.shape, f32) for v in state] + [S((1, 128), f32)],
+        scratch_shapes=[pltpu.VMEM((sh.nrow * sh.ncol * sh.erows, 256), f32)],
+        compiler_params=pltpu.CompilerParams(vmem_limit_bytes=60 << 20),
+        name="update",
+    )(*grads, *state)
+    small = lambda v: v.reshape(SMALL) if v.shape == (SMALL // 128, 128) else v
+    return tuple(turn([small(v) for v in outs[:18]])) + (outs[18][0, 0], outs[18][0, 1])
+
+
 def local(pixels, keep_idx, restore, *state):
     weights, firsts, seconds = state[0:6], state[6:12], state[12:18]
     nrow, ncol = lax.axis_size("row"), lax.axis_size("col")
@@ -992,29 +1031,18 @@
     denom = 1.0 * n * nrow * ncol * (PATCHES - KEEP)
 
     dec_pos, enc_pos = tables()
-    pix = jnp.pad(pixels, ((0, 0), (0, DS - PATCHES), (0, 0)))
     fill = lambda count, value: jnp.full((n, count), value, jnp.int32)
-    keepc = jnp.concatenate([keep_idx, fill(1, NOROW - 1), fill(ES - KEEP - 1, NOROW)], axis=1).reshape(n * ES, 1)
+    keep = jnp.concatenate([keep_idx, fill(ES - KEEP, NOROW)], axis=1).reshape(n, 1, ES)
     code = jnp.concatenate([jnp.where(restore < KEEP, restore, 64), fill(1, KEEP), fill(DS - PATCHES - 1, NOROW)], axis=1)
     head, sv = weights[4], weights[5].reshape(1, SMALL)
 
-    aw, bw, c, dt = gather_weights(nrow, ncol, *windows(nrow, ncol, weights[0:4]))
-    y, *saved = encoder_fwd(sh, pix, keepc, jnp.asarray(enc_pos), sv, aw, bw)
-    dy, dc, ddt, dhead, dsm_d, loss = decoder(
-        y.reshape(n, ES, DD), code.reshape(n, DS, 1), code.reshape(n, 1, DS), pix, jnp.asarray(dec_pos), sv, c, dt, head, 1.0 / denom)
-    da, dbt, dsm_e = encoder_bwd(sh, dy.reshape(n * ES, DD), keepc, sv, aw, bw, saved)
-
-    count = nrow * ncol * sh.erows * 256
-    flat = jnp.concatenate([dhead.reshape(-1), (dsm_d + dsm_e).reshape(-1), jnp.zeros((count - DD * PIX - SMALL,), f32)])
-    ga, gb, gc, gd, ge = reduce_grads(nrow, ncol, da, dbt, dc, ddt, flat.reshape(nrow * ncol, sh.erows, 256), loss)
-    flat = ge[:, : sh.erows].reshape(-1)
-    grads = [*unwindow(nrow, ncol, ga, gb, gc, gd), flat[: DD * PIX].reshape(DD, PIX), flat[DD * PIX : DD * PIX + SMALL]]
-    aux = jnp.sum(ge[:, sh.erows], axis=0)
-    norm = jnp.sqrt(jnp.sum(aux[:128]))
-    loss = aux[128]
-    factor = 0.0001 / jnp.maximum(norm, 0.0001)
-    done = [adamw(w, m, v, g * factor) for w, m, v, g in zip(weights, firsts, seconds, grads)]
-    return tuple(d[0] for d in done) + tuple(d[1] for d in done) + tuple(d[2] for d in done) + (loss, norm)
+    aw, bw, c, dt = gather_weights(sh, GATHERED, *windows(sh, weights[0:4]))
+    y, *saved = encoder_fwd(sh, pixels, keep, jnp.asarray(enc_pos), sv, aw, bw)
+    dy, dc, ddt, dhead, dsm, loss = decoder(
+        y.reshape(n, ES, DD), code.reshape(n, 1, DS), pixels, jnp.asarray(dec_pos), sv, c, dt, head, 1.0 / denom)
+    da, dbt, shared = encoder_bwd(sh, dy.reshape(n * ES, DD), dsm, dhead, sv, aw, bw, saved)
+    sums = reduce_grads(sh, REDUCED, loss, da, dbt, dc, ddt, shared.reshape(nrow * ncol, sh.erows, 256))
+    return update(sh, sums, weights, firsts, seconds)
 
 
 def solution(mesh):

time: 573 us -> 537 us (0.937)
  Pallas kernels: 528 us -> 512 us
  other arithmetic: 18.8 us -> 6.71 us
  local copies, waits for them, and re-layouts: 18.8 us -> 7.97 us
    pallas_call x2 -> x3, Pallas kernels: 247 us -> 228 us  [the longest x1 121 us: reduce_grads(): pl.pallas_call(functools.partial(reduce_kernel, sh, mats), in_specs=[anys...]
    pallas_call x1, Pallas kernels: 163 us -> 177 us  [decoder(): pl.pallas_call(functools.partial(dec_kernel, scale, nb), grid=(n // nb,),...]
    sub x6 -> x0, other arithmetic: 11.1 us -> none  [adamw(): weight - 0.08 * (first_hat / (jnp.sqrt(second_hat) + 1e-08) + 0.05 * weight)]
    pallas_call x1, Pallas kernels: 56.4 us -> 46 us  [encoder_fwd(): pl.pallas_call(functools.partial(enc_fwd_kernel, sh), in_specs=vspec(4) +...]
where the time goes in v4:
time: 537 us; the launch traced here: 528 us
  Pallas kernels  512 us (95%)
  local copies, waits for them, and re-layouts  7.97 us (1%)
  other arithmetic  6.71 us (1%)
    pallas_call x1, Pallas kernels, decoder(): pl.pallas_call(functools.partial(dec_kernel, scale, nb), grid=(n // nb,),...  177 us
    pallas_call x1, Pallas kernels, reduce_grads(): pl.pallas_call(functools.partial(reduce_kernel, sh, mats), in_specs=[anys...  121 us
    pallas_call x1, Pallas kernels, gather_weights(): pl.pallas_call(functools.partial(gather_kernel, sh, mats), in_specs=[anys...  94.4 us
    pallas_call x1, Pallas kernels, encoder_bwd(): pl.pallas_call(functools.partial(enc_bwd_kernel, sh), in_specs=[anyspec i...  61 us
    pallas_call x1, Pallas kernels, encoder_fwd(): pl.pallas_call(functools.partial(enc_fwd_kernel, sh), in_specs=vspec(4) +...  46 us
    pallas_call x1, Pallas kernels, update(): pl.pallas_call(functools.partial(update_kernel, sh), in_specs=vspec(5 + 1...  12.1 us

profile of v4, /device:TPU:0, one launch (start us, length us, event | category | flops | bytes accessed | tf_op | source)
XLA Modules:
  0.0 527.6 jit_solution(3548288739170952811)
XLA Ops:
  0.7 0.1 pad.3.clone
  0.8 0.1 pad.2.clone
  0.8 0.7 concatenate.6
  1.5 0.6 reshape.76.keep
  2.1 0.7 compare_select_fusion
  2.9 0.6 reshape.79.coder
  3.5 1.5 convert_bitcast_fusion.1.refs_3_
  5.0 1.6 reshape.77.sv
  6.6 1.6 convert_element_type.14.refs_2_
  8.2 1.6 convert_bitcast_fusion.refs_1_
  9.9 1.2 convert_element_type.12
  11.1 2.3 dynamic_update_slice.3.refs_0_
  13.4 0.0 copy-start
  13.4 0.7 copy-done
  14.1 94.4 %gather_weights.1 = (bf16[8,768,1024]{2,1,0:T(8,128)(2,1)}, bf16[4,768,768]{2,1,0:T(8,128)(2,1)}, bf16[512,4096]{1,0:T(8,128)(2,1)}, bf16[512,2048]{1,0:T(8,128)(2,1)}) custom-call(bf16[192,1024]{1,0:T(8,128)(2,1)} %copy-done, bf16[96,768]{1,0:T(8,128)(2,1)} %convert_bitcast_fusion.refs_1_, bf16[128,512]{1,0:T(8,128)(2,1)} %convert_element_type.14.refs_2_, ...), custom_call_target="tpu_custom_call" | custom-call | tf_op jit(solution)/shard_map/gather_weights/pallas_call | solution.py:525
  108.5 46.0 %encoder_fwd.1 = (f32[672,512]{1,0:T(8,128)}, bf16[672,768]{1,0:T(8,128)(2,1)}, f32[672,768]{1,0:T(8,128)}, f32[672,768]{1,0:T(8,128)}, f32[672,768]{1,0:T(8,128...) custom-call(bf16[12,196,768]{2,1,0:T(8,128)(2,1)} %pix.3, ...), custom_call_target="tpu_custom_call" | custom-call | tf_op jit(solution)/shard_map/encoder_fwd/pallas_call | solution.py:809
  154.6 177.1 %decoder.1 = (f32[12,56,512]{2,1,0:T(8,128)}, bf16[512,4096]{1,0:T(8,128)(2,1)}, bf16[512,2048]{1,0:T(8,128)(2,1)}, f32[1536,256]{1,0:T(8,128)}, f32[1,21248]{1,0:T(1,128)}, /*index=5*/f32[1,128]{1,0:T(1,128)}) custom-call(f32[12,56,512]{2,1,0:T(8,128)} %bitcast.29, s32[12,1,208]{2,1,0:T(1,128)} %reshape.79.coder, bf16[12,196,768]{2,1,0:T(8,128)(2,1)} %pix.3, ...), custom_call_target="tpu_custom_call" | custom-call | tf_op jit(solution)/shard_map/decoder/pallas_call | solution.py:333
  331.7 61.0 %encoder_bwd.1 = (bf16[768,7424]{1,0:T(8,128)(2,1)}, bf16[768,3072]{1,0:T(8,128)(2,1)}, f32[1792,256]{1,0:T(8,128)}) custom-call(f32[672,512]{1,0:T(8,128)} %bitcast.30, f32[1,21248]{1,0:T(1,128)} %get-tuple-element.79.dsm_in, f32[1536,256]{1,0:T(8,128)} %get-tuple-element.80.dhw, f32[1,21248]{1,0:T(1,128)} %reshape.77.sv, ...), custom_call_target="tpu_custom_call" | custom-call | tf_op jit(solution)/shard_map/encoder_bwd/pallas_call | solution.py:930
  392.7 121.1 %reduce_grads.1 = (f32[192,1024]{1,0:T(8,128)}, f32[96,768]{1,0:T(8,128)}, f32[128,512]{1,0:T(8,128)}, f32[64,512]{1,0:T(8,128)}, f32[32,64,256]{2,1,0:T(8,128)}) custom-call(bf16[768,7424]{1,0:T(8,128)(2,1)} %get-tuple-element.96.refs_0_, bf16[768,3072]{1,0:T(8,128)(2,1)} %get-tuple-element.97.refs_1_, bf16[512,4096]{1,0:T(8,128)(2,1)} %get-tuple-element.98.refs_2_, ...), custom_call_target="tpu_custom_call" | custom-call | tf_op jit(solution)/shard_map/reduce_grads/pallas_call | solution.py:645
  513.8 12.1 %update.1 = (f32[192,928]{1,0:T(8,128)}, f32[96,768]{1,0:T(8,128)}, f32[128,512]{1,0:T(8,128)}, f32[64,512]{1,0:T(8,128)}, f32[512,768]{1,0:T(8,128)}, /*index=5...) custom-call(f32[192,1024]{1,0:T(8,128)} %get-tuple-element.102.ga, ...), custom_call_target="tpu_custom_call" | custom-call | tf_op jit(solution)/shard_map/update/pallas_call | solution.py:1014
  525.9 1.3 fusion
  (3 shorter events, 0.0 us)
Async XLA Ops:
  13.4 0.7 copy-start

commit v5 on v4

--- a/solution.py
+++ b/solution.py
@@ -382,8 +382,8 @@
 
 
 ORDER = {
-    "A0": ("z", "x", "y"), "A1": ("z", "y", "x"), "B": ("y", "x", "z"),
-    "C": ("z", "x", "y"), "D": ("z", "y", "x"), "E": ("z", "y", "x"),
+    "A0": ("z", "x", "y"), "A1": ("z", "y", "x"), "A2": ("x", "y", "z"), "B": ("z", "y", "x"),
+    "C": ("z", "x", "y"), "D": ("y", "x", "z"), "E": ("z", "y", "x"),
 }
 DIRECT = ("E",)
 
@@ -397,12 +397,13 @@
         self.awide, self.bwide = (5 * D + FF + DD) // ncol, FF // nrow
         self.alanes, self.blanes = self.window(self.awide, ncol), self.window(self.bwide, nrow)
         self.arows, self.brows = D // nrow, D // ncol
-        self.acut = self.arows // 32 * 16
+        cut = [self.arows * t // 12 // 16 * 16 for t in (5, 4)]
+        self.acut = (0, cut[0], cut[0] + cut[1], self.arows)
         self.crows, self.clanes = DD // nrow, (4 * DD + DFF) // ncol
         self.drows, self.dlanes = DD // ncol, DFF // nrow
         self.erows = -(-(DD * PIX + SMALL) // (nrow * ncol * 256 * 8)) * 8
         self.blocks = {
-            "A0": (self.acut, self.alanes), "A1": (self.arows - self.acut, self.alanes), "B": (self.brows, self.blanes),
+            "A0": (cut[0], self.alanes), "A1": (cut[1], self.alanes), "A2": (self.arows - self.acut[2], self.alanes), "B": (self.brows, self.blanes),
             "C": (self.crows, self.clanes), "D": (self.drows, self.dlanes), "E": (self.erows, 256)}
 
     @staticmethod
@@ -420,7 +421,7 @@
     def axes(self, m):
         return ORDER[m], tuple(self.n[a] for a in ORDER[m])
 
-    def steps(self, mats, back):
+    def steps(self, mats, back, keys=False):
         out = []
         for pos, m in enumerate(mats):
             _, (na, nb, nc) = self.axes(m)
@@ -429,7 +430,7 @@
                     for k in range(na):
                         key = (na - 1 - k) + (nb - 1 - j) + (nc - 1 - i) if back else i + j + (min(k, 1) if m in DIRECT else k)
                         out.append((key, pos, m, i, j, k))
-        return [t[2:] for t in sorted(out)]
+        return [t if keys else t[2:] for t in sorted(out)]
 
     def onward(self, m, i, j, k):
         (a, b, c), (na, nb, nc) = self.axes(m)
@@ -446,36 +447,49 @@
         return slot, out
 
 
-def spread(place, sh, mats, first, spot, send, recv, csend, crecv):
-    sent, late = [], []
-    for m, i, j, k in sh.steps(mats, False):
-        (a, b, c), _ = sh.axes(m)
-        slot, onward = sh.onward(m, i, j, k)
+class Spread:
+    def __init__(self, place, sh, first, spot, send, recv, csend, crecv):
+        self.place, self.sh, self.first, self.spot = place, sh, first, spot
+        self.send, self.recv, self.csend, self.crecv = send, recv, csend, crecv
+        self.sent, self.late = [], []
+
+    def step(self, m, i, j, k):
+        place = self.place
+        (a, b, c), _ = self.sh.axes(m)
+        slot, onward = self.sh.onward(m, i, j, k)
         by = {c: -i, b: -j, a: -k}
-        dst = spot(m, *place.moved(**by))
+        dst = self.spot(m, *place.moved(**by))
         own = i == j == k == 0
-        src = first(m) if own else dst
+        src = self.first(m) if own else dst
+        csend, crecv = self.csend[m].at[slot], self.crecv[m].at[slot]
         if not own:
-            place.remote(dst, dst, send[m].at[slot], recv[m].at[slot], core=1).wait_recv()
+            place.remote(dst, dst, self.send[m].at[slot], self.recv[m].at[slot], core=1).wait_recv()
         for axis, far, there in onward:
-            copy = place.remote(src, dst, send[m].at[there], recv[m].at[there], **{axis: far})
+            copy = place.remote(src, dst, self.send[m].at[there], self.recv[m].at[there], **{axis: far})
             copy.start()
-            sent.append(copy)
-        copy = place.remote(src, dst, csend[m].at[slot], crecv[m].at[slot], core=1)
+            self.sent.append(copy)
+        copy = place.remote(src, dst, csend, crecv, core=1)
         copy.start()
-        sent.append(copy)
-        other = spot(m, *place.moved(core=1, **by))
-        late.append(place.remote(other, other, csend[m].at[slot], crecv[m].at[slot], core=1))
-    for copy in late:
-        copy.wait_recv()
-    for copy in sent:
-        copy.wait_send()
+        self.sent.append(copy)
+        other = self.spot(m, *place.moved(core=1, **by))
+        self.late.append((m, place.remote(other, other, csend, crecv, core=1)))
+
+    def arrived(self, which):
+        for m, copy in self.late:
+            if m[0] in which:
+                copy.wait_recv()
+        self.late = [t for t in self.late if t[0][0] not in which]
+
+    def end(self):
+        self.arrived("ABCDE")
+        for copy in self.sent:
+            copy.wait_send()
 
 
 def block_at(sh, m, ref, row, col, gathered):
     mul = pl.multiple_of
-    if m in ("A0", "A1"):
-        skip = 0 if m == "A0" else sh.acut
+    if m[0] == "A":
+        skip = sh.acut[int(m[1])]
         r = pl.ds(mul(row * sh.arows + skip, 16), sh.blocks[m][0])
         return ref.at[col, r, :] if gathered else ref.at[r, pl.ds(mul(sh.start("A", col), 128), sh.alanes)]
     if m == "B":
@@ -488,12 +502,8 @@
     return ref.at[row * sh.ncol + col]
 
 
-def gather_kernel(sh, mats, *refs):
+def start_gather(sh, mats, ins, outs, sems):
     place = Place(sh.nrow, sh.ncol)
-    whole = sorted({m[0] for m in mats})
-    n = len(whole)
-    ins, outs = dict(zip(whole, refs[:n])), dict(zip(whole, refs[n : 2 * n]))
-    sems = refs[2 * n :]
     send, recv, csend, crecv = (dict(zip(mats, sems[t * len(mats) :])) for t in range(4))
     lsem = sems[4 * len(mats)]
 
@@ -501,34 +511,15 @@
         return block_at(sh, m, outs[m[0]], row, col, True)
 
     def first(m):
-        if m == "A0":
-            return ins["A"].at[pl.ds(0, sh.acut), :]
-        if m == "A1":
-            return ins["A"].at[pl.ds(sh.acut, sh.arows - sh.acut), :]
+        if m[0] == "A":
+            return ins["A"].at[pl.ds(sh.acut[int(m[1])], sh.blocks[m][0]), :]
         return ins[m]
 
     place.greet()
     own = [pltpu.make_async_copy(first(m), spot(m, *place.moved()), lsem.at[i]) for i, m in enumerate(mats)]
     for copy in own:
         copy.start()
-    spread(place, sh, mats, first, spot, send, recv, csend, crecv)
-    for copy in own:
-        copy.wait()
-
-
-def gather_weights(sh, mats, *blocks):
-    S = jax.ShapeDtypeStruct
-    anyspec = pl.BlockSpec(memory_space=pl.ANY)
-    sem = pltpu.SemaphoreType.DMA
-    out = {"A": S((sh.ncol, D, sh.alanes), bf), "B": S((sh.nrow, D, sh.blanes), bf), "C": S((DD, 4 * DD + DFF), bf), "D": S((DD, DFF), bf)}
-    out = [out[m] for m in sorted({m[0] for m in mats})]
-    return pl.pallas_call(
-        functools.partial(gather_kernel, sh, mats),
-        in_specs=[anyspec] * len(out), out_specs=[anyspec] * len(out), out_shape=out,
-        scratch_shapes=[sem((sh.half,))] * (4 * len(mats)) + [sem((len(mats),))],
-        compiler_params=pltpu.CompilerParams(collective_id=0, has_side_effects=True),
-        name="gather_weights",
-    )(*blocks)
+    return Spread(place, sh, first, spot, send, recv, csend, crecv), dict(zip(mats, own))
 
 
 def reduce_kernel(sh, mats, *refs):
@@ -556,16 +547,15 @@
         (a, b, c), _ = sh.axes(m)
         slot, _ = sh.onward(m, i, j, k)
         by = {c: -i, b: -j, a: -k}
-        copy = place.remote(spot(m, *place.moved(core=1, **by)), sib[m].at[slot], csend[m].at[slot], crecv[m].at[slot], core=1)
+        copy = place.remote(spot(m, *place.moved(core=1, **by)), sib[m].at[slot], csend[m].at[0], crecv[m].at[slot], core=1)
         copy.start()
-        sent.append((m, copy))
         pltpu.make_async_copy(spot(m, *place.moved(**by)), acc[m].at[slot], lsem.at[mats.index(m)]).start()
     for m in mats:
         pltpu.make_async_copy(acc[m], acc[m], lsem.at[mats.index(m)]).wait()
     for m, i, j, k in steps:
         (a, b, c), (na, nb, nc) = sh.axes(m)
         slot, onward = sh.onward(m, i, j, k)
-        place.remote(sib[m].at[slot], sib[m].at[slot], csend[m].at[slot], crecv[m].at[slot], core=1).wait_recv()
+        place.remote(sib[m].at[slot], sib[m].at[slot], csend[m].at[0], crecv[m].at[slot], core=1).wait_recv()
         terms = [(sib[m], slot)]
         for axis, far, from_slot in onward:
             buf = {a: ra, b: rb, c: rc}[axis][m]
@@ -583,11 +573,11 @@
                 acc[m][slot, r, :] = v.astype(acc[m].dtype)
             elif m == "E":
                 ge[r, :] = v
-            elif m == "A1":
-                outs["A"][pl.ds(pl.multiple_of(r.start + sh.acut, 16), r.size), :] = v
+            elif m[0] == "A":
+                outs["A"][pl.ds(pl.multiple_of(r.start + sh.acut[int(m[1])], 16), r.size), :] = v
             else:
                 outs[m[0]][r, :] = v
-        rows(total, 8 if m == "E" else (32 if total % 32 == 0 else 16), add)
+        rows(total, 8 if m == "E" else (16), add)
         if last:
             continue
         if i > 0:
@@ -622,8 +612,13 @@
     eall[row * sh.ncol + col] = ge[...]
     for m, copy in sent:
         copy.wait_send()
+    for m in mats:
+        place.remote(sib[m], sib[m], csend[m].at[0], crecv[m].at[0], core=1).wait_send()
     one = lambda v: {"E": v}
-    spread(place, sh, ["E"], lambda m: ge, lambda m, r, c: eall.at[r * sh.ncol + c], one(send["E"]), one(erecv), one(csend["E"]), one(ecr))
+    run = Spread(place, sh, lambda m: ge, lambda m, r, c: eall.at[r * sh.ncol + c], one(send["E"]), one(erecv), one(csend["E"]), one(ecr))
+    for step in sh.steps(["E"], False):
+        run.step(*step)
+    run.end()
 
 
 def reduce_grads(sh, mats, aux, *grads):
@@ -640,7 +635,7 @@
         lambda na, nb, nc: (nb - 1) * na, lambda na, nb, nc: na - 1,
     ):
         scratch += [V((count(*sh.axes(m)[1]),) + sh.blocks[m], f32 if m == "E" else bf) for m in mats]
-    scratch += [sem((sh.half,))] * (4 * len(mats))
+    scratch += [sem((sh.half if m == "E" else 1,)) for m in mats] + [sem((sh.half,))] * (3 * len(mats))
     scratch += [V((sh.erows + 8, 256), f32), sem((len(mats),)), sem((sh.half,)), sem((sh.half,))]
     return pl.pallas_call(
         functools.partial(reduce_kernel, sh, mats),
@@ -664,8 +659,8 @@
     return put(a, "A", col, sh.awide, sh.alanes), put(b.T, "B", row, sh.bwide, sh.blanes), c, d.T
 
 
-GATHERED = ["A0", "A1", "B", "C", "D"]
-REDUCED = ["A0", "A1", "B", "C", "D", "E"]
+GATHERED = ["A0", "A1", "A2", "B", "C", "D"]
+REDUCED = ["A0", "A1", "A2", "B", "C", "D", "E"]
 
 
 def tile_plan(sh, which):
@@ -722,14 +717,18 @@
 O_Q, O_P, O_F, O_E = D, 4 * D, 5 * D, 5 * D + FF
 
 
-def enc_fwd_kernel(sh, pix, keep, pos3, sv, awin, bwin,
-                   y, kept, xh1, xh2, xhf, rs1, rs2, rsf, a1, a2, e16, o, qkv, p, hid, gp, x, bias, win, wout, atmp, btmp, asem, bsem):
-    enda = joiner(sh, "A", awin, win, atmp, asem)
-    endb = joiner(sh, "B", bwin, wout, btmp, bsem)
+def enc_fwd_kernel(sh, pix, keep, pos3, sv, ain, bin_, cin, din,
+                   y, kept, xh1, xh2, xhf, rs1, rs2, rsf, a1, a2, e16, o, qkv, p, hid, gp, awin, bwin, cout, dout,
+                   x, bias, win, wout, atmp, btmp, asem, bsem, *sems):
     n = pix.shape[0]
     M = n * ES
     R = M // 2
     W = D
+    run, own = start_gather(sh, GATHERED, dict(zip("ABCD", (ain, bin_, cin, din))), dict(zip("ABCD", (awin, bwin, cout, dout))), sems)
+    ahead = sh.steps(["A0", "A1", "A2", "B"], False)
+    for step in ahead[:4]:
+        run.step(*step)
+
     kind = lax.rem(lax.broadcasted_iota(jnp.int32, (EG, 1), 0), ES)
     for i in range(0, n, 2):
         two = []
@@ -739,11 +738,35 @@
             at = pos3[0:PATCHES, :], pos3[DS : DS + PATCHES, :], pos3[2 * DS : 2 * DS + PATCHES, :]
             x[b * ES : (b + 1) * ES, :] = dg(pick, at[0], 0, 0) + dg(pick, at[1], 0, 0) + dg(pick, at[2], 0, 0)
         kept[i * ES : (i + 2) * ES, :] = jnp.concatenate(two, axis=0).astype(bf)
+    ki = lax.broadcasted_iota(jnp.int32, (EG, EG), 0)
+    qi = lax.broadcasted_iota(jnp.int32, (EG, EG), 1)
+    same = jnp.zeros((EG, EG), jnp.bool_)
+    for j in range(4):
+        same = same | ((ki >= j * ES) & (ki < j * ES + KEEP + 1) & (qi >= j * ES) & (qi < (j + 1) * ES))
+    bias[...] = jnp.where(same, 0.0, -1e30).astype(f32)
+    for step in ahead[4:]:
+        run.step(*step)
+
+    todo = sh.steps(["C", "D"], False)
+    each = -(-len(todo) // 32)
+
+    def tick(count=each):
+        for _ in range(min(count, len(todo))):
+            run.step(*todo.pop(0))
+    tick(2)
+    run.arrived("A")
+    for m in ("A0", "A1", "A2"):
+        own[m].wait()
+    enda = joiner(sh, "A", awin, win, atmp, asem)
+    run.arrived("B")
+    own["B"].wait()
+    endb = joiner(sh, "B", bwin, wout, btmp, bsem)
     enda()
     for lo in range(0, M, EG):
         sl = slice(lo, lo + EG)
         v = x[sl, :] + nn(kept[sl, :], win[:, 0:W]) + part(sv, 10)
         x[sl, :] = jnp.where(kind < KEEP, v, jnp.where(kind == KEEP, part(sv, 11), 0.0))
+        tick()
 
     def ln1(r):
         xh, rs, a = norm_rows(x[r, :], part(sv, 0), part(sv, 1))
@@ -751,24 +774,21 @@
         rs1[r, :] = rs
         a1[r, :] = a.astype(bf)
     rows(M, R, ln1)
+    tick()
     qkv[:, 0:W] = (nn(a1[...], win[:, O_Q : O_Q + W]) + sv[:, OFF[2] : OFF[2] + W]).astype(bf)
+    tick()
     qkv[:, W : 2 * W] = nn(a1[...], win[:, O_Q + W : O_Q + 2 * W]).astype(bf)
+    tick()
     qkv[:, 2 * W :] = (nn(a1[...], win[:, O_Q + 2 * W : O_P]) + sv[:, OFF[2] + W : OFF[3]]).astype(bf)
-
-    ki = lax.broadcasted_iota(jnp.int32, (EG, EG), 0)
-    qi = lax.broadcasted_iota(jnp.int32, (EG, EG), 1)
-    same = jnp.zeros((EG, EG), jnp.bool_)
-    for j in range(4):
-        same = same | ((ki >= j * ES) & (ki < j * ES + KEEP + 1) & (qi >= j * ES) & (qi < (j + 1) * ES))
-    bias[...] = jnp.where(same, 0.0, -1e30).astype(f32)
-
-    @pl.loop(0, n // 4)
-    def _(i):
-        rsl = pl.ds(pl.multiple_of(i * EG, 16), EG)
+    tick()
+    for i in range(n // 4):
         for g in range(6):
-            att_fwd(qkv, o, p, bias[...], rsl, W, g, i * 12 + g * 2, 64)
+            att_fwd(qkv, o, p, bias[...], slice(i * EG, (i + 1) * EG), W, g, i * 12 + g * 2, 64)
+            if g % GROUPS == GROUPS - 1:
+                tick(GROUPS * each)
 
     x[...] += nn(o[...], win[:, O_P : O_P + W]) + part(sv, 3)
+    tick()
 
     def ln2(r):
         xh, rs, a = norm_rows(x[r, :], part(sv, 4), part(sv, 5))
@@ -776,14 +796,17 @@
         rs2[r, :] = rs
         a2[r, :] = a.astype(bf)
     rows(M, R, ln2)
+    tick()
 
     for c in range(0, FF, 512):
         h = nn(a2[...], win[:, O_F + c : O_F + c + 512])
         g, dg_ = gelu_pair(h + sv[:, OFF[6] + c : OFF[6] + c + 512])
         hid[:, c : c + 512] = g.astype(bf)
         gp[:, c : c + 512] = dg_.astype(bf)
+        tick()
     endb()
     x[...] += nt(hid[...], wout[...]) + part(sv, 7)
+    tick()
 
     def lnf(r):
         xh, rs, a = norm_rows(x[r, :], part(sv, 8), part(sv, 9))
@@ -791,28 +814,40 @@
         rsf[r, :] = rs
         e16[r, :] = a.astype(bf)
     rows(M, R, lnf)
+    tick()
     y[...] = nn(e16[...], win[:, O_E:]) + part(sv, 12)
+    tick(len(todo))
+    run.end()
+    own["C"].wait()
+    own["D"].wait()
+
+
+GROUPS = 3
 
 
 def vspec(k):
     return [pl.BlockSpec(memory_space=pltpu.VMEM)] * k
 
 
-def encoder_fwd(sh, pix, keep, pos3, sv, awin, bwin):
+def encoder_fwd(sh, pix, keep, pos3, sv, *blocks):
     n = pix.shape[0]
     M = n * ES
     S = jax.ShapeDtypeStruct
     V = pltpu.VMEM
+    sem = pltpu.SemaphoreType.DMA
+    anyspec = pl.BlockSpec(memory_space=pl.ANY)
     outs = [S((M, DD), f32), S((M, D), bf), S((M, D), f32), S((M, D), f32), S((M, D), f32),
             S((M, 1), f32), S((M, 1), f32), S((M, 1), f32), S((M, D), bf), S((M, D), bf), S((M, D), bf), S((M, D), bf),
             S((M, 3 * D), bf), S((n // 4 * HEADS, EG, EG), bf), S((M, FF), bf), S((M, FF), bf)]
-    return pl.pallas_call(
+    weights = [S((sh.ncol, D, sh.alanes), bf), S((sh.nrow, D, sh.blanes), bf), S((DD, 4 * DD + DFF), bf), S((DD, DFF), bf)]
+    out = pl.pallas_call(
         functools.partial(enc_fwd_kernel, sh),
-        in_specs=vspec(4) + [pl.BlockSpec(memory_space=pl.ANY)] * 2, out_specs=vspec(len(outs)), out_shape=outs,
-        scratch_shapes=[V((M, D), f32), V((EG, EG), f32)] + joiner_scratch(sh),
-        compiler_params=pltpu.CompilerParams(vmem_limit_bytes=60 << 20),
+        in_specs=vspec(4) + [anyspec] * 4, out_specs=vspec(len(outs)) + [anyspec] * 4, out_shape=outs + weights,
+        scratch_shapes=[V((M, D), f32), V((EG, EG), f32)] + joiner_scratch(sh) + [sem((sh.half,))] * (4 * len(GATHERED)) + [sem((len(GATHERED),))],
+        compiler_params=pltpu.CompilerParams(vmem_limit_bytes=60 << 20, collective_id=0, has_side_effects=True),
         name="encoder_fwd",
-    )(pix, keep, pos3, sv, awin, bwin)
+    )(pix, keep, pos3, sv, *blocks)
+    return out[0], out[1 : len(outs)], out[len(outs) :]
 
 
 def enc_bwd_kernel(sh, dy, dsm_in, dhw, sv, awin, bwin, kept, xh1_in, xh2, xhf_in, rs1, rs2, rsf, a1_in, a2, e16_in, o, qkv, p, hid, gp,
@@ -1036,8 +1071,7 @@
     code = jnp.concatenate([jnp.where(restore < KEEP, restore, 64), fill(1, KEEP), fill(DS - PATCHES - 1, NOROW)], axis=1)
     head, sv = weights[4], weights[5].reshape(1, SMALL)
 
-    aw, bw, c, dt = gather_weights(sh, GATHERED, *windows(sh, weights[0:4]))
-    y, *saved = encoder_fwd(sh, pixels, keep, jnp.asarray(enc_pos), sv, aw, bw)
+    y, saved, (aw, bw, c, dt) = encoder_fwd(sh, pixels, keep, jnp.asarray(enc_pos), sv, *windows(sh, weights[0:4]))
     dy, dc, ddt, dhead, dsm, loss = decoder(
         y.reshape(n, ES, DD), code.reshape(n, 1, DS), pixels, jnp.asarray(dec_pos), sv, c, dt, head, 1.0 / denom)
     da, dbt, shared = encoder_bwd(sh, dy.reshape(n * ES, DD), dsm, dhead, sv, aw, bw, saved)

time: 537 us -> 507 us (0.944)
  Pallas kernels: 512 us -> 486 us
    pallas_call x1 -> x0, Pallas kernels: 94.4 us -> none  [gather_weights(): pl.pallas_call(functools.partial(gather_kernel, sh, mats), in_specs=[anys...]
    pallas_call x1, Pallas kernels: 46 us -> 133 us  [encoder_fwd(): pl.pallas_call(functools.partial(enc_fwd_kernel, sh), in_specs=vspec(4) +...]
    pallas_call x1, Pallas kernels: 177 us -> 164 us  [decoder(): pl.pallas_call(functools.partial(dec_kernel, scale, nb), grid=(n // nb,),...]
where the time goes in v5:
time: 507 us; the launch traced here: 502 us
  Pallas kernels  486 us (96%)
  local copies, waits for them, and re-layouts  8.05 us (2%)
  other arithmetic  6.71 us (1%)
    pallas_call x1, Pallas kernels, decoder(): pl.pallas_call(functools.partial(dec_kernel, scale, nb), grid=(n // nb,),...  164 us
    pallas_call x1, Pallas kernels, encoder_fwd(): pl.pallas_call(functools.partial(enc_fwd_kernel, sh), in_specs=vspec(4) +...  133 us
    pallas_call x1, Pallas kernels, reduce_grads(): pl.pallas_call(functools.partial(reduce_kernel, sh, mats), in_specs=[anys...  116 us
    pallas_call x1, Pallas kernels, encoder_bwd(): pl.pallas_call(functools.partial(enc_bwd_kernel, sh), in_specs=[anyspec i...  61 us
    pallas_call x1, Pallas kernels, update(): pl.pallas_call(functools.partial(update_kernel, sh), in_specs=vspec(5 + 1...  12.1 us

profile of v5, /device:TPU:0, one launch (start us, length us, event | category | flops | bytes accessed | tf_op | source)
XLA Modules:
  0.0 501.8 jit_solution(1297304631424304826)
XLA Ops:
  0.7 0.1 pad.3.clone
  0.8 0.1 pad.2.clone
  0.8 0.7 concatenate.6
  1.5 0.6 reshape.76.keep
  2.1 0.7 compare_select_fusion
  2.9 0.6 reshape.79.coder
  3.5 1.5 convert_bitcast_fusion.1.din
  5.0 1.6 reshape.77.sv
  6.6 1.6 convert_element_type.14.cin
  8.2 1.6 convert_bitcast_fusion.bin_
  9.9 1.2 convert_element_type.12
  11.1 2.3 dynamic_update_slice.3.ain
  13.4 0.0 copy-start
  13.4 0.7 copy-done
  14.1 132.8 %encoder_fwd.1 = (f32[672,512]{1,0:T(8,128)}, bf16[672,768]{1,0:T(8,128)(2,1)}, f32[672,768]{1,0:T(8,128)}, f32[672,768]{1,0:T(8,128)}, f32[672,768]{1,0:T(8,128...) custom-call(bf16[12,196,768]{2,1,0:T(8,128)(2,1)} %pix.3, ...), custom_call_target="tpu_custom_call" | custom-call | tf_op jit(solution)/shard_map/encoder_fwd/pallas_call | solution.py:843
  146.9 164.5 %decoder.1 = (f32[12,56,512]{2,1,0:T(8,128)}, bf16[512,4096]{1,0:T(8,128)(2,1)}, bf16[512,2048]{1,0:T(8,128)(2,1)}, f32[1536,256]{1,0:T(8,128)}, f32[1,21248]{1,0:T(1,128)}, /*index=5*/f32[1,128]{1,0:T(1,128)}) custom-call(f32[12,56,512]{2,1,0:T(8,128)} %bitcast.29, s32[12,1,208]{2,1,0:T(1,128)} %reshape.79.coder, bf16[12,196,768]{2,1,0:T(8,128)(2,1)} %pix.3, ...), custom_call_target="tpu_custom_call" | custom-call | tf_op jit(solution)/shard_map/decoder/pallas_call | solution.py:333
  311.4 61.0 %encoder_bwd.1 = (bf16[768,7424]{1,0:T(8,128)(2,1)}, bf16[768,3072]{1,0:T(8,128)(2,1)}, f32[1792,256]{1,0:T(8,128)}) custom-call(f32[672,512]{1,0:T(8,128)} %bitcast.30, f32[1,21248]{1,0:T(1,128)} %get-tuple-element.77.dsm_in, f32[1536,256]{1,0:T(8,128)} %get-tuple-element.78.dhw, f32[1,21248]{1,0:T(1,128)} %reshape.77.sv, ...), custom_call_target="tpu_custom_call" | custom-call | tf_op jit(solution)/shard_map/encoder_bwd/pallas_call | solution.py:965
  372.4 115.8 %reduce_grads.1 = (f32[192,1024]{1,0:T(8,128)}, f32[96,768]{1,0:T(8,128)}, f32[128,512]{1,0:T(8,128)}, f32[64,512]{1,0:T(8,128)}, f32[32,64,256]{2,1,0:T(8,128)}) custom-call(bf16[768,7424]{1,0:T(8,128)(2,1)} %get-tuple-element.96.refs_0_, bf16[768,3072]{1,0:T(8,128)(2,1)} %get-tuple-element.97.refs_1_, bf16[512,4096]{1,0:T(8,128)(2,1)} %get-tuple-element.98.refs_2_, ...), custom_call_target="tpu_custom_call" | custom-call | tf_op jit(solution)/shard_map/reduce_grads/pallas_call | solution.py:640
  488.2 12.1 %update.1 = (f32[192,928]{1,0:T(8,128)}, f32[96,768]{1,0:T(8,128)}, f32[128,512]{1,0:T(8,128)}, f32[64,512]{1,0:T(8,128)}, f32[512,768]{1,0:T(8,128)}, /*index=5...) custom-call(f32[192,1024]{1,0:T(8,128)} %get-tuple-element.102.ga, ...), custom_call_target="tpu_custom_call" | custom-call | tf_op jit(solution)/shard_map/update/pallas_call | solution.py:1049
  500.3 1.3 fusion
  (3 shorter events, 0.0 us)
Async XLA Ops:
  13.4 0.7 copy-start

commit v6 on v5

--- a/solution.py
+++ b/solution.py
@@ -207,9 +207,8 @@
 
     bias = jnp.where(lax.broadcasted_iota(jnp.int32, (DS, 1), 0) <= PATCHES, 0.0, -1e30).astype(f32)
 
-    @pl.loop(0, nb)
-    def _(i):
-        rsl = pl.ds(pl.multiple_of(i * DS, 16), DS)
+    for i in range(nb):
+        rsl = slice(i * DS, (i + 1) * DS)
         for g in range(4):
             att_fwd(qkv, o, p, bias, rsl, W, g, i * 16 + g * 4, 32)
 
@@ -290,9 +289,8 @@
     o[...] = nt(d16[...], win[:, 3 * W : 4 * W]).astype(bf)
     dqkv = gp
 
-    @pl.loop(0, nb)
-    def _(i):
-        rsl = pl.ds(pl.multiple_of(i * DS, 16), DS)
+    for i in range(nb):
+        rsl = slice(i * DS, (i + 1) * DS)
         for g in range(4):
             att_bwd(qkv, o, p, dqkv, rsl, W, g, i * 16 + g * 4, 32)
 
@@ -647,16 +645,36 @@
     )(*grads, aux)
 
 
-def windows(sh, weights):
+def prepare_kernel(sh, a, b, c, d, small, aout, bout, cout, dout, sv, awide, bwide):
     row, col = lax.axis_index("row"), lax.axis_index("col")
 
-    def put(v, which, index, wide, lanes):
-        if wide == lanes:
-            return v
-        shift = index * wide - sh.start(which, index)
-        return lax.dynamic_update_slice(jnp.zeros((v.shape[0], lanes), v.dtype), v, (0, shift))
-    a, b, c, d = (w.astype(bf) for w in weights)
-    return put(a, "A", col, sh.awide, sh.alanes), put(b.T, "B", row, sh.bwide, sh.blanes), c, d.T
+    def put(ref, out, wide, which, index):
+        count, lanes = ref.shape[1], out.shape[1]
+        if count == lanes:
+            out[...] = ref[...].astype(bf)
+            return
+        wide[...] = jnp.zeros_like(wide)
+        wide[:, 0:count] = ref[...]
+        out[...] = pltpu.roll(wide[...], index * count - sh.start(which, index), 1).astype(bf)
+    put(a, aout, awide, "A", col)
+    put(b, bout, bwide, "B", row)
+    cout[...] = c[...].astype(bf)
+    dout[...] = d[...].astype(bf)
+    for i in range(SMALL // 128):
+        sv[:, i * 128 : (i + 1) * 128] = small[i : i + 1, :]
+
+
+def prepare(sh, weights, small):
+    a, b, c, d = weights
+    S = jax.ShapeDtypeStruct
+    alone = lambda m: (sh.brows, sh.blanes) if m == "B" else sh.blocks[m]
+    return pl.pallas_call(
+        functools.partial(prepare_kernel, sh),
+        in_specs=vspec(5), out_specs=vspec(5),
+        out_shape=[S((sh.arows, sh.alanes), bf)] + [S(alone(m), bf) for m in "BCD"] + [S((1, SMALL), f32)],
+        scratch_shapes=[pltpu.VMEM((sh.arows, sh.alanes), f32), pltpu.VMEM((sh.brows, sh.blanes), f32)],
+        name="prepare",
+    )(a, b.T, c, d.T, small.reshape(SMALL // 128, 128))
 
 
 GATHERED = ["A0", "A1", "A2", "B", "C", "D"]
@@ -925,9 +943,8 @@
     put(dwin, O_P, dg(o[...], d16[...], 0, 0))
     d16[...] = nt(d16[...], win[:, O_P:O_F]).astype(bf)
 
-    @pl.loop(0, M // EG)
-    def _(i):
-        rsl = pl.ds(pl.multiple_of(i * EG, 16), EG)
+    for i in range(M // EG):
+        rsl = slice(i * EG, (i + 1) * EG)
         for g in range(6):
             att_bwd(qkv, d16, p, dqkv, rsl, W, g, i * 12 + g * 2, 64)
 
@@ -1069,9 +1086,10 @@
     fill = lambda count, value: jnp.full((n, count), value, jnp.int32)
     keep = jnp.concatenate([keep_idx, fill(ES - KEEP, NOROW)], axis=1).reshape(n, 1, ES)
     code = jnp.concatenate([jnp.where(restore < KEEP, restore, 64), fill(1, KEEP), fill(DS - PATCHES - 1, NOROW)], axis=1)
-    head, sv = weights[4], weights[5].reshape(1, SMALL)
-
-    y, saved, (aw, bw, c, dt) = encoder_fwd(sh, pixels, keep, jnp.asarray(enc_pos), sv, *windows(sh, weights[0:4]))
+    head = weights[4]
+    *blocks, sv = prepare(sh, weights[0:4], weights[5])
+
+    y, saved, (aw, bw, c, dt) = encoder_fwd(sh, pixels, keep, jnp.asarray(enc_pos), sv, *blocks)
     dy, dc, ddt, dhead, dsm, loss = decoder(
         y.reshape(n, ES, DD), code.reshape(n, 1, DS), pixels, jnp.asarray(dec_pos), sv, c, dt, head, 1.0 / denom)
     da, dbt, shared = encoder_bwd(sh, dy.reshape(n * ES, DD), dsm, dhead, sv, aw, bw, saved)

time: 507 us -> 481 us (0.949)
  Pallas kernels: 486 us -> 471 us
  other arithmetic: 6.71 us -> 0.73 us
    pallas_call x1, Pallas kernels: 164 us -> 149 us  [decoder(): pl.pallas_call(functools.partial(dec_kernel, scale, nb), grid=(n // nb,),...]
where the time goes in v6:
time: 481 us; the launch traced here: 476 us
  Pallas kernels  471 us (98%)
    pallas_call x1, Pallas kernels, decoder(): pl.pallas_call(functools.partial(dec_kernel, scale, nb), grid=(n // nb,),...  149 us
    pallas_call x1, Pallas kernels, encoder_fwd(): pl.pallas_call(functools.partial(enc_fwd_kernel, sh), in_specs=vspec(4) +...  132 us
    pallas_call x1, Pallas kernels, reduce_grads(): pl.pallas_call(functools.partial(reduce_kernel, sh, mats), in_specs=[anys...  116 us
    pallas_call x1, Pallas kernels, encoder_bwd(): pl.pallas_call(functools.partial(enc_bwd_kernel, sh), in_specs=[anyspec i...  59.2 us
    pallas_call x1, Pallas kernels, update(): pl.pallas_call(functools.partial(update_kernel, sh), in_specs=vspec(5 + 1...  12.1 us

profile of v6, /device:TPU:0, one launch (start us, length us, event | category | flops | bytes accessed | tf_op | source)
XLA Modules:
  0.0 476.3 jit_solution(3059691007014763179)
XLA Ops:
  0.7 0.1 pad.3.clone
  0.7 0.1 pad.2.clone
  0.8 0.7 concatenate.6
  1.5 0.6 reshape.74.keep
  2.1 0.7 compare_select_fusion
  2.8 0.6 reshape.77.coder
  3.5 2.5 prepare.1
  6.0 131.9 %encoder_fwd.1 = (f32[672,512]{1,0:T(8,128)}, bf16[672,768]{1,0:T(8,128)(2,1)}, f32[672,768]{1,0:T(8,128)}, f32[672,768]{1,0:T(8,128)}, f32[672,768]{1,0:T(8,128...) custom-call(bf16[12,196,768]{2,1,0:T(8,128)(2,1)} %pix.3, ...), custom_call_target="tpu_custom_call" | custom-call | tf_op jit(solution)/shard_map/encoder_fwd/pallas_call | solution.py:861
  137.9 149.4 %decoder.1 = (f32[12,56,512]{2,1,0:T(8,128)}, bf16[512,4096]{1,0:T(8,128)(2,1)}, bf16[512,2048]{1,0:T(8,128)(2,1)}, f32[1536,256]{1,0:T(8,128)}, f32[1,21248]{1,0:T(1,128)}, /*index=5*/f32[1,128]{1,0:T(1,128)}) custom-call(f32[12,56,512]{2,1,0:T(8,128)} %bitcast.25, s32[12,1,208]{2,1,0:T(1,128)} %reshape.77.coder, bf16[12,196,768]{2,1,0:T(8,128)(2,1)} %pix.3, ...), custom_call_target="tpu_custom_call" | custom-call | tf_op jit(solution)/shard_map/decoder/pallas_call | solution.py:331
  287.3 59.2 %encoder_bwd.1 = (bf16[768,7424]{1,0:T(8,128)(2,1)}, bf16[768,3072]{1,0:T(8,128)(2,1)}, f32[1792,256]{1,0:T(8,128)}) custom-call(f32[672,512]{1,0:T(8,128)} %bitcast.26, f32[1,21248]{1,0:T(1,128)} %get-tuple-element.87.dsm_in, f32[1536,256]{1,0:T(8,128)} %get-tuple-element.88.dhw, f32[1,21248]{1,0:T(1,128)} %get-tuple-element.78.sv, ...), custom_call_target="tpu_custom_call" | custom-call | tf_op jit(solution)/shard_map/encoder_bwd/pallas_call | solution.py:982
  346.6 116.0 %reduce_grads.1 = (f32[192,1024]{1,0:T(8,128)}, f32[96,768]{1,0:T(8,128)}, f32[128,512]{1,0:T(8,128)}, f32[64,512]{1,0:T(8,128)}, f32[32,64,256]{2,1,0:T(8,128)}) custom-call(bf16[768,7424]{1,0:T(8,128)(2,1)} %get-tuple-element.106.refs_0_, bf16[768,3072]{1,0:T(8,128)(2,1)} %get-tuple-element.107.refs_1_, bf16[512,4096]{1,0:T(8,128)(2,1)} %get-tuple-element.108.refs_2_, ...), custom_call_target="tpu_custom_call" | custom-call | tf_op jit(solution)/shard_map/reduce_grads/pallas_call | solution.py:638
  462.6 12.1 %update.1 = (f32[192,928]{1,0:T(8,128)}, f32[96,768]{1,0:T(8,128)}, f32[128,512]{1,0:T(8,128)}, f32[64,512]{1,0:T(8,128)}, f32[512,768]{1,0:T(8,128)}, /*index=5...) custom-call(f32[192,1024]{1,0:T(8,128)} %get-tuple-element.112.ga, ...), custom_call_target="tpu_custom_call" | custom-call | tf_op jit(solution)/shard_map/update/pallas_call | solution.py:1066
  474.7 1.3 fusion
  (2 shorter events, 0.0 us)

commit v7 on v6

--- a/solution.py
+++ b/solution.py
@@ -640,7 +640,7 @@
         in_specs=[anyspec] * (len(whole) + 1) + [vm], out_specs=[vm] * (len(whole) + 1),
         out_shape=[S(outs[m], f32) for m in whole] + [S((sh.nrow * sh.ncol, sh.erows + 8, 256), f32)],
         scratch_shapes=scratch,
-        compiler_params=pltpu.CompilerParams(collective_id=1, has_side_effects=True, vmem_limit_bytes=60 << 20),
+        compiler_params=pltpu.CompilerParams(collective_id=1, has_side_effects=True, vmem_limit_bytes=44 << 20),
         name="reduce_grads",
     )(*grads, aux)
 
@@ -1068,7 +1068,7 @@
         in_specs=vspec(5 + 18), out_specs=vspec(19),
         out_shape=[S(v.shape, f32) for v in state] + [S((1, 128), f32)],
         scratch_shapes=[pltpu.VMEM((sh.nrow * sh.ncol * sh.erows, 256), f32)],
-        compiler_params=pltpu.CompilerParams(vmem_limit_bytes=60 << 20),
+        compiler_params=pltpu.CompilerParams(vmem_limit_bytes=34 << 20),
         name="update",
     )(*grads, *state)
     small = lambda v: v.reshape(SMALL) if v.shape == (SMALL // 128, 128) else v

time: 481 us -> 477 us (level)
  Pallas kernels: 471 us -> 465 us
where the time goes in v7:
time: 477 us; the launch traced here: 472 us
  Pallas kernels  465 us (97%)
  local copies, waits for them, and re-layouts  5.84 us (1%)
    pallas_call x1, Pallas kernels, decoder(): pl.pallas_call(functools.partial(dec_kernel, scale, nb), grid=(n // nb,),...  149 us
    pallas_call x1, Pallas kernels, encoder_fwd(): pl.pallas_call(functools.partial(enc_fwd_kernel, sh), in_specs=vspec(4) +...  132 us
    pallas_call x1, Pallas kernels, reduce_grads(): pl.pallas_call(functools.partial(reduce_kernel, sh, mats), in_specs=[anys...  114 us
    pallas_call x1, Pallas kernels, encoder_bwd(): pl.pallas_call(functools.partial(enc_bwd_kernel, sh), in_specs=[anyspec i...  59.2 us

profile of v7, /device:TPU:0, one launch (start us, length us, event | category | flops | bytes accessed | tf_op | source)
XLA Modules:
  0.0 472.4 jit_solution(785073255351121485)
XLA Ops:
  0.7 0.1 pad.3.clone
  0.7 0.1 pad.2.clone
  0.8 0.7 concatenate.6
  1.5 0.6 reshape.74.keep
  2.1 0.7 compare_select_fusion
  2.8 0.6 reshape.77.coder
  3.5 2.5 prepare.1
  6.0 131.9 %encoder_fwd.1 = (f32[672,512]{1,0:T(8,128)}, bf16[672,768]{1,0:T(8,128)(2,1)}, f32[672,768]{1,0:T(8,128)}, f32[672,768]{1,0:T(8,128)}, f32[672,768]{1,0:T(8,128...) custom-call(bf16[12,196,768]{2,1,0:T(8,128)(2,1)} %pix.3, ...), custom_call_target="tpu_custom_call" | custom-call | tf_op jit(solution)/shard_map/encoder_fwd/pallas_call | solution.py:861
  137.9 149.4 %decoder.1 = (f32[12,56,512]{2,1,0:T(8,128)}, bf16[512,4096]{1,0:T(8,128)(2,1)}, bf16[512,2048]{1,0:T(8,128)(2,1)}, f32[1536,256]{1,0:T(8,128)}, f32[1,21248]{1,0:T(1,128)}, /*index=5*/f32[1,128]{1,0:T(1,128)}) custom-call(f32[12,56,512]{2,1,0:T(8,128)} %bitcast.37, s32[12,1,208]{2,1,0:T(1,128)} %reshape.77.coder, bf16[12,196,768]{2,1,0:T(8,128)(2,1)} %pix.3, ...), custom_call_target="tpu_custom_call" | custom-call | tf_op jit(solution)/shard_map/decoder/pallas_call | solution.py:331
  287.3 0.0 copy-start.20
  287.3 59.2 %encoder_bwd.1 = (bf16[768,7424]{1,0:T(8,128)(2,1)}, bf16[768,3072]{1,0:T(8,128)(2,1)}, f32[1792,256]{1,0:T(8,128)}) custom-call(f32[672,512]{1,0:T(8,128)} %bitcast.38, f32[1,21248]{1,0:T(1,128)} %get-tuple-element.87.dsm_in, f32[1536,256]{1,0:T(8,128)} %get-tuple-element.88.dhw, f32[1,21248]{1,0:T(1,128)} %get-tuple-element.78.sv, ...), custom_call_target="tpu_custom_call" | custom-call | tf_op jit(solution)/shard_map/encoder_bwd/pallas_call | solution.py:982
  346.6 0.0 copy-done.20
  346.6 0.0 copy-start.2
  346.6 1.6 copy-done.2
  348.2 1.5 copy-done.3
  349.7 0.0 copy-start.6
  349.7 0.0 copy-start.7
  349.7 0.0 copy-start.8
  349.7 0.0 copy-start.9
  349.7 0.0 copy-start.10
  349.8 0.0 copy-start.11
  349.8 0.0 copy-start.12
  349.8 0.0 copy-start.13
  349.8 0.0 copy-start.14
  349.8 0.0 copy-start.15
  349.8 0.0 copy-start.16
  349.8 0.0 copy-start.17
  349.8 0.0 copy-start.18
  349.8 0.0 copy-start.19
  349.9 113.8 %reduce_grads.1 = (f32[192,1024]{1,0:T(8,128)S(1)}, f32[96,768]{1,0:T(8,128)S(1)}, f32[128,512]{1,0:T(8,128)S(1)}, f32[64,512]{1,0:T(8,128)S(1)}, f32[32,64,256]{2,1,0:T(8,128)S(1)}) custom-call(bf16[768,7424]{1,0:T(8,128)(2,1)} %get-tuple-element.106.refs_0_, bf16[768,3072]{1,0:T(8,128)(2,1)} %get-tuple-element.107.refs_1_, ...), custom_call_target="tpu_custom_call" | custom-call | tf_op jit(solution)/shard_map/reduce_grads/pallas_call | solution.py:638
  463.9 7.7 %update.1 = (f32[192,928]{1,0:T(8,128)}, f32[96,768]{1,0:T(8,128)}, f32[128,512]{1,0:T(8,128)}, f32[64,512]{1,0:T(8,128)}, f32[512,768]{1,0:T(8,128)}, /*index=5...) custom-call(f32[192,1024]{1,0:T(8,128)S(1)} %get-tuple-element.112.g, ...), custom_call_target="tpu_custom_call" | custom-call | tf_op jit(solution)/shard_map/update/pallas_call | solution.py:1066
  471.6 0.6 fusion
  (25 shorter events, 0.1 us)
Async XLA Ops:
  287.3 59.3 %copy-start.20 = (f32[1,128]{1,0:T(1,128)S(1)}, f32[1,128]{1,0:T(1,128)}, u32[]{:S(2)}) copy-start(f32[1,128]{1,0:T(1,128)} %get-tuple-element.111.refs_5_) | copy-start | bytes 1540
  346.6 1.6 copy-start.2
  348.2 1.5 copy-start.3
  349.7 114.0 %copy-start = (f32[512,768]{1,0:T(8,128)S(1)}, f32[512,768]{1,0:T(8,128)}, u32[]{:S(2)}) copy-start(f32[512,768]{1,0:T(8,128)} %refs_4_.1) | copy-start | bytes 4718596
  349.7 114.0 %copy-start.1 = (f32[192,928]{1,0:T(8,128)S(1)}, f32[192,928]{1,0:T(8,128)}, u32[]{:S(2)}) copy-start(f32[192,928]{1,0:T(8,128)} %refs_0_.1) | copy-start | bytes 2138116
  349.7 114.0 %copy-start.4 = (f32[512,768]{1,0:T(8,128)S(1)}, f32[512,768]{1,0:T(8,128)}, u32[]{:S(2)}) copy-start(f32[512,768]{1,0:T(8,128)} %refs_10_.1) | copy-start | bytes 4718596
  349.7 114.0 %copy-start.5 = (f32[512,768]{1,0:T(8,128)S(1)}, f32[512,768]{1,0:T(8,128)}, u32[]{:S(2)}) copy-start(f32[512,768]{1,0:T(8,128)} %refs_16_.1) | copy-start | bytes 4718596
  349.7 114.0 %copy-start.6 = (f32[768,96]{0,1:T(8,128)S(1)}, f32[768,96]{0,1:T(8,128)}, u32[]{:S(2)}) copy-start(f32[768,96]{0,1:T(8,128)} %param.27) | copy-start | bytes 884740
  349.7 114.0 %copy-start.7 = (f32[128,512]{1,0:T(8,128)S(1)}, f32[128,512]{1,0:T(8,128)}, u32[]{:S(2)}) copy-start(f32[128,512]{1,0:T(8,128)} %refs_2_.1) | copy-start | bytes 786436
  349.7 114.0 %copy-start.8 = (f32[192,928]{1,0:T(8,128)S(1)}, f32[192,928]{1,0:T(8,128)}, u32[]{:S(2)}) copy-start(f32[192,928]{1,0:T(8,128)} %refs_6_.1) | copy-start | bytes 2138116
  349.7 114.0 %copy-start.9 = (f32[192,928]{1,0:T(8,128)S(1)}, f32[192,928]{1,0:T(8,128)}, u32[]{:S(2)}) copy-start(f32[192,928]{1,0:T(8,128)} %refs_12_.1) | copy-start | bytes 2138116
  349.7 114.0 %copy-start.10 = (f32[512,64]{0,1:T(8,128)S(1)}, f32[512,64]{0,1:T(8,128)}, u32[]{:S(2)}) copy-start(f32[512,64]{0,1:T(8,128)} %param.29) | copy-start | bytes 393220
  349.8 114.0 %copy-start.11 = (f32[21248]{0:T(1024)S(1)}, f32[21248]{0:T(1024)}, u32[]{:S(2)}) copy-start(f32[21248]{0:T(1024)} %param.31) | copy-start | bytes 254980
  349.8 114.0 %copy-start.12 = (f32[768,96]{0,1:T(8,128)S(1)}, f32[768,96]{0,1:T(8,128)}, u32[]{:S(2)}) copy-start(f32[768,96]{0,1:T(8,128)} %param.33) | copy-start | bytes 884740
  349.8 114.0 %copy-start.13 = (f32[768,96]{0,1:T(8,128)S(1)}, f32[768,96]{0,1:T(8,128)}, u32[]{:S(2)}) copy-start(f32[768,96]{0,1:T(8,128)} %param.39) | copy-start | bytes 884740
  349.8 114.0 %copy-start.14 = (f32[128,512]{1,0:T(8,128)S(1)}, f32[128,512]{1,0:T(8,128)}, u32[]{:S(2)}) copy-start(f32[128,512]{1,0:T(8,128)} %refs_8_.1) | copy-start | bytes 786436
  349.8 114.0 %copy-start.15 = (f32[128,512]{1,0:T(8,128)S(1)}, f32[128,512]{1,0:T(8,128)}, u32[]{:S(2)}) copy-start(f32[128,512]{1,0:T(8,128)} %refs_14_.1) | copy-start | bytes 786436
  349.8 114.0 %copy-start.16 = (f32[512,64]{0,1:T(8,128)S(1)}, f32[512,64]{0,1:T(8,128)}, u32[]{:S(2)}) copy-start(f32[512,64]{0,1:T(8,128)} %param.35) | copy-start | bytes 393220
  349.8 114.0 %copy-start.17 = (f32[512,64]{0,1:T(8,128)S(1)}, f32[512,64]{0,1:T(8,128)}, u32[]{:S(2)}) copy-start(f32[512,64]{0,1:T(8,128)} %param.41) | copy-start | bytes 393220
  349.8 114.0 %copy-start.18 = (f32[21248]{0:T(1024)S(1)}, f32[21248]{0:T(1024)}, u32[]{:S(2)}) copy-start(f32[21248]{0:T(1024)} %param.37) | copy-start | bytes 254980
  349.8 114.0 %copy-start.19 = (f32[21248]{0:T(1024)S(1)}, f32[21248]{0:T(1024)}, u32[]{:S(2)}) copy-start(f32[21248]{0:T(1024)} %param.43) | copy-start | bytes 254980
